TPU v7x, 32 devices: a whole 2x2x4 slice. The times are simulated.
32 devices in a mesh: space: 8 (over z, y), dir: 4 (over x, core).
Axes of the slice: x: 2, y: 2, z: 4, core: 2. Of those that a mesh axis runs over, the one named last changes fastest.
Arguments:
- state: float32 [36, 32, 128, 256], P('dir', None, 'space'), may hold values from -6 to 6
- target: float32 [36, 32, 128, 256], P('dir', None, 'space'), may hold values from -6 to 6
- w_in: bfloat16 [36, 32, 256], P('dir'), may hold values from -0.1875 to 0.1875
- w_out: bfloat16 [256, 36, 32], P(None, 'dir'), may hold values from -0.375 to 0.375
- sea_mask: int32 [128, 256], P('space'), may hold values from 0 to 1
- sea_count: int32 [128], P('space'), may hold values from 1 to 256, as said below
- turn_sign: int32 [128, 256], P('space'), may hold values from -1 to 1, as said below
Outputs:
- next_state: float32 [36, 32, 128, 256], P('dir', None, 'space')
- grad_in: float32 [36, 32, 256], P('dir')
- grad_out: float32 [256, 36, 32], P(None, 'dir')
Inputs may be any that keep to these rules, and one draw needn't show every extreme that they name: sea_count holds, for each row, the number of ones of sea_mask in that row. turn_sign is -1 or +1.
All inputs are finite; a program needn't handle non-finite values.
Results may differ from a plain program's by a relative error of at most 0.003.
Values may be sent and summed in bfloat16 or wider, within the bound.
No kernel may reach another device: no remote copies, remote signals or barrier semaphores. Data moves between devices by JAX's collectives and lax.ppermute only.
A program may use at most 128 MiB of HBM per device.

v0:
```python
import math

import jax
import jax.numpy as jnp
from jax import lax
from jax.sharding import PartitionSpec as P

NDIR = 36


def padded(block, sides, width, periodic):
    for axis, dim in sides:
        count = lax.axis_size(axis)
        forward = [(i, i + 1) for i in range(count - 1)]
        if periodic:
            forward.append((count - 1, 0))
        backward = [(target, source) for source, target in forward]
        low = lax.ppermute(
            lax.slice_in_dim(block, block.shape[dim] - width, None, axis=dim), axis, forward
        )
        high = lax.ppermute(lax.slice_in_dim(block, 0, width, axis=dim), axis, backward)
        block = jnp.concatenate([low, block, high], axis=dim)
    return block


def courant(first, count, nfreq):
    bins = (first + jnp.arange(count, dtype=jnp.int32)).astype(jnp.float32)
    angle = 2.0 * math.pi * (bins + 0.5) / NDIR
    speed = 1.0 / (1.0 + 2.3 * jnp.arange(nfreq, dtype=jnp.float32) / nfreq)
    cx = 0.4 * jnp.cos(angle)[:, None] * speed[None, :]
    cy = 0.4 * jnp.sin(angle)[:, None] * speed[None, :]
    return (cx[:, :, None, None], cy[:, :, None, None])


def on_device(state, target, w_in, w_out, sea_mask, sea_count, turn_sign):
    dir_dev, nfreq, rows, ncols = state.shape
    maskf = sea_mask.astype(jnp.float32)
    field = state * maskf[None, None]
    circled = padded(field, (("dir", 0),), 1, True)
    bands = padded(field, (("space", 2),), 1, False)
    cx, cy = courant(lax.axis_index("dir") * dir_dev, dir_dev, nfreq)
    sides = jnp.pad(field, ((0, 0), (0, 0), (0, 0), (1, 1)))
    west = sides[:, :, :, :-2]
    east = sides[:, :, :, 2:]
    south = bands[:, :, :-2]
    north = bands[:, :, 2:]
    advect = -(jnp.maximum(cx, 0.0) * (field - west) + jnp.minimum(cx, 0.0) * (east - field))
    advect = advect - (
        jnp.maximum(cy, 0.0) * (field - south) + jnp.minimum(cy, 0.0) * (north - field)
    )
    upstream = jnp.where((turn_sign > 0)[None, None], circled[:-2], circled[2:])
    turning = -0.3 * (field - upstream)
    spec_in = field.astype(jnp.bfloat16)
    partial_pre = jnp.einsum("dfyx,dfh->hyx", spec_in, w_in, preferred_element_type=jnp.float32)
    pre = lax.psum(partial_pre, "dir")
    hidden = jax.nn.silu(pre).astype(jnp.bfloat16)
    source = jnp.einsum("hyx,hdf->dfyx", hidden, w_out, preferred_element_type=jnp.float32)
    next_state = maskf[None, None] * (field + advect + turning + 0.5 * source)
    weight = (1.0 / sea_count.astype(jnp.float32))[:, None] * maskf
    back_src = (1.0 * weight[None, None] * (next_state - target)).astype(jnp.bfloat16)
    local_out = jnp.einsum("hyx,dfyx->hdf", hidden, back_src, preferred_element_type=jnp.float32)
    partial_back = jnp.einsum("hdf,dfyx->hyx", w_out, back_src, preferred_element_type=jnp.float32)
    back_hidden = lax.psum(partial_back, "dir")
    sig = jax.nn.sigmoid(pre)
    back_pre = (back_hidden * sig * (1.0 + pre * (1.0 - sig))).astype(jnp.bfloat16)
    local_in = jnp.einsum("dfyx,hyx->dfh", spec_in, back_pre, preferred_element_type=jnp.float32)
    grad_in, grad_out = lax.psum((local_in, local_out), "space")
    return (next_state, grad_in, grad_out)


def solution(mesh):
    in_specs = (
        P("dir", None, "space", None),
        P("dir", None, "space", None),
        P("dir", None, None),
        P(None, "dir", None),
        P("space", None),
        P("space"),
        P("space", None),
    )
    out_specs = (P("dir", None, "space", None), P("dir", None, None), P(None, "dir", None))
    return jax.shard_map(
        on_device, mesh=mesh, in_specs=in_specs, out_specs=out_specs, check_vma=False
    )
```

profile of v0, /device:TPU:0, one launch (start us, length us, event | category | flops | bytes accessed | tf_op | source)
XLA Modules:
  0.0 319.8 jit_solution(15171567703229712217)
XLA Ops:
  7.2 0.8 convert_element_type.30
  8.0 5.1 %copy_multiply_fusion = f32[9,32,16,256]{3,1,0,2:T(8,128)S(1)} fusion(f32[9,32,16,256]{3,2,1,0:T(8,128)} %param.7, f32[16,256]{1,0:T(8,128)S(1)} %convert_element_type.30), kind=kLoop, calls=%fused_computation.28 | loop fusion | flops 1179648 | bytes 9453568 | tf_op jit(solution)/shard_map/mul | solution.py:38
  13.1 2.2 copy-done.1
  15.3 3.3 %convolution_bitcast_fusion.1 = f32[256,16,256]{0,2,1:T(8,128)} fusion(f32[9,32,16,256]{3,1,0,2:T(8,128)S(1)} %copy_multiply_fusion, bf16[9,32,256]{2,1,0:T(8,128)(2,1)S(1)} %copy-done.4), kind=kOutput, calls=%fused_computation.33 | convolution fusion | flops 605159424 | bytes 9060352 | tf_op jit(solution)/shard_map/dfyx,dfh->hyx/dot_general | solution.py:54
  18.6 1.1 fusion.40
  19.7 4.9 %collective-permute-start = (f32[9,32,1,256]{3,1,0,2:T(8,128)S(1)}, f32[9,32,1,256]{3,1,0,2:T(8,128)S(1)}, u32[]{:S(2)}, u32[]{:S(2)}) collective-permute-start(f32[9,32,1,256]{3,1,0,2:T(8,128)S(1)} %get-tuple-element.8), channel_id=1, source_target_pairs={{0,4},{4,8},{8,12},{12,16},{16,20},{20,24},{24,28},{1,5},{5,9},{9,... | collective-permute-start | bytes 884744 | tf_op jit(solution)/shard_map/ppermute | solution.py:18
  24.6 1.3 collective-permute-start.1
  25.9 1.6 fusion.41
  27.6 1.7 collective-permute-start.3
  29.5 0.1 multiply_maximum_fusion.1
  29.6 7.6 %collective-permute-done = f32[9,32,1,256]{3,1,0,2:T(8,128)S(1)} collective-permute-done((f32[9,32,1,256]{3,1,0,2:T(8,128)S(1)}, f32[9,32,1,256]{3,1,0,2:T(8,128)S(1)}, u32[]{:S(2)}, u32[]{:S(2)}) %collective-permute-start) | collective-permute-done | bytes 294944 | tf_op jit(solution)/shard_map/ppermute | solution.py:18
  37.2 15.2 %collective-permute-done.2 = f32[1,32,16,256]{3,1,0,2:T(8,128)S(1)} collective-permute-done((f32[1,32,16,256]{3,1,0,2:T(8,128)S(1)}, f32[1,32,16,256]{3,1,0,2:T(8,128)S(1)}, u32[]{:S(2)}, u32[]{:S(2)}) %collective-permute-start.2) | collective-permute-done | bytes 524320 | tf_op jit(solution)/shard_map/ppermute | solution.py:18
  52.4 0.1 collective-permute-done.3
  52.5 65.6 %all-reduce.6.cloned.1.call-done = f32[256,16,256]{0,2,1:T(8,128)} async-done(((f32[256,16,256]{0,2,1:T(8,128)}), f32[256,16,256]{0,2,1:T(8,128)}) %all-reduce.6.cloned.1.call-update) | async-done | bytes 4194320 | tf_op jit(solution)/shard_map/psum | solution.py:55
  118.1 20.1 %fusion.20 = (bf16[9,32,16,256]{3,1,0,2:T(8,128)(2,1)}, f32[9,32,16,256]{3,1,0,2:T(8,128)}) fusion(f32[9,32,16,256]{3,2,1,0:T(8,128)} %param.8, f32[16,256]{1,0:T(8,128)S(1)} %broadcast_multiply_fusion, bf16[256,9,32]{0,2,1:T(8,128)(2,1)S(1)} %copy-done, f32[256,16,256]{0,2,1:T(8,128)} %all-reduce.6.cloned.1.call-done, f32[9,32,16,256]{3,1,0,2:T(8,128)} %copy-done.1, ...), kind=kOutput, calls=%fused_computation.27 | convolution fusion | flops 641073152 | bytes 22536704 | tf_op jit(solution)/shard_map/hyx,hdf->dfyx/dot_general | solution.py:57
  138.3 5.0 %convolution_bitcast_fusion = f32[256,16,256]{0,2,1:T(8,128)} fusion(bf16[9,32,16,256]{3,1,0,2:T(8,128)(2,1)} %get-tuple-element.18, bf16[256,9,32]{0,2,1:T(8,128)(2,1)S(1)} %copy-done), kind=kOutput, calls=%fused_computation.32 | convolution fusion | flops 603979776 | bytes 6701056 | tf_op jit(solution)/shard_map/hdf,dfyx->hyx/dot_general | solution.py:62
  143.4 0.2 all-reduce.10.cloned.1.call-start
  143.6 4.4 %fusion.28 = f32[256,9,32]{0,2,1:T(8,128)} fusion(bf16[9,32,16,256]{3,1,0,2:T(8,128)(2,1)S(1)} %copy-done.6, f32[256,16,256]{0,2,1:T(8,128)} %all-reduce.6.cloned.1.call-done), kind=kOutput, calls=%fused_computation.41 | convolution fusion | flops 609222656 | bytes 6848512 | tf_op jit(solution)/shard_map/hyx,dfyx->hdf/dot_general | solution.py:61
  147.9 81.2 %all-reduce.8.cloned.1.call-done = f32[256,16,256]{0,2,1:T(8,128)} async-done(((f32[256,16,256]{0,2,1:T(8,128)}), f32[256,16,256]{0,2,1:T(8,128)}) %all-reduce.8.cloned.1.call-update) | async-done | bytes 4194320 | tf_op jit(solution)/shard_map/psum | solution.py:63
  229.1 7.5 %fusion.31 = f32[9,32,256]{2,1,0:T(8,128)} fusion(f32[256,16,256]{0,2,1:T(8,128)} %all-reduce.6.cloned.1.call-done, f32[256,16,256]{0,2,1:T(8,128)} %all-reduce.8.cloned.1.call-done, f32[9,32,16,256]{3,1,0,2:T(8,128)} %copy-done.1), kind=kOutput, calls=%fused_computation.42 | convolution fusion | flops 614596608 | bytes 13402112 | tf_op jit(solution)/shard_map/dfyx,hyx->dfh/dot_general | solution.py:66
  236.7 7.3 %copy.17 = f32[9,32,16,256]{3,2,1,0:T(8,128)} copy(f32[9,32,16,256]{3,1,0,2:T(8,128)} %get-tuple-element.19) | data formatting | bytes 9437184
  244.0 65.9 %all-reduce.10.cloned.1.call-done = (f32[9,32,256]{2,1,0:T(8,128)}, f32[256,9,32]{0,2,1:T(8,128)}) async-done(((f32[9,32,256]{2,1,0:T(8,128)}, f32[256,9,32]{0,2,1:T(8,128)}), (f32[9,32,256]{2,1,0:T(8,128)}, f32[256,9,32]{0,2,1:T(8,128)})) %all-reduce.10.cloned.1.call-update) | async-done | bytes 589840 | tf_op jit(solution)/shard_map/psum | solution.py:67
  309.9 1.7 copy.40
  311.6 1.7 copy.41
  (25 shorter events, 0.4 us)
Async XLA Ops:
  7.2 111.0 %copy-start = (bf16[256,9,32]{0,2,1:T(8,128)(2,1)S(1)}, bf16[256,9,32]{0,2,1:T(8,128)(2,1)}, u32[]{:S(2)}) copy-start(bf16[256,9,32]{0,2,1:T(8,128)(2,1)} %param.10) | copy-start | bytes 442372
  7.2 111.0 %all-reduce.6.cloned.1.call-start = ((), (), s32[]{:S(2)}) async-start(), calls=%async_computation | async-start | bytes 8388608 | tf_op jit(solution)/shard_map/psum | solution.py:55
  8.0 7.3 %copy-start.4 = (bf16[9,32,256]{2,1,0:T(8,128)(2,1)S(1)}, bf16[9,32,256]{2,1,0:T(8,128)(2,1)}, u32[]{:S(2)}) copy-start(bf16[9,32,256]{2,1,0:T(8,128)(2,1)} %param.9) | copy-start | bytes 442372
  13.1 2.2 copy-start.1
  18.5 10.9 %copy-start.5 = (s32[16]{0:T(128)S(1)}, s32[16]{0:T(128)}, u32[]{:S(2)}) copy-start(s32[16]{0:T(128)} %param.12) | copy-start | bytes 196
  18.5 10.9 %copy-start.2 = (s32[16,256]{1,0:T(8,128)S(1)}, s32[16,256]{1,0:T(8,128)}, u32[]{:S(2)}) copy-start(s32[16,256]{1,0:T(8,128)} %param.11) | copy-start | bytes 49156
  18.5 11.0 %copy-start.3 = (s32[16,256]{1,0:T(8,128)S(1)}, s32[16,256]{1,0:T(8,128)}, u32[]{:S(2)}) copy-start(s32[16,256]{1,0:T(8,128)} %param.13) | copy-start | bytes 49156
  18.6 210.6 %all-reduce.8.cloned.1.call-start = ((), (), s32[]{:S(2)}) async-start(), calls=%async_computation.1 | async-start | bytes 8388608 | tf_op jit(solution)/shard_map/psum | solution.py:63
  19.7 17.4 %collective-permute-start = (f32[9,32,1,256]{3,1,0,2:T(8,128)S(1)}, f32[9,32,1,256]{3,1,0,2:T(8,128)S(1)}, u32[]{:S(2)}, u32[]{:S(2)}) collective-permute-start(f32[9,32,1,256]{3,1,0,2:T(8,128)S(1)} %get-tuple-element.8), channel_id=1, source_target_pairs={{0,4},{4,8},{8,12},{12,16},{16,20},{20,24},{24,28},{1,5},{5,9},{9,... | collective-permute-start | bytes 884744 | tf_op jit(solution)/shard_map/ppermute | solution.py:18
  24.6 12.6 %collective-permute-start.1 = (f32[9,32,1,256]{3,1,0,2:T(8,128)S(1)}, f32[9,32,1,256]{3,1,0,2:T(8,128)S(1)}, u32[]{:S(2)}, u32[]{:S(2)}) collective-permute-start(f32[9,32,1,256]{3,1,0,2:T(8,128)S(1)} %get-tuple-element.9), channel_id=1, source_target_pairs={{4,0},{8,4},{12,8},{16,12},{20,16},{24,20},{28,24},{5,1},{9,5},{13... | collective-permute-start | bytes 884744 | tf_op jit(solution)/shard_map/ppermute | solution.py:21
  27.6 24.9 %collective-permute-start.2 = (f32[1,32,16,256]{3,1,0,2:T(8,128)S(1)}, f32[1,32,16,256]{3,1,0,2:T(8,128)S(1)}, u32[]{:S(2)}, u32[]{:S(2)}) collective-permute-start(f32[1,32,16,256]{3,1,0,2:T(8,128)S(1)} %get-tuple-element.10), channel_id=1, source_target_pairs={{0,1},{1,2},{2,3},{3,0},{4,5},{5,6},{6,7},{7,4},{8,9},{9,10},{10,1... | collective-permute-start | bytes 1572872 | tf_op jit(solution)/shard_map/ppermute | solution.py:18
  27.6 24.9 %collective-permute-start.3 = (f32[1,32,16,256]{3,1,0,2:T(8,128)S(1)}, f32[1,32,16,256]{3,1,0,2:T(8,128)S(1)}, u32[]{:S(2)}, u32[]{:S(2)}) collective-permute-start(f32[1,32,16,256]{3,1,0,2:T(8,128)S(1)} %get-tuple-element.11), channel_id=1, source_target_pairs={{1,0},{2,1},{3,2},{0,3},{5,4},{6,5},{7,6},{4,7},{9,8},{10,9},{11,1... | collective-permute-start | bytes 1572872 | tf_op jit(solution)/shard_map/ppermute | solution.py:21
  138.3 5.3 %copy-start.6 = (bf16[9,32,16,256]{3,1,0,2:T(8,128)(2,1)S(1)}, bf16[9,32,16,256]{3,1,0,2:T(8,128)(2,1)}, u32[]{:S(2)}) copy-start(bf16[9,32,16,256]{3,1,0,2:T(8,128)(2,1)} %get-tuple-element.18) | copy-start | bytes 7077892
  143.4 166.6 %all-reduce.10.cloned.1.call-start = ((), (), s32[]{:S(2)}) async-start(), calls=%async_computation.2 | async-start | bytes 1179648 | tf_op jit(solution)/shard_map/psum | solution.py:67
Sparse Core Ops, SparseCore 0:
  18.7 99.4 all-reduce.5
  143.5 85.6 all-reduce.7
  236.8 73.0 all-reduce.9
where the time goes:
time: 320 us
  waiting for transfers between devices  236 us (74%)
  matrix products  40.3 us (13%)
  local copies, waits for them, and re-layouts  15.6 us (5%)
  between operations  13.9 us (4%)
  starting transfers between devices  8.27 us (3%)
  other arithmetic  6.07 us (2%)
    psum x1, waiting for transfers between devices, on_device(): back_hidden = lax.psum(partial_back, 'dir')  81.2 us
    psum x1, waiting for transfers between devices, on_device(): grad_in, grad_out = lax.psum((local_in, local_out), 'space')  65.9 us
    psum x1, waiting for transfers between devices, on_device(): pre = lax.psum(partial_pre, 'dir')  65.6 us
    ppermute x2, waiting for transfers between devices, padded(): lax.ppermute(lax.slice_in_dim(block, block.shape[dim] - width, None, axis...  22.8 us
    dot_general x1, matrix products, on_device(): jnp.einsum('hyx,hdf->dfyx', hidden, w_out, preferred_element_type=jnp.flo...  20.1 us
    unnamed x17, local copies, waits for them, and re-layouts  12.9 us
    dot_general x1, matrix products, on_device(): jnp.einsum('dfyx,hyx->dfh', spec_in, back_pre, preferred_element_type=jnp...  7.48 us
  transfers between devices with their start and end apart: 7, of which 6 were waited for; matrix products, arithmetic and copies ran while one was open for 5% of the time, Pallas kernels for 0%

commit v1 on v0

v1 whole, which is shorter than its diff:
```python
import math

import jax
import jax.numpy as jnp
from jax import lax
from jax.experimental import pallas as pl
from jax.experimental.pallas import tpu as pltpu
from jax.sharding import PartitionSpec as P

NDIR = 36
ROWS = 8
LANES = 128
PRE_SCALE = 64.0
BACK_SCALE = 2.0**-8

BF16, F16, F32 = jnp.bfloat16, jnp.float16, jnp.float32


def swap(value, axis, bit):
    count = lax.axis_size(axis)
    return lax.ppermute(value, axis, [(i, i ^ bit) for i in range(count)])


def call(body, grid, ins, outs, cost, aliases=None, name=None):
    return pl.pallas_call(
        body,
        grid=grid,
        in_specs=[spec for _, spec in ins],
        out_specs=[spec for _, spec in outs],
        out_shape=[shape for shape, _ in outs],
        input_output_aliases=aliases or {},
        compiler_params=pltpu.CompilerParams(vmem_limit_bytes=40 << 20),
        cost_estimate=pl.CostEstimate(flops=cost[0], bytes_accessed=cost[1], transcendentals=0),
        name=name,
    )(*[value for value, _ in ins])


def shape(dims, dtype):
    return jax.ShapeDtypeStruct(dims, dtype)


def first_row(core, side, half):
    return core * half if side == 0 else (1 - core) * half


def encode_body(core_ref, state_ref, mask_ref, w_ref, spec_ref, own_ref, send_ref):
    core = core_ref[0]
    bins, rows, lanes = state_ref.shape
    flat = state_ref.reshape(bins * rows, lanes)
    half = rows // 2
    for side, out in ((0, own_ref), (1, send_ref)):
        first = first_row(core, side, half)
        cols = []
        for i in range(half):
            row = flat[pl.ds(first + i, bins, stride=rows), :]
            cols.append((row * mask_ref[pl.ds(first + i, 1), :]).astype(BF16))
        field = jnp.concatenate(cols, axis=1)
        spec_ref[:, side * half * lanes : (side + 1) * half * lanes] = field
        out[...] = lax.dot_general(
            w_ref[...], field, (((0,), (0,)), ((), ())), preferred_element_type=F32
        )


def encode(core, state, mask, w_in, chunk):
    bins, rows, lon = state.shape
    hidden = w_in.shape[1]
    parts = lon // LANES
    wide = ROWS * LANES
    return call(
        encode_body,
        (parts,),
        [
            (core, pl.BlockSpec(memory_space=pltpu.SMEM)),
            (state, pl.BlockSpec((bins, ROWS, LANES), lambda j: (0, chunk, j))),
            (mask, pl.BlockSpec((ROWS, LANES), lambda j: (chunk, j))),
            (w_in, pl.BlockSpec((bins, hidden), lambda j: (0, 0))),
        ],
        [
            (shape((bins, parts * wide), BF16), pl.BlockSpec((bins, wide), lambda j: (0, j))),
            (shape((hidden, parts * wide // 2), F32), pl.BlockSpec((hidden, wide // 2), lambda j: (0, j))),
            (shape((hidden, parts * wide // 2), F32), pl.BlockSpec((hidden, wide // 2), lambda j: (0, j))),
        ],
        (2 * bins * hidden * parts * wide, 4 * bins * parts * wide + 8 * hidden * parts * wide),
        name="encode",
    )


def stencil_body(coef_ref, state_ref, low_ref, high_ref, edge_ref, mask_ref, sign_ref, base_ref):
    d = pl.program_id(0)
    ndir = pl.num_programs(0)
    nfreq, rows, lon = base_ref.shape
    mask = mask_ref[...]
    ahead = sign_ref[...] > 0
    lane = lax.broadcasted_iota(jnp.int32, (rows, lon), 1)
    row = lax.broadcasted_iota(jnp.int32, (rows, lon), 0)

    def sector(below, above):
        def one(f, _):
            b = d * nfreq + f
            here = state_ref[b]
            field = here * mask
            west = jnp.where(lane == 0, 0.0, pltpu.roll(field, 1, 1))
            east = jnp.where(lane == lon - 1, 0.0, pltpu.roll(field, lon - 1, 1))
            edge = edge_ref[pl.ds(b, 1), :]
            south = jnp.where(row == 0, edge, pltpu.roll(field, 1, 0))
            north = jnp.where(row == rows - 1, edge, pltpu.roll(field, rows - 1, 0))
            upstream = jnp.where(ahead, below(b, f), above(b, f))
            total = coef_ref[0, b] * here + coef_ref[1, b] * west + coef_ref[2, b] * east
            total = total + coef_ref[3, b] * south + coef_ref[4, b] * north + 0.3 * upstream
            base_ref[f] = total * mask
            return 0

        lax.fori_loop(0, nfreq, one, 0, unroll=4)

    def inside_low(b, f):
        return state_ref[b - nfreq]

    def inside_high(b, f):
        return state_ref[b + nfreq]

    @pl.when(d == 0)
    def _():
        sector(lambda b, f: low_ref[f], inside_high)

    @pl.when(d == ndir - 1)
    def _():
        sector(inside_low, lambda b, f: high_ref[f])

    @pl.when(jnp.logical_and(d > 0, d < ndir - 1))
    def _():
        sector(inside_low, inside_high)


def stencil(coef, state, low, high, edge, mask, sign, ndir):
    bins, rows, lon = state.shape
    nfreq = bins // ndir

    def whole(value):
        return (value, pl.BlockSpec(value.shape, lambda d: (0,) * value.ndim))

    return call(
        stencil_body,
        (ndir,),
        [(coef, pl.BlockSpec(memory_space=pltpu.SMEM))]
        + [whole(v) for v in (state, low, high, edge, mask, sign)],
        [(shape(state.shape, F32), pl.BlockSpec((nfreq, rows, lon), lambda d: (d, 0, 0)))],
        (20 * state.size, 8 * state.size),
        name="stencil",
    )[0]


def decode_body(
    core_ref, own_ref, other_ref, w_ref, base_ref, target_ref, mask_ref, weight_ref, seed_ref,
    next_ref, grad_ref, back_own_ref, back_send_ref, back_scr,
):
    core = core_ref[0]
    bins, rows, lanes = base_ref.shape
    base = base_ref.reshape(bins * rows, lanes)
    target = target_ref.reshape(bins * rows, lanes)
    result = next_ref.reshape(bins * rows, lanes)
    half = rows // 2

    @pl.when(pl.program_id(0) == 0)
    def _():
        grad_ref[...] = seed_ref[...]

    for side, hid_ref, out in ((0, own_ref, back_own_ref), (1, other_ref, back_send_ref)):
        first = first_row(core, side, half)
        hid = hid_ref[...]
        source = lax.dot_general(w_ref[...], hid, (((0,), (0,)), ((), ())), preferred_element_type=F32)
        for i in range(half):
            y = first + i
            at = pl.ds(y, bins, stride=rows)
            part = source[:, i * lanes : (i + 1) * lanes]
            new = base[at, :] + (0.5 * mask_ref[pl.ds(y, 1), :]) * part
            result[at, :] = new
            back = (weight_ref[pl.ds(y, 1), :] * (new - target[at, :])).astype(BF16)
            back_scr[:, i * lanes : (i + 1) * lanes] = back
        back = back_scr[...]
        grad_ref[...] += lax.dot_general(hid, back, (((1,), (1,)), ((), ())), preferred_element_type=F32)
        out[...] = jnp.dot(w_ref[...], back, preferred_element_type=F32)


def decode(core, own, other, w_out, base, target, mask, weight, seed, chunk):
    bins, rows, lon = base.shape
    hidden = w_out.shape[0]
    parts = lon // LANES
    wide = ROWS * LANES // 2
    cells = pl.BlockSpec((bins, ROWS, LANES), lambda j: (0, chunk, j))
    units = pl.BlockSpec((hidden, wide), lambda j: (0, j))
    plane = pl.BlockSpec((ROWS, LANES), lambda j: (chunk, j))
    fixed = pl.BlockSpec((hidden, bins), lambda j: (0, 0))
    return pl.pallas_call(
        decode_body,
        grid=(parts,),
        in_specs=[pl.BlockSpec(memory_space=pltpu.SMEM), units, units, fixed, cells, cells, plane, plane, fixed],
        out_specs=[cells, fixed, units, units],
        out_shape=[
            shape(base.shape, F32),
            shape((hidden, bins), F32),
            shape((hidden, parts * wide), F32),
            shape((hidden, parts * wide), F32),
        ],
        scratch_shapes=[pltpu.VMEM((bins, wide), BF16)],
        input_output_aliases={4: 0},
        compiler_params=pltpu.CompilerParams(vmem_limit_bytes=40 << 20),
        cost_estimate=pl.CostEstimate(
            flops=12 * bins * hidden * parts * wide,
            bytes_accessed=24 * bins * parts * wide + 12 * hidden * parts * wide,
            transcendentals=0,
        ),
        name="decode",
    )(core, own, other, w_out, base, target, mask, weight, seed)


def collect_body(spec_ref, own_ref, other_ref, seed_ref, grad_ref):
    @pl.when(pl.program_id(0) == 0)
    def _():
        grad_ref[...] = seed_ref[...]

    back = jnp.concatenate([own_ref[...], other_ref[...]], axis=1)
    grad_ref[...] += lax.dot_general(
        spec_ref[...], back, (((1,), (1,)), ((), ())), preferred_element_type=F32
    )


def collect(spec, own, other, seed):
    bins, cells = spec.shape
    hidden = own.shape[0]
    wide = ROWS * LANES
    units = pl.BlockSpec((hidden, wide // 2), lambda j: (0, j))
    fixed = pl.BlockSpec((bins, hidden), lambda j: (0, 0))
    return call(
        collect_body,
        (cells // wide,),
        [(spec, pl.BlockSpec((bins, wide), lambda j: (0, j))), (own, units), (other, units), (seed, fixed)],
        [(shape((bins, hidden), F32), fixed)],
        (2 * bins * hidden * cells, 2 * bins * cells + 2 * hidden * cells),
        name="collect",
    )[0]


def space_sum(value):
    n = value.shape[0]
    extra = 16

    def packed(total, power):
        scaled = (total * jnp.exp2(-power)).astype(F16)
        return jnp.concatenate(
            [scaled, jnp.broadcast_to(power.astype(F16), (extra, value.shape[1]))], axis=0
        )

    def opened(sent):
        power = sent[n : n + 1].astype(F32)
        return (sent[:n].astype(F32) * jnp.exp2(power), power)

    most = jnp.maximum(jnp.max(jnp.abs(value)), 2.0**-100)
    power = jnp.full((1, value.shape[1]), jnp.ceil(jnp.log2(most)), F32)
    total = value
    bit = 1
    count = lax.axis_size("space")
    assert count & (count - 1) == 0
    while bit < count:
        mine = packed(total, power)
        other, other_power = opened(swap(mine, "space", bit))
        total, _ = opened(mine)
        total = total + other
        power = jnp.maximum(power, other_power) + 1.0
        bit *= 2
    return total


def courant(first, count, nfreq):
    bins = (first + jnp.arange(count, dtype=jnp.int32)).astype(F32)
    angle = 2.0 * math.pi * (bins + 0.5) / NDIR
    speed = 1.0 / (1.0 + 2.3 * jnp.arange(nfreq, dtype=F32) / nfreq)
    cx = 0.4 * jnp.cos(angle)[:, None] * speed[None, :]
    cy = 0.4 * jnp.sin(angle)[:, None] * speed[None, :]
    return (cx.reshape(-1), cy.reshape(-1))


def on_device(state, target, w_in, w_out, sea_mask, sea_count, turn_sign):
    ndir, nfreq, rows, lon = state.shape
    bins = ndir * nfreq
    hidden = w_in.shape[2]
    place = lax.axis_index("dir")
    sectors = lax.axis_size("dir")
    spaces = lax.axis_size("space")
    assert sectors == 4 and ndir * sectors == NDIR
    core = place % 2
    core_ref = core.reshape(1)
    state = state.reshape(bins, rows, lon)
    target = target.reshape(bins, rows, lon)
    w_in = w_in.reshape(bins, hidden)
    w_out = w_out.reshape(hidden, bins)
    maskf = sea_mask.astype(F32)
    countf = sea_count.astype(F32)
    weight = (1.0 / countf)[:, None] * maskf
    parts = lon // LANES
    chunks = rows // ROWS
    half = ROWS // 2

    north = place >= sectors // 2
    edge = lax.dynamic_index_in_dim(state, jnp.where(north, 0, rows - 1), 1, False)
    edge = edge * lax.dynamic_index_in_dim(maskf, jnp.where(north, 0, rows - 1), 0, True)
    pairs = []
    for s in range(spaces):
        for d in range(sectors):
            to = s - 1 if d >= sectors // 2 else s + 1
            if 0 <= to < spaces:
                pairs.append((s * sectors + d, to * sectors + d))
    last, first = state[bins - nfreq :], state[:nfreq]
    upper = core == 1
    near = swap(jnp.where(upper, first, last).astype(F16), "dir", 1).astype(F32)
    far = swap(jnp.where(upper, last, first).astype(F16), "dir", 3).astype(F32)
    edge = lax.ppermute(edge.astype(F16), ("space", "dir"), pairs).astype(F32)
    low = jnp.where(upper, near, far)
    high = jnp.where(upper, far, near)
    cx, cy = courant(place * ndir, ndir, nfreq)
    coef = jnp.stack(
        [
            1.0 - jnp.abs(cx) - jnp.abs(cy) - 0.3,
            jnp.maximum(cx, 0.0),
            -jnp.minimum(cx, 0.0),
            jnp.maximum(cy, 0.0),
            -jnp.minimum(cy, 0.0),
        ]
    )

    encoded = [encode(core_ref, state, maskf, w_in, c) for c in range(chunks)]
    base = stencil(coef, state, low, high, edge, maskf, turn_sign, ndir)

    pres, hids = [], []
    for c in range(chunks):
        _, own, send = encoded[c]
        chip = ((own + swap(send, "dir", 1)) * PRE_SCALE).astype(F16)
        pre = (chip.astype(F32) + swap(chip, "dir", 2).astype(F32)) * (1.0 / PRE_SCALE)
        pres.append(pre)
        hids.append(jax.nn.silu(pre).astype(BF16))

    grad_out = jnp.zeros((hidden, bins), F32)
    backs = []
    for c in range(chunks):
        other = swap(hids[c], "dir", 1)
        base, grad_out, own, send = decode(
            core_ref, hids[c], other, w_out, base, target, maskf, weight, grad_out, c
        )
        counts = lax.dynamic_slice_in_dim(countf, c * ROWS + core * half, half, 0)
        counts = jnp.tile(jnp.repeat(counts, LANES), parts)[None]
        chip = ((own + swap(send, "dir", 1)) * (counts * BACK_SCALE)).astype(F16)
        backs.append((chip, counts))

    grad_in = jnp.zeros((bins, hidden), F32)
    for c in range(chunks):
        chip, counts = backs[c]
        back = (chip.astype(F32) + swap(chip, "dir", 2).astype(F32)) * ((1.0 / BACK_SCALE) / counts)
        pre = pres[c]
        sig = jax.nn.sigmoid(pre)
        back_pre = (back * sig * (1.0 + pre * (1.0 - sig))).astype(BF16)
        grad_in = collect(encoded[c][0], back_pre, swap(back_pre, "dir", 1), grad_in)

    grad_out = space_sum(grad_out)
    grad_in = space_sum(grad_in)
    return (
        base.reshape(ndir, nfreq, rows, lon),
        grad_in.reshape(ndir, nfreq, hidden),
        grad_out.reshape(hidden, ndir, nfreq),
    )


def solution(mesh):
    in_specs = (
        P("dir", None, "space", None),
        P("dir", None, "space", None),
        P("dir", None, None),
        P(None, "dir", None),
        P("space", None),
        P("space"),
        P("space", None),
    )
    out_specs = (P("dir", None, "space", None), P("dir", None, None), P(None, "dir", None))
    return jax.shard_map(
        on_device, mesh=mesh, in_specs=in_specs, out_specs=out_specs, check_vma=False
    )
```

time: 320 us -> 150 us (0.47)
  waiting for transfers between devices: 236 us -> 58.1 us
  matrix products: 40.3 us -> 0 us
  Pallas kernels: 0 us -> 26.9 us
  other arithmetic: 6.07 us -> 25 us
  starting transfers between devices: 8.27 us -> 20.4 us
  between operations: 13.9 us -> 2.64 us
    psum x3 -> x0, waiting for transfers between devices: 213 us -> none  [the longest x1 81.2 us: on_device(): back_hidden = lax.psum(partial_back, 'dir')]
    dot_general x5 -> x0, matrix products: 40.3 us -> none  [the longest x1 20.1 us: on_device(): jnp.einsum('hyx,hdf->dfyx', hidden, w_out, preferred_element_type=jnp.flo...]
    ppermute x4 -> x21, waiting for transfers between devices: 22.9 us -> 58.1 us  [the longest x20 58.1 us: swap(): return lax.ppermute(value, axis, [(i, i ^ bit) for i in range(count)])]
    pallas_call x0 -> x7, Pallas kernels: none -> 26.9 us  [the longest x5 16.5 us: call(): pl.pallas_call(body, grid=grid, in_specs=[spec for _, spec in ins], out_s...]
    convert_element_type x1 -> x23, other arithmetic: 0.75 us -> 21 us  [the longest x2 4.78 us: on_device(): chip = ((own + swap(send, 'dir', 1)) * PRE_SCALE).astype(F16)]
    ppermute x4 -> x21, starting transfers between devices: 7.97 us -> 20.4 us  [the longest x20 16.4 us: swap(): return lax.ppermute(value, axis, [(i, i ^ bit) for i in range(count)])]
    mul x2 -> x1, other arithmetic: 5.18 us -> 0.07 us  [on_device(): weight = (1.0 / countf)[:, None] * maskf]
    unnamed x17 -> x38, local copies, waits for them, and re-layouts: 12.9 us -> 11.8 us
  transfers between devices with their start and end apart: 7 -> 21, of which waited for: 6 -> 11; matrix products, arithmetic and copies ran while one was open for 5% -> 18% of each run, Pallas kernels for 0% -> 16%
where the time goes in v1:
time: 150 us; the launch traced here: 149 us
  waiting for transfers between devices  58.1 us (39%)
  Pallas kernels  26.9 us (18%)
  other arithmetic  25 us (17%)
  starting transfers between devices  20.4 us (14%)
  local copies, waits for them, and re-layouts  16.4 us (11%)
  between operations  2.64 us (2%)
    ppermute x20, waiting for transfers between devices, swap(): return lax.ppermute(value, axis, [(i, i ^ bit) for i in range(count)])  58.1 us
    pallas_call x5, Pallas kernels, call(): pl.pallas_call(body, grid=grid, in_specs=[spec for _, spec in ins], out_s...  16.5 us
    ppermute x20, starting transfers between devices, swap(): return lax.ppermute(value, axis, [(i, i ^ bit) for i in range(count)])  16.4 us
    unnamed x38, local copies, waits for them, and re-layouts  11.8 us
    pallas_call x2, Pallas kernels, decode(): pl.pallas_call(decode_body, grid=(parts,), in_specs=[pl.BlockSpec(memory_...  10.4 us
    convert_element_type x2, other arithmetic, on_device(): chip = ((own + swap(send, 'dir', 1)) * PRE_SCALE).astype(F16)  4.78 us
    ppermute x1, starting transfers between devices, on_device(): edge = lax.ppermute(edge.astype(F16), ('space', 'dir'), pairs).astype(F32)  4.08 us
    convert_element_type x2, other arithmetic, on_device(): back_pre = (back * sig * (1.0 + pre * (1.0 - sig))).astype(BF16)  3.67 us
  transfers between devices with their start and end apart: 21, of which 11 were waited for; matrix products, arithmetic and copies ran while one was open for 18% of the time, Pallas kernels for 16%

profile of v1, /device:TPU:0, one launch (start us, length us, event | category | flops | bytes accessed | tf_op | source)
XLA Modules:
  0.0 149.4 jit_solution(464485728395945194)
XLA Ops:
  1.4 2.3 %copy-done = f32[9,32,16,256]{3,2,1,0:T(8,128)S(1)} copy-done((f32[9,32,16,256]{3,2,1,0:T(8,128)S(1)}, f32[9,32,16,256]{3,2,1,0:T(8,128)}, u32[]{:S(2)}) %copy-start) | copy-done | bytes 4718616
  4.6 2.3 %encode.3 = (bf16[288,2048]{1,0:T(8,128)(2,1)S(1)}, f32[256,1024]{1,0:T(8,128)S(1)}, f32[256,1024]{1,0:T(8,128)}) custom-call(s32[1]{0:T(128)} %bitcast.core_ref, f32[288,16,256]{2,1,0:T(8,128)S(1)} %bitcast.45, f32[16,256]{1,0:T(8,128)S(1)} %convert_element_type.212.mask_ref, bf16[288,256]{1,0:T(8,128)(2,1)S(1)} %bitcast.52), custom_call_target="tpu_custom_call" | custom-call | flops 301989888 | bytes 6553600 | tf_op jit(solution)/shard_map/encode/pallas_call | solution.py:25
  7.4 2.1 %fusion.1 = (f16[32,16,256]{2,1,0:T(8,128)(2,1)}, f16[32,16,256]{2,1,0:T(8,128)(2,1)}) fusion(f32[9,32,16,256]{3,2,1,0:T(8,128)} %param.7, pred[]{:T(512)S(6)} %eq.5), kind=kLoop, calls=%fused_computation.28 | loop fusion | flops 524288 | bytes 1572865 | tf_op jit(solution)/shard_map/convert_element_type | solution.py:314
  9.6 2.6 %collective-permute-start.7 = (f16[32,16,256]{2,1,0:T(8,128)(2,1)}, f16[32,16,256]{2,1,0:T(8,128)(2,1)}, u32[]{:S(2)}, u32[]{:S(2)}) collective-permute-start(f16[32,16,256]{2,1,0:T(8,128)(2,1)} %get-tuple-element.47), channel_id=1, source_target_pairs={{0,3},{1,2},{2,1},{3,0},{4,7},{5,6},{6,5},{7,4},{8,11},{9,10},{10,... | collective-permute-start | bytes 786440 | tf_op jit(solution)/shard_map/ppermute | solution.py:21
  12.1 1.9 %constant_dynamic-slice_fusion.1 = f32[288,1,256]{2,1,0:T(1,128)S(1)} fusion(f32[288,16,256]{2,1,0:T(8,128)} %bitcast.44, s32[]{:T(128)S(6)} %select_n.53), kind=kLoop, calls=%fused_computation.90 | loop fusion | bytes 589828 | tf_op jit(solution)/shard_map/jit(dynamic_index_in_dim)/dynamic_slice | solution.py:304
  14.7 4.1 %collective-permute-start.8 = (f16[288,256]{1,0:T(8,128)(2,1)}, f16[288,256]{1,0:T(8,128)(2,1)}, u32[]{:S(2)}, u32[]{:S(2)}) collective-permute-start(f16[288,256]{1,0:T(8,128)(2,1)} %fusion), channel_id=1, source_target_pairs={{0,4},{1,5},{4,8},{5,9},{6,2},{7,3},{8,12},{9,13},{10,6},{11,7},{1... | collective-permute-start | bytes 442376 | tf_op jit(solution)/shard_map/ppermute | solution.py:316
  18.8 2.3 %copy-done.1 = f32[9,32,16,256]{3,2,1,0:T(8,128)S(1)} copy-done((f32[9,32,16,256]{3,2,1,0:T(8,128)S(1)}, f32[9,32,16,256]{3,2,1,0:T(8,128)}, u32[]{:S(2)}) %copy-start.1) | copy-done | bytes 4718616
  22.0 2.3 %encode.2 = (bf16[288,2048]{1,0:T(8,128)(2,1)S(1)}, f32[256,1024]{1,0:T(8,128)S(1)}, f32[256,1024]{1,0:T(8,128)}) custom-call(s32[1]{0:T(128)} %bitcast.core_ref, f32[288,16,256]{2,1,0:T(8,128)S(1)} %bitcast.46, f32[16,256]{1,0:T(8,128)S(1)} %convert_element_type.212.mask_ref, bf16[288,256]{1,0:T(8,128)(2,1)S(1)} %bitcast.53), custom_call_target="tpu_custom_call" | custom-call | flops 301989888 | bytes 6553600 | tf_op jit(solution)/shard_map/encode/pallas_call | solution.py:25
  25.9 2.2 %multiply_convert_fusion.5 = f16[256,1024]{1,0:T(8,128)(2,1)} fusion(f32[256,1024]{1,0:T(8,128)S(1)} %get-tuple-element.19, f32[256,1024]{1,0:T(8,128)} %collective-permute-done.3), kind=kLoop, calls=%fused_computation.7 | loop fusion | flops 786432 | bytes 2621440 | tf_op jit(solution)/shard_map/convert_element_type | solution.py:336
  28.3 2.5 %multiply_convert_fusion.7 = f16[256,1024]{1,0:T(8,128)(2,1)} fusion(f32[256,1024]{1,0:T(8,128)} %copy-done.5, f32[256,1024]{1,0:T(8,128)} %collective-permute-done), kind=kLoop, calls=%fused_computation.11 | loop fusion | flops 786432 | bytes 2621440 | tf_op jit(solution)/shard_map/convert_element_type | solution.py:336
  30.9 1.9 %collective-permute-start.1 = (f16[256,1024]{1,0:T(8,128)(2,1)}, f16[256,1024]{1,0:T(8,128)(2,1)}, u32[]{:S(2)}, u32[]{:S(2)}) collective-permute-start(f16[256,1024]{1,0:T(8,128)(2,1)} %multiply_convert_fusion.7), channel_id=1, source_target_pairs={{0,2},{1,3},{2,0},{3,1},{4,6},{5,7},{6,4},{7,5},{8,10},{9,11},{10,... | collective-permute-start | bytes 1572872 | tf_op jit(solution)/shard_map/ppermute | solution.py:21
  34.3 8.9 %collective-permute-done.4 = f16[256,1024]{1,0:T(8,128)(2,1)} collective-permute-done((f16[256,1024]{1,0:T(8,128)(2,1)}, f16[256,1024]{1,0:T(8,128)(2,1)}, u32[]{:S(2)}, u32[]{:S(2)}) %collective-permute-start.4) | collective-permute-done | bytes 524320 | tf_op jit(solution)/shard_map/ppermute | solution.py:21
  44.9 9.0 %collective-permute-done.1 = f16[256,1024]{1,0:T(8,128)(2,1)} collective-permute-done((f16[256,1024]{1,0:T(8,128)(2,1)}, f16[256,1024]{1,0:T(8,128)(2,1)}, u32[]{:S(2)}, u32[]{:S(2)}) %collective-permute-start.1) | collective-permute-done | bytes 524320 | tf_op jit(solution)/shard_map/ppermute | solution.py:21
  57.7 2.3 %copy-done.2 = f32[9,32,16,256]{3,2,1,0:T(8,128)S(1)} copy-done((f32[9,32,16,256]{3,2,1,0:T(8,128)S(1)}, f32[9,32,16,256]{3,2,1,0:T(8,128)}, u32[]{:S(2)}) %copy-start.2) | copy-done | bytes 4718616
  60.1 10.0 %stencil.1.base_ref = f32[288,16,256]{2,1,0:T(8,128)} custom-call(f32[5,288]{1,0:T(8,128)S(1)} %stack.2.coef_ref, f32[288,16,256]{2,1,0:T(8,128)S(1)} %bitcast.47, f32[32,16,256]{2,1,0:T(8,128)S(1)} %get-tuple-element.49.low_ref, f32[32,16,256]{2,1,0:T(8,128)S(1)} %get-tuple-element.48.high_ref, f32[288,256]{1,0:T(8,128)S(1)} %convert_element_type.229.edge_ref, ...), custom_call_target="tpu_custom_call" | custom-call | flops 23592960 | bytes 9437184 | tf_op jit(solution)/shard_map/stencil/pallas_call | solution.py:25
  70.1 5.3 %decode.2 = (f32[288,16,256]{2,1,0:T(8,128)}, f32[256,288]{1,0:T(8,128)S(1)}, f32[256,1024]{1,0:T(8,128)S(1)}, f32[256,1024]{1,0:T(8,128)}) custom-call(s32[1]{0:T(128)} %bitcast.core_ref, bf16[256,1024]{1,0:T(8,128)(2,1)S(1)} %multiply_convert_fusion.4.own_ref, ...), custom_call_target="tpu_custom_call", output_to_operand_aliasing={{0}: (4, {})} | custom-call | flops 905969664 | bytes 10223616 | tf_op jit(solution)/shard_map/decode/pallas_call | solution.py:193
  75.9 5.1 %decode.3 = (f32[288,16,256]{2,1,0:T(8,128)}, f32[256,288]{1,0:T(8,128)S(1)}, f32[256,1024]{1,0:T(8,128)S(1)}, f32[256,1024]{1,0:T(8,128)S(1)}) custom-call(s32[1]{0:T(128)} %bitcast.core_ref, bf16[256,1024]{1,0:T(8,128)(2,1)S(1)} %multiply_convert_fusion.6.own_ref, ...), custom_call_target="tpu_custom_call", output_to_operand_aliasing={{0}: (4, {})} | custom-call | flops 905969664 | bytes 10223616 | tf_op jit(solution)/shard_map/decode/pallas_call | solution.py:193
  85.9 6.3 %collective-permute-done.18 = f16[272,288]{1,0:T(8,128)(2,1)S(1)} collective-permute-done((f16[272,288]{1,0:T(8,128)(2,1)S(1)}, f16[272,288]{1,0:T(8,128)(2,1)S(1)}, u32[]{:S(2)}, u32[]{:S(2)}) %collective-permute-start.18) | collective-permute-done | bytes 156704 | tf_op jit(solution)/shard_map/ppermute | solution.py:21
  99.1 9.8 %collective-permute-done.13 = f16[256,1024]{1,0:T(8,128)(2,1)S(1)} collective-permute-done((f16[256,1024]{1,0:T(8,128)(2,1)S(1)}, f16[256,1024]{1,0:T(8,128)(2,1)S(1)}, u32[]{:S(2)}, u32[]{:S(2)}) %collective-permute-start.13) | collective-permute-done | bytes 524320 | tf_op jit(solution)/shard_map/ppermute | solution.py:21
  109.0 1.8 %multiply_convert_fusion.own_ref = bf16[256,1024]{1,0:T(8,128)(2,1)S(1)} fusion(f16[256,1024]{1,0:T(8,128)(2,1)S(1)} %collective-permute-done.13, f16[256,1024]{1,0:T(8,128)(2,1)S(1)} %multiply_convert_fusion.1, f16[256,1024]{1,0:T(8,128)(2,1)} %collective-permute-done.4, f16[256,1024]{1,0:T(8,128)(2,1)} %multiply_convert_fusion.5, f32[1024]{0:T(1024)S(1)} %bitcast.58), kind=kLoop, calls=%fused_computation | loop fusion | flops 4456448 | bytes 2625536 | tf_op jit(solution)/shard_map/convert_element_type | solution.py:359
  110.9 7.6 %collective-permute-done.10 = f16[256,1024]{1,0:T(8,128)(2,1)S(1)} collective-permute-done((f16[256,1024]{1,0:T(8,128)(2,1)S(1)}, f16[256,1024]{1,0:T(8,128)(2,1)S(1)}, u32[]{:S(2)}, u32[]{:S(2)}) %collective-permute-start.10) | collective-permute-done | bytes 524320 | tf_op jit(solution)/shard_map/ppermute | solution.py:21
  126.7 2.7 %collective-permute-start.20 = (f16[272,288]{1,0:T(8,128)(2,1)S(1)}, f16[272,288]{1,0:T(8,128)(2,1)S(1)}, u32[]{:S(2)}, u32[]{:S(2)}) collective-permute-start(f16[272,288]{1,0:T(8,128)(2,1)S(1)} %pad_maximum_fusion.1), channel_id=1, source_target_pairs={{0,16},{4,20},{8,24},{12,28},{16,0},{20,4},{24,8},{28,12},{1,17},{... | collective-permute-start | bytes 470024 | tf_op jit(solution)/shard_map/ppermute | solution.py:21
  132.0 7.2 %collective-permute-done.20 = f16[272,288]{1,0:T(8,128)(2,1)S(1)} collective-permute-done((f16[272,288]{1,0:T(8,128)(2,1)S(1)}, f16[272,288]{1,0:T(8,128)(2,1)S(1)}, u32[]{:S(2)}, u32[]{:S(2)}) %collective-permute-start.20) | collective-permute-done | bytes 156704 | tf_op jit(solution)/shard_map/ppermute | solution.py:21
  142.1 6.5 %collective-permute-done.17 = f16[304,256]{1,0:T(8,128)(2,1)S(1)} collective-permute-done((f16[304,256]{1,0:T(8,128)(2,1)S(1)}, f16[304,256]{1,0:T(8,128)(2,1)S(1)}, u32[]{:S(2)}, u32[]{:S(2)}) %collective-permute-start.17) | collective-permute-done | bytes 155680 | tf_op jit(solution)/shard_map/ppermute | solution.py:21
  (132 shorter events, 37.7 us)
Async XLA Ops:
  6.9 19.0 %collective-permute-start.3 = (f32[256,1024]{1,0:T(8,128)}, f32[256,1024]{1,0:T(8,128)}, u32[]{:S(2)}, u32[]{:S(2)}) collective-permute-start(f32[256,1024]{1,0:T(8,128)} %get-tuple-element.20), channel_id=1, source_target_pairs={{0,1},{1,0},{2,3},{3,2},{4,5},{5,4},{6,7},{7,6},{8,9},{9,8},{10,11... | collective-permute-start | bytes 3145736 | tf_op jit(solution)/shard_map/ppermute | solution.py:21
  9.5 47.0 %collective-permute-start.6 = (f16[32,16,256]{2,1,0:T(8,128)(2,1)}, f16[32,16,256]{2,1,0:T(8,128)(2,1)}, u32[]{:S(2)}, u32[]{:S(2)}) collective-permute-start(f16[32,16,256]{2,1,0:T(8,128)(2,1)} %get-tuple-element.46), channel_id=1, source_target_pairs={{0,1},{1,0},{2,3},{3,2},{4,5},{5,4},{6,7},{7,6},{8,9},{9,8},{10,11... | collective-permute-start | bytes 786440 | tf_op jit(solution)/shard_map/ppermute | solution.py:21
  9.6 46.9 %collective-permute-start.7 = (f16[32,16,256]{2,1,0:T(8,128)(2,1)}, f16[32,16,256]{2,1,0:T(8,128)(2,1)}, u32[]{:S(2)}, u32[]{:S(2)}) collective-permute-start(f16[32,16,256]{2,1,0:T(8,128)(2,1)} %get-tuple-element.47), channel_id=1, source_target_pairs={{0,3},{1,2},{2,1},{3,0},{4,7},{5,6},{6,5},{7,4},{8,11},{9,10},{10,... | collective-permute-start | bytes 786440 | tf_op jit(solution)/shard_map/ppermute | solution.py:21
  14.7 40.9 %collective-permute-start.8 = (f16[288,256]{1,0:T(8,128)(2,1)}, f16[288,256]{1,0:T(8,128)(2,1)}, u32[]{:S(2)}, u32[]{:S(2)}) collective-permute-start(f16[288,256]{1,0:T(8,128)(2,1)} %fusion), channel_id=1, source_target_pairs={{0,4},{1,5},{4,8},{5,9},{6,2},{7,3},{8,12},{9,13},{10,6},{11,7},{1... | collective-permute-start | bytes 442376 | tf_op jit(solution)/shard_map/ppermute | solution.py:316
  25.3 30.2 %copy-start.11 = (s32[16,256]{1,0:T(8,128)S(1)}, s32[16,256]{1,0:T(8,128)}, u32[]{:S(2)}) copy-start(s32[16,256]{1,0:T(8,128)} %param.11) | copy-start | bytes 49156
  25.3 3.0 %collective-permute-start = (f32[256,1024]{1,0:T(8,128)}, f32[256,1024]{1,0:T(8,128)}, u32[]{:S(2)}, u32[]{:S(2)}) collective-permute-start(f32[256,1024]{1,0:T(8,128)} %get-tuple-element.18), channel_id=1, source_target_pairs={{0,1},{1,0},{2,3},{3,2},{4,5},{5,4},{6,7},{7,6},{8,9},{9,8},{10,11... | collective-permute-start | bytes 3145736 | tf_op jit(solution)/shard_map/ppermute | solution.py:21
  28.2 29.5 %copy-start.8 = (s32[16,256]{1,0:T(8,128)S(1)}, s32[16,256]{1,0:T(8,128)}, u32[]{:S(2)}) copy-start(s32[16,256]{1,0:T(8,128)} %sign_ref.1) | copy-start | bytes 49156
  28.2 15.1 %collective-permute-start.4 = (f16[256,1024]{1,0:T(8,128)(2,1)}, f16[256,1024]{1,0:T(8,128)(2,1)}, u32[]{:S(2)}, u32[]{:S(2)}) collective-permute-start(f16[256,1024]{1,0:T(8,128)(2,1)} %multiply_convert_fusion.5), channel_id=1, source_target_pairs={{0,2},{1,3},{2,0},{3,1},{4,6},{5,7},{6,4},{7,5},{8,10},{9,11},{10,... | collective-permute-start | bytes 1572872 | tf_op jit(solution)/shard_map/ppermute | solution.py:21
  30.9 23.0 %collective-permute-start.1 = (f16[256,1024]{1,0:T(8,128)(2,1)}, f16[256,1024]{1,0:T(8,128)(2,1)}, u32[]{:S(2)}, u32[]{:S(2)}) collective-permute-start(f16[256,1024]{1,0:T(8,128)(2,1)} %multiply_convert_fusion.7), channel_id=1, source_target_pairs={{0,2},{1,3},{2,0},{3,1},{4,6},{5,7},{6,4},{7,5},{8,10},{9,11},{10,... | collective-permute-start | bytes 1572872 | tf_op jit(solution)/shard_map/ppermute | solution.py:21
  33.1 37.0 %slice-start = ((s8[4718592]{0:T(1024)(128)(4,1)}), s8[524288]{0:T(1024)(128)(4,1)S(1)}, s32[]{:S(2)}) async-start(s8[4718592]{0:T(1024)(128)(4,1)} %bitcast.48), calls=%async_computation | async-start | bytes 1048576
  44.8 25.3 %collective-permute-start.5 = (bf16[256,1024]{1,0:T(8,128)(2,1)S(1)}, bf16[256,1024]{1,0:T(8,128)(2,1)S(1)}, u32[]{:S(2)}, u32[]{:S(2)}) collective-permute-start(bf16[256,1024]{1,0:T(8,128)(2,1)S(1)} %multiply_convert_fusion.4.own_ref), channel_id=1, source_target_pairs={{0,1},{1,0},{2,3},{3,2},{4,5},{5,4},{6,7},{7,6},{8,9},{9,8},{10,11... | collective-permute-start | bytes 1572872 | tf_op jit(solution)/shard_map/ppermute | solution.py:21
  55.4 20.5 %collective-permute-start.2 = (bf16[256,1024]{1,0:T(8,128)(2,1)S(1)}, bf16[256,1024]{1,0:T(8,128)(2,1)S(1)}, u32[]{:S(2)}, u32[]{:S(2)}) collective-permute-start(bf16[256,1024]{1,0:T(8,128)(2,1)S(1)} %multiply_convert_fusion.6.own_ref), channel_id=1, source_target_pairs={{0,1},{1,0},{2,3},{3,2},{4,5},{5,4},{6,7},{7,6},{8,9},{9,8},{10,11... | collective-permute-start | bytes 1572872 | tf_op jit(solution)/shard_map/ppermute | solution.py:21
  75.4 16.9 %collective-permute-start.12 = (f32[256,1024]{1,0:T(8,128)}, f32[256,1024]{1,0:T(8,128)}, u32[]{:S(2)}, u32[]{:S(2)}) collective-permute-start(f32[256,1024]{1,0:T(8,128)} %get-tuple-element.29), channel_id=1, source_target_pairs={{0,1},{1,0},{2,3},{3,2},{4,5},{5,4},{6,7},{7,6},{8,9},{9,8},{10,11... | collective-permute-start | bytes 3145736 | tf_op jit(solution)/shard_map/ppermute | solution.py:21
  84.4 10.0 %collective-permute-start.9 = (f32[256,1024]{1,0:T(8,128)}, f32[256,1024]{1,0:T(8,128)}, u32[]{:S(2)}, u32[]{:S(2)}) collective-permute-start(f32[256,1024]{1,0:T(8,128)} %copy-done.9), channel_id=1, source_target_pairs={{0,1},{1,0},{2,3},{3,2},{4,5},{5,4},{6,7},{7,6},{8,9},{9,8},{10,11... | collective-permute-start | bytes 3145736 | tf_op jit(solution)/shard_map/ppermute | solution.py:21
  84.9 7.3 %collective-permute-start.18 = (f16[272,288]{1,0:T(8,128)(2,1)S(1)}, f16[272,288]{1,0:T(8,128)(2,1)S(1)}, u32[]{:S(2)}, u32[]{:S(2)}) collective-permute-start(f16[272,288]{1,0:T(8,128)(2,1)S(1)} %concatenate.21), channel_id=1, source_target_pairs={{0,4},{4,0},{8,12},{12,8},{16,20},{20,16},{24,28},{28,24},{1,5},{5... | collective-permute-start | bytes 470024 | tf_op jit(solution)/shard_map/ppermute | solution.py:21
  94.0 14.9 %collective-permute-start.13 = (f16[256,1024]{1,0:T(8,128)(2,1)S(1)}, f16[256,1024]{1,0:T(8,128)(2,1)S(1)}, u32[]{:S(2)}, u32[]{:S(2)}) collective-permute-start(f16[256,1024]{1,0:T(8,128)(2,1)S(1)} %multiply_convert_fusion.1), channel_id=1, source_target_pairs={{0,2},{1,3},{2,0},{3,1},{4,6},{5,7},{6,4},{7,5},{8,10},{9,11},{10,... | collective-permute-start | bytes 1572872 | tf_op jit(solution)/shard_map/ppermute | solution.py:21
  96.2 22.4 %collective-permute-start.10 = (f16[256,1024]{1,0:T(8,128)(2,1)S(1)}, f16[256,1024]{1,0:T(8,128)(2,1)S(1)}, u32[]{:S(2)}, u32[]{:S(2)}) collective-permute-start(f16[256,1024]{1,0:T(8,128)(2,1)S(1)} %multiply_convert_fusion.3), channel_id=1, source_target_pairs={{0,2},{1,3},{2,0},{3,1},{4,6},{5,7},{6,4},{7,5},{8,10},{9,11},{10,... | collective-permute-start | bytes 1572872 | tf_op jit(solution)/shard_map/ppermute | solution.py:21
  98.2 22.3 %collective-permute-start.19 = (f16[272,288]{1,0:T(8,128)(2,1)S(1)}, f16[272,288]{1,0:T(8,128)(2,1)S(1)}, u32[]{:S(2)}, u32[]{:S(2)}) collective-permute-start(f16[272,288]{1,0:T(8,128)(2,1)S(1)} %pad_maximum_fusion), channel_id=1, source_target_pairs={{0,8},{4,12},{8,0},{12,4},{16,24},{20,28},{24,16},{28,20},{1,9},{5... | collective-permute-start | bytes 470024 | tf_op jit(solution)/shard_map/ppermute | solution.py:21
  110.8 9.7 %collective-permute-start.14 = (bf16[256,1024]{1,0:T(8,128)(2,1)S(1)}, bf16[256,1024]{1,0:T(8,128)(2,1)S(1)}, u32[]{:S(2)}, u32[]{:S(2)}) collective-permute-start(bf16[256,1024]{1,0:T(8,128)(2,1)S(1)} %multiply_convert_fusion.own_ref), channel_id=1, source_target_pairs={{0,1},{1,0},{2,3},{3,2},{4,5},{5,4},{6,7},{7,6},{8,9},{9,8},{10,11... | collective-permute-start | bytes 1572872 | tf_op jit(solution)/shard_map/ppermute | solution.py:21
  120.3 2.0 %collective-permute-start.11 = (bf16[256,1024]{1,0:T(8,128)(2,1)S(1)}, bf16[256,1024]{1,0:T(8,128)(2,1)S(1)}, u32[]{:S(2)}, u32[]{:S(2)}) collective-permute-start(bf16[256,1024]{1,0:T(8,128)(2,1)S(1)} %multiply_convert_fusion.2.own_ref), channel_id=1, source_target_pairs={{0,1},{1,0},{2,3},{3,2},{4,5},{5,4},{6,7},{7,6},{8,9},{9,8},{10,11... | collective-permute-start | bytes 1572872 | tf_op jit(solution)/shard_map/ppermute | solution.py:21
  124.7 6.1 %collective-permute-start.15 = (f16[304,256]{1,0:T(8,128)(2,1)S(1)}, f16[304,256]{1,0:T(8,128)(2,1)S(1)}, u32[]{:S(2)}, u32[]{:S(2)}) collective-permute-start(f16[304,256]{1,0:T(8,128)(2,1)S(1)} %concatenate.18), channel_id=1, source_target_pairs={{0,4},{4,0},{8,12},{12,8},{16,20},{20,16},{24,28},{28,24},{1,5},{5... | collective-permute-start | bytes 466952 | tf_op jit(solution)/shard_map/ppermute | solution.py:21
  126.7 12.5 %collective-permute-start.20 = (f16[272,288]{1,0:T(8,128)(2,1)S(1)}, f16[272,288]{1,0:T(8,128)(2,1)S(1)}, u32[]{:S(2)}, u32[]{:S(2)}) collective-permute-start(f16[272,288]{1,0:T(8,128)(2,1)S(1)} %pad_maximum_fusion.1), channel_id=1, source_target_pairs={{0,16},{4,20},{8,24},{12,28},{16,0},{20,4},{24,8},{28,12},{1,17},{... | collective-permute-start | bytes 470024 | tf_op jit(solution)/shard_map/ppermute | solution.py:21
  131.0 8.7 %collective-permute-start.16 = (f16[304,256]{1,0:T(8,128)(2,1)S(1)}, f16[304,256]{1,0:T(8,128)(2,1)S(1)}, u32[]{:S(2)}, u32[]{:S(2)}) collective-permute-start(f16[304,256]{1,0:T(8,128)(2,1)S(1)} %pad_maximum_fusion.2), channel_id=1, source_target_pairs={{0,8},{4,12},{8,0},{12,4},{16,24},{20,28},{24,16},{28,20},{1,9},{5... | collective-permute-start | bytes 466952 | tf_op jit(solution)/shard_map/ppermute | solution.py:21
  139.9 8.7 %collective-permute-start.17 = (f16[304,256]{1,0:T(8,128)(2,1)S(1)}, f16[304,256]{1,0:T(8,128)(2,1)S(1)}, u32[]{:S(2)}, u32[]{:S(2)}) collective-permute-start(f16[304,256]{1,0:T(8,128)(2,1)S(1)} %pad_maximum_fusion.3), channel_id=1, source_target_pairs={{0,16},{4,20},{8,24},{12,28},{16,0},{20,4},{24,8},{28,12},{1,17},{... | collective-permute-start | bytes 466952 | tf_op jit(solution)/shard_map/ppermute | solution.py:21
  (12 other events, 48.8 us)

commit v2 on v0

v2 whole, which is shorter than its diff:
```python
import math

import jax
import jax.numpy as jnp
import numpy as np
from jax import lax
from jax.experimental import pallas as pl
from jax.experimental.pallas import tpu as pltpu
from jax.sharding import PartitionSpec as P

NDIR = 36
ROWS = 8
LANES = 128
PRE_SCALE = 64.0
BACK_SCALE = 2.0**-8
POWER_ROWS = 16

BF16, F16, F32 = jnp.bfloat16, jnp.float16, jnp.float32
VMEM = pl.BlockSpec(memory_space=pltpu.VMEM)
SMEM = pl.BlockSpec(memory_space=pltpu.SMEM)
HBM = pl.BlockSpec(memory_space=pltpu.HBM)
ANY = pl.BlockSpec(memory_space=pl.ANY)


def swap(value, axis, bit):
    count = lax.axis_size(axis)
    return lax.ppermute(value, axis, [(i, i ^ bit) for i in range(count)])


def call(body, ins, outs, cost, after=(), aliases=None, scratch=(), limit=16, name=None):
    n = len(ins)

    def run(*refs):
        body(*refs[:n], *refs[n + len(after) :])

    return pl.pallas_call(
        run,
        in_specs=[spec for _, spec in ins] + [ANY] * len(after),
        out_specs=[VMEM if len(out) == 2 else out[2] for out in outs],
        out_shape=[jax.ShapeDtypeStruct(*out[:2]) for out in outs],
        scratch_shapes=list(scratch),
        input_output_aliases=aliases or {},
        compiler_params=pltpu.CompilerParams(vmem_limit_bytes=limit << 20),
        cost_estimate=pl.CostEstimate(flops=cost[0], bytes_accessed=cost[1], transcendentals=0),
        name=name,
    )(*[value for value, _ in ins], *after)


def first_row(core, own):
    half = ROWS // 2
    return core * half if own else (1 - core) * half


def pick(ref, core, own, chunk, i, j):
    at = chunk * ROWS + i
    lanes = slice(j * LANES, (j + 1) * LANES)
    low, high = ref[at : at + 1, lanes], ref[at + ROWS // 2 : at + ROWS // 2 + 1, lanes]
    return jnp.where((core == 0) == own, low, high).astype(F32)


def count_of(count_ref, core, own, chunk, i):
    value = count_ref[chunk * ROWS + first_row(core, own) + i]
    return jnp.full((1, LANES), value, jnp.int32).astype(F32)


def encode_rows(place_ref, tiles_ref, mask_ref, w_ref, spec_ref, out_ref, chunk, own):
    parts, bins = tiles_ref.shape[1:3]
    half = ROWS // 2
    wide = half * LANES
    core = place_ref[0] % 2
    first = first_row(core, own)
    for j in range(parts):
        flat = tiles_ref.at[chunk, j].reshape(bins * ROWS, LANES)
        cols = []
        for i in range(half):
            row = flat[pl.ds(first + i, bins, stride=ROWS), :]
            cols.append((row * pick(mask_ref, core, own, chunk, i, j)).astype(BF16))
        field = jnp.concatenate(cols, axis=1)
        spec_ref[:, j * wide : (j + 1) * wide] = field
        out_ref[:, j * wide : (j + 1) * wide] = lax.dot_general(
            w_ref[...], field, (((0,), (0,)), ((), ())), preferred_element_type=F32
        )


def encode_first(place, state, mask, w_in, after=()):
    bins, rows, lon = state.shape
    hidden = w_in.shape[1]
    chunks, parts = rows // ROWS, lon // LANES
    cells = parts * ROWS * LANES // 2

    def body(place_ref, state_ref, mask_ref, w_ref, tiles_ref, spec_ref, out_ref, sems):
        copies = [
            [
                pltpu.make_async_copy(
                    state_ref.at[:, pl.ds(c * ROWS, ROWS), pl.ds(j * LANES, LANES)],
                    tiles_ref.at[c, j],
                    sems.at[c * parts + j],
                )
                for j in range(parts)
            ]
            for c in range(chunks)
        ]
        for row in copies:
            for copy in row:
                copy.start()
        for copy in copies[0]:
            copy.wait()
        encode_rows(place_ref, tiles_ref, mask_ref, w_ref, spec_ref, out_ref, 0, False)
        for row in copies[1:]:
            for copy in row:
                copy.wait()

    return call(
        body,
        [(place, SMEM), (state, HBM), (mask, VMEM), (w_in, VMEM)],
        [((chunks, parts, bins, ROWS, LANES), F32), ((bins, cells), BF16), ((hidden, cells), F32)],
        (2 * bins * hidden * cells, 4 * bins * rows * lon),
        scratch=[pltpu.SemaphoreType.DMA((chunks * parts,))],
        after=after,
        limit=54,
        name="encode_first",
    )


def encode(place, tiles, mask, w_in, chunk, own, after=()):
    parts, bins = tiles.shape[1:3]
    hidden = w_in.shape[1]
    cells = parts * ROWS * LANES // 2

    def body(*refs):
        encode_rows(*refs, chunk, own)

    return call(
        body,
        [(place, SMEM), (tiles, VMEM), (mask, VMEM), (w_in, VMEM)],
        [((bins, cells), BF16), ((hidden, cells), F32)],
        (2 * bins * hidden * cells, 4 * bins * cells),
        after=after,
        name="encode",
    )


def stencil(place, coef, tiles, low, high, edge, mask, sign, count, target, chunk, ndir, after=()):
    chunks, parts, bins = tiles.shape[:3]
    nfreq = bins // ndir
    half = ROWS // 2
    wide = half * LANES

    def body(
        place_ref, coef_ref, tiles_ref, low_ref, high_ref, edge_ref, mask_ref, sign_ref, count_ref, target_ref,
        base_ref, goal_ref, unit_ref, down_ref, up_ref, sems,
    ):
        copies = []
        for j in range(parts):
            copy = pltpu.make_async_copy(
                target_ref.at[:, pl.ds(chunk * ROWS, ROWS), pl.ds(j * LANES, LANES)], goal_ref.at[j], sems.at[j]
            )
            copy.start()
            copies.append(copy)
        place = place_ref[0]
        unit_ref[...] = jnp.full(unit_ref.shape, 1.0 / PRE_SCALE, F32)
        for i in range(half):
            counts = count_of(count_ref, place % 2, False, chunk, i)
            for j in range(parts):
                at = slice(j * wide + i * LANES, j * wide + (i + 1) * LANES)
                down_ref[:, at] = counts * BACK_SCALE
                up_ref[:, at] = (1.0 / BACK_SCALE) / counts
        lane = lax.broadcasted_iota(jnp.int32, (ROWS, LANES), 1)
        row = lax.broadcasted_iota(jnp.int32, (ROWS, LANES), 0)

        def plane(ref, c, j):
            return ref[c * ROWS : (c + 1) * ROWS, j * LANES : (j + 1) * LANES]

        masks = [[plane(mask_ref, c, j).astype(F32) for j in range(parts)] for c in range(chunks)]
        ahead = [plane(sign_ref, chunk, j) > 0 for j in range(parts)]

        def quadrant(q):
            east = q in (1, 2)
            north = q in (2, 3)
            beside = chunk + 1 if north else chunk - 1

            def sector(d, below, above):
                def group(g, _):
                    start = pl.multiple_of(d * nfreq + g * 8, 8)
                    edges = None
                    if not 0 <= beside < chunks:
                        edges = [edge_ref[j, pl.ds(start, 8), :] for j in range(parts)]
                    for u in range(8):
                        b, f = start + u, g * 8 + u
                        here = [tiles_ref[chunk, j, b] for j in range(parts)]
                        field = [here[j] * masks[chunk][j] for j in range(parts)]
                        for j in range(parts):
                            k = j + 1 if east else j - 1
                            outer = field[k] if 0 <= k < parts else 0.0
                            if east:
                                x = pltpu.roll(jnp.where(lane == 0, outer, field[j]), LANES - 1, 1)
                            else:
                                x = pltpu.roll(jnp.where(lane == LANES - 1, outer, field[j]), 1, 1)
                            if edges is None:
                                outer = tiles_ref[beside, j, b] * masks[beside][j]
                            else:
                                outer = jnp.broadcast_to(edges[j][u : u + 1], (ROWS, LANES))
                            if north:
                                y = pltpu.roll(jnp.where(row == 0, outer, field[j]), ROWS - 1, 0)
                            else:
                                y = pltpu.roll(jnp.where(row == ROWS - 1, outer, field[j]), 1, 0)
                            upstream = jnp.where(ahead[j], below(b, f, j), above(b, f, j))
                            total = coef_ref[3 * q, b] * here[j] + coef_ref[3 * q + 1, b] * x
                            total = total + (coef_ref[3 * q + 2, b] * y + 0.3 * upstream)
                            base_ref[j, b] = total * masks[chunk][j]
                    return 0

                lax.fori_loop(0, nfreq // 8, group, 0)

            def halo(ref):
                return lambda b, f, j: ref[f, chunk * ROWS : (chunk + 1) * ROWS, j * LANES : (j + 1) * LANES]

            def inside(shift):
                return lambda b, f, j: tiles_ref[chunk, j, b + shift]

            sector(0, halo(low_ref), inside(nfreq))

            def middle(d, _):
                sector(d, inside(-nfreq), inside(nfreq))
                return 0

            lax.fori_loop(1, ndir - 1, middle, 0)
            sector(ndir - 1, inside(-nfreq), halo(high_ref))

        for q in range(4):
            pl.when(place == q)(lambda q=q: quadrant(q))
        for copy in copies:
            copy.wait()

    cells = parts * ROWS * LANES
    return call(
        body,
        [(place, SMEM), (coef, SMEM)]
        + [(v, VMEM) for v in (tiles, low, high, edge, mask, sign)]
        + [(count, SMEM), (target, HBM)],
        [
            ((parts, bins, ROWS, LANES), F32),
            ((parts, bins, ROWS, LANES), F32),
            ((1, cells // 2), F32),
            ((1, cells // 2), F32),
            ((1, cells // 2), F32),
        ],
        (40 * bins * cells, 8 * bins * cells),
        scratch=[pltpu.SemaphoreType.DMA((parts,))],
        after=after,
        limit=32,
        name="stencil",
    )


def decode(place, hid, w_out, base, goal, mask, count, seed, chunk, own, after=()):
    parts, bins = base.shape[:2]
    hidden = w_out.shape[1]
    half = ROWS // 2
    wide = half * LANES
    cells = parts * wide
    seeds = [seed] if seed is not None else []

    def body(place_ref, count_ref, hid_ref, w_ref, base_ref, goal_ref, mask_ref, *refs):
        next_ref, grad_ref, out_ref, unit_ref, back_ref = refs[len(seeds) :]
        core = place_ref[0] % 2
        first = first_row(core, own)
        unit_ref[...] = jnp.full(unit_ref.shape, 1.0 / PRE_SCALE, F32)
        total = refs[0][...] if seeds else jnp.zeros(grad_ref.shape, F32)
        for j in range(parts):
            base = base_ref.at[j].reshape(bins * ROWS, LANES)
            goal = goal_ref.at[j].reshape(bins * ROWS, LANES)
            result = next_ref.at[j].reshape(bins * ROWS, LANES)
            hid = hid_ref[:, j * wide : (j + 1) * wide]
            source = jnp.dot(w_ref[...], hid, preferred_element_type=F32)
            for i in range(half):
                at = pl.ds(first + i, bins, stride=ROWS)
                mask = pick(mask_ref, core, own, chunk, i, j)
                weight = (1.0 / count_of(count_ref, core, own, chunk, i)) * mask
                part = source[:, i * LANES : (i + 1) * LANES]
                new = base[at, :] + (0.5 * mask) * part
                result[at, :] = new
                back_ref[:, i * LANES : (i + 1) * LANES] = (weight * (new - goal[at, :])).astype(BF16)
            back = back_ref[...]
            total = total + lax.dot_general(back, hid, (((1,), (1,)), ((), ())), preferred_element_type=F32)
            out_ref[:, j * wide : (j + 1) * wide] = lax.dot_general(
                w_ref[...], back, (((0,), (0,)), ((), ())), preferred_element_type=F32
            )
        grad_ref[...] = total

    return call(
        body,
        [(place, SMEM), (count, SMEM)] + [(v, VMEM) for v in (hid, w_out, base, goal, mask, *seeds)],
        [(base.shape, F32), ((bins, hidden), F32), ((hidden, cells), F32), ((1, cells), F32)],
        (6 * bins * hidden * cells, 12 * bins * cells),
        scratch=[pltpu.VMEM((bins, wide), BF16)],
        aliases={4: 0},
        after=after,
        name="decode",
    )


def store(nexts, rows, after=()):
    parts, bins = nexts[0].shape[:2]
    n = len(nexts)

    def body(*refs):
        copies = []
        for c in range(n):
            for j in range(parts):
                to = refs[n].at[:, pl.ds(c * ROWS, ROWS), pl.ds(j * LANES, LANES)]
                copies.append(pltpu.make_async_copy(refs[c].at[j], to, refs[n + 1].at[c * parts + j]))
        for copy in copies:
            copy.start()
        for copy in copies:
            copy.wait()

    size = bins * rows * parts * LANES
    return call(
        body,
        [(v, VMEM) for v in nexts],
        [((bins, rows, parts * LANES), F32, HBM)],
        (0, 8 * size),
        scratch=[pltpu.SemaphoreType.DMA((n * parts,))],
        after=after,
        name="store",
    )[0]


def write_packed(ref, total):
    n = total.shape[0]
    most = jnp.max(jnp.max(jnp.abs(total), axis=1, keepdims=True), axis=0, keepdims=True)
    power = jnp.ceil(jnp.log2(jnp.maximum(most, 2.0**-100)))
    ref[0:n, :] = total
    ref[n:, :] = jnp.broadcast_to(power, (POWER_ROWS, total.shape[1]))


def pack(total, after=()):
    def body(total_ref, out_ref):
        write_packed(out_ref, total_ref[...])

    n, width = total.shape
    return call(
        body, [(total, VMEM)], [((n + POWER_ROWS, width), F32)], (n * width, 8 * n * width), after=after, name="pack"
    )[0]


def collect(spec, back, seed, last=False, after=()):
    bins, cells = spec.shape
    hidden = back.shape[0]
    seeds = [seed] if seed is not None else []

    def body(spec_ref, back_ref, *refs):
        total = lax.dot_general(spec_ref[...], back_ref[...], (((1,), (1,)), ((), ())), preferred_element_type=F32)
        if seeds:
            total = total + refs[0][...]
        if last:
            write_packed(refs[-1], total)
        else:
            refs[-1][...] = total

    return call(
        body,
        [(v, VMEM) for v in (spec, back, *seeds)],
        [((bins + (POWER_ROWS if last else 0), hidden), F32)],
        (2 * bins * hidden * cells, 2 * bins * cells + 2 * hidden * cells),
        after=after,
        name="collect",
    )[0]


def space_sum(packed):
    n = packed.shape[0] - POWER_ROWS
    body = lax.broadcasted_iota(jnp.int32, packed.shape, 0) < n
    count = lax.axis_size("space")
    assert count & (count - 1) == 0
    total = packed
    bit = 1
    while bit < count:
        power = total[n : n + 1]
        mine = jnp.where(body, total * jnp.exp2(-power), total).astype(F16)
        other = swap(mine, "space", bit)
        mine, other = mine.astype(F32), other.astype(F32)
        here, there = mine[n : n + 1], other[n : n + 1]
        total = jnp.where(
            body, mine * jnp.exp2(here) + other * jnp.exp2(there), jnp.maximum(mine, other) + 1.0
        )
        bit *= 2
    return total[:n]


def courant(sectors, ndir, nfreq):
    angle = 2.0 * math.pi * (np.arange(NDIR) + 0.5) / NDIR
    speed = 1.0 / (1.0 + 2.3 * np.arange(nfreq) / nfreq)
    cx = np.abs(0.4 * np.cos(angle)[:, None] * speed[None, :])
    cy = np.abs(0.4 * np.sin(angle)[:, None] * speed[None, :])
    table = np.stack([1.0 - cx - cy - 0.3, cx, cy]).reshape(3, sectors, ndir * nfreq)
    return np.ascontiguousarray(table.transpose(1, 0, 2).reshape(3 * sectors, ndir * nfreq), np.float32)


def on_device(state, target, w_in, w_out, sea_mask, sea_count, turn_sign):
    ndir, nfreq, rows, lon = state.shape
    bins = ndir * nfreq
    hidden = w_in.shape[2]
    place = lax.axis_index("dir")
    sectors = lax.axis_size("dir")
    spaces = lax.axis_size("space")
    assert sectors == 4 and ndir * sectors == NDIR
    chunks, parts = rows // ROWS, lon // LANES
    upper = place % 2 == 1
    north = place >= sectors // 2
    place_ref = place.reshape(1)
    state = state.reshape(bins, rows, lon)
    target = target.reshape(bins, rows, lon)
    w_in = w_in.reshape(bins, hidden)
    w_out = jnp.transpose(w_out, (1, 2, 0)).reshape(bins, hidden)
    coef = jnp.asarray(courant(sectors, ndir, nfreq))

    def edge_bin(first):
        start = jnp.where(first, 0, bins - nfreq)
        return lax.dynamic_slice_in_dim(state, start, nfreq, 0).astype(F16)

    far = swap(edge_bin(jnp.logical_not(upper)), "dir", 3)
    near = swap(edge_bin(upper), "dir", 1)
    at = jnp.where(north, 0, rows - 1)
    edge = lax.dynamic_index_in_dim(state, at, 1, False)
    edge = edge * lax.dynamic_index_in_dim(sea_mask, at, 0, True).astype(F32)
    pairs = []
    for s in range(spaces):
        for d in range(sectors):
            to = s - 1 if d >= sectors // 2 else s + 1
            if 0 <= to < spaces:
                pairs.append((s * sectors + d, to * sectors + d))
    edge = lax.ppermute(edge.astype(F16), ("space", "dir"), pairs).astype(F32)
    edge = jnp.stack([edge[:, j * LANES : (j + 1) * LANES] for j in range(parts)])
    low = jnp.where(upper, near, far).astype(F32)
    high = jnp.where(upper, far, near).astype(F32)

    tiles, spec, send = encode_first(place_ref, state, sea_mask, w_in)
    specs, owns, sends = {(0, 0): spec}, [], [send]
    for c in range(chunks):
        for own in (0, 1):
            if (c, own) not in specs:
                specs[c, own], out = encode(place_ref, tiles, sea_mask, w_in, c, bool(own))
                (owns if own else sends).append(out)
    chips = [((owns[c] + swap(sends[c], "dir", 1)) * PRE_SCALE).astype(F16) for c in range(chunks)]

    stencils = []
    for c in range(chunks):
        stencils.append(
            stencil(
                place_ref, coef, tiles, low, high, edge, sea_mask, turn_sign, sea_count, target, c, ndir,
                after=owns[-1:] if c == 0 else [stencils[-1][2]],
            )
        )
    unit = stencils[-1][2]

    grad_out = None
    backs, slopes, nexts, tokens = [], [], [], []
    for c in range(chunks):
        base, goal, _, down, up = stencils[c]
        pre = (chips[c].astype(F32) + swap(chips[c], "dir", 2).astype(F32)) * unit
        hid = jax.nn.silu(pre).astype(BF16)
        sig = jax.nn.sigmoid(pre)
        slopes.append(swap(sig * (1.0 + pre * (1.0 - sig)), "dir", 1))
        other = swap(hid, "dir", 1)
        base, grad_out, send, _ = decode(
            place_ref, hid, w_out, base, goal, sea_mask, sea_count, grad_out, c, True, after=tokens[-1:]
        )
        base, grad_out, own, unit = decode(
            place_ref, other, w_out, base, goal, sea_mask, sea_count, grad_out, c, False
        )
        nexts.append(base)
        backs.append((((own + swap(send, "dir", 1)) * down).astype(F16), up))
        tokens.append(backs[-1][0][:8, :LANES].astype(F32))

    next_state = store(nexts, rows, after=tokens[-1:])
    grad_out = space_sum(pack(grad_out, after=tokens[-1:]))

    grad_in = None
    for c in range(chunks):
        chip, up = backs[c]
        back = (chip.astype(F32) + swap(chip, "dir", 2).astype(F32)) * up
        back = (back * slopes[c]).astype(BF16)
        last = c + 1 == chunks
        grad_in = collect(specs[c, 0], back, grad_in, after=[grad_out] if last else [])
        grad_in = collect(specs[c, 1], swap(back, "dir", 1), grad_in, last=last)

    grad_in = space_sum(grad_in)
    return (
        next_state.reshape(ndir, nfreq, rows, lon),
        grad_in.reshape(ndir, nfreq, hidden),
        jnp.transpose(grad_out.reshape(ndir, nfreq, hidden), (2, 0, 1)),
    )


def solution(mesh):
    in_specs = (
        P("dir", None, "space", None),
        P("dir", None, "space", None),
        P("dir", None, None),
        P(None, "dir", None),
        P("space", None),
        P("space"),
        P("space", None),
    )
    out_specs = (P("dir", None, "space", None), P("dir", None, None), P(None, "dir", None))
    return jax.shard_map(
        on_device, mesh=mesh, in_specs=in_specs, out_specs=out_specs, check_vma=False
    )
```

time: 320 us -> 115 us (0.36)
  waiting for transfers between devices: 236 us -> 49.3 us
  matrix products: 40.3 us -> 0 us
  Pallas kernels: 0 us -> 31.2 us
  starting transfers between devices: 8.27 us -> 22.8 us
  between operations: 13.9 us -> 1.31 us
  local copies, waits for them, and re-layouts: 15.6 us -> 4.3 us
    psum x3 -> x0, waiting for transfers between devices: 213 us -> none  [the longest x1 81.2 us: on_device(): back_hidden = lax.psum(partial_back, 'dir')]
    dot_general x5 -> x0, matrix products: 40.3 us -> none  [the longest x1 20.1 us: on_device(): jnp.einsum('hyx,hdf->dfyx', hidden, w_out, preferred_element_type=jnp.flo...]
    pallas_call x0 -> x16, Pallas kernels: none -> 31.2 us  [call(): pl.pallas_call(run, in_specs=[spec for _, spec in ins] + [ANY] * len(afte...]
    ppermute x4 -> x23, waiting for transfers between devices: 22.9 us -> 49.3 us  [the longest x22 49.3 us: swap(): return lax.ppermute(value, axis, [(i, i ^ bit) for i in range(count)])]
    ppermute x4 -> x23, starting transfers between devices: 7.97 us -> 22.8 us  [the longest x22 18.3 us: swap(): return lax.ppermute(value, axis, [(i, i ^ bit) for i in range(count)])]
    unnamed x17 -> x26, local copies, waits for them, and re-layouts: 12.9 us -> 2.41 us
    mul x3 -> x2, other arithmetic: 5.23 us -> 0.95 us  [on_device(): slopes.append(swap(sig * (1.0 + pre * (1.0 - sig)), 'dir', 1))]
  transfers between devices with their start and end apart: 7 -> 23, of which waited for: 6 -> 11; matrix products, arithmetic and copies ran while one was open for 5% -> 6% of each run, Pallas kernels for 0% -> 21%
where the time goes in v2:
time: 115 us
  waiting for transfers between devices  49.3 us (43%)
  Pallas kernels  31.2 us (27%)
  starting transfers between devices  22.8 us (20%)
  other arithmetic  6.25 us (5%)
  local copies, waits for them, and re-layouts  4.3 us (4%)
  between operations  1.31 us (1%)
    ppermute x22, waiting for transfers between devices, swap(): return lax.ppermute(value, axis, [(i, i ^ bit) for i in range(count)])  49.3 us
    pallas_call x16, Pallas kernels, call(): pl.pallas_call(run, in_specs=[spec for _, spec in ins] + [ANY] * len(afte...  31.2 us
    ppermute x22, starting transfers between devices, swap(): return lax.ppermute(value, axis, [(i, i ^ bit) for i in range(count)])  18.3 us
    ppermute x1, starting transfers between devices, on_device(): edge = lax.ppermute(edge.astype(F16), ('space', 'dir'), pairs).astype(F32)  4.46 us
    unnamed x26, local copies, waits for them, and re-layouts  2.41 us
  transfers between devices with their start and end apart: 23, of which 11 were waited for; matrix products, arithmetic and copies ran while one was open for 6% of the time, Pallas kernels for 21%

profile of v2, /device:TPU:0, one launch (start us, length us, event | category | flops | bytes accessed | tf_op | source)
XLA Modules:
  0.0 115.1 jit_solution(13740366983816549995)
XLA Ops:
  0.6 6.1 %encode_first.1 = (f32[2,2,288,8,128]{4,3,2,1,0:T(8,128)}, bf16[288,1024]{1,0:T(8,128)(2,1)}, f32[256,1024]{1,0:T(8,128)}) custom-call(s32[1]{0:T(128)} %bitcast.refs_0_, f32[288,16,256]{2,1,0:T(8,128)} %bitcast.67, s32[16,256]{1,0:T(8,128)} %refs_6_.11, bf16[288,256]{1,0:T(8,128)(2,1)} %bitcast.52), custom_call_target="tpu_custom_call" | custom-call | flops 150994944 | bytes 4718592 | tf_op jit(solution)/shard_map/encode_first/pallas_call | solution.py:36
  7.3 1.9 %constant_dynamic-slice_fusion = f32[288,1,256]{2,1,0:T(1,128)S(1)} fusion(f32[288,16,256]{2,1,0:T(8,128)} %bitcast.68, s32[]{:T(128)S(6)} %select_n.78), kind=kLoop, calls=%fused_computation.87 | loop fusion | bytes 589828 | tf_op jit(solution)/shard_map/jit(dynamic_index_in_dim)/dynamic_slice | solution.py:426
  9.2 4.5 %collective-permute-start.4 = (f16[288,256]{1,0:T(8,128)(2,1)S(1)}, f16[288,256]{1,0:T(8,128)(2,1)S(1)}, u32[]{:S(2)}, u32[]{:S(2)}) collective-permute-start(f16[288,256]{1,0:T(8,128)(2,1)S(1)} %fusion.6), channel_id=1, source_target_pairs={{0,4},{1,5},{4,8},{5,9},{6,2},{7,3},{8,12},{9,13},{10,6},{11,7},{1... | collective-permute-start | bytes 442376 | tf_op jit(solution)/shard_map/ppermute | solution.py:434
  15.4 2.3 %copy-done = f32[2,2,288,8,128]{4,3,2,1,0:T(8,128)S(1)} copy-done((f32[2,2,288,8,128]{4,3,2,1,0:T(8,128)S(1)}, f32[2,2,288,8,128]{4,3,2,1,0:T(8,128)}, u32[]{:S(2)}) %copy-start) | copy-done | bytes 4718616
  20.0 1.8 %collective-permute-start.1 = (f16[256,1024]{1,0:T(8,128)(2,1)S(1)}, f16[256,1024]{1,0:T(8,128)(2,1)S(1)}, u32[]{:S(2)}, u32[]{:S(2)}) collective-permute-start(f16[256,1024]{1,0:T(8,128)(2,1)S(1)} %multiply_convert_fusion.7), channel_id=1, source_target_pairs={{0,2},{1,3},{2,0},{3,1},{4,6},{5,7},{6,4},{7,5},{8,10},{9,11},{10,... | collective-permute-start | bytes 1572872 | tf_op jit(solution)/shard_map/ppermute | solution.py:27
  23.7 4.6 %stencil.2 = (f32[2,288,8,128]{3,2,1,0:T(8,128)S(1)}, f32[2,288,8,128]{3,2,1,0:T(8,128)S(1)}, f32[1,1024]{1,0:T(1,128)S(1)}, f32[1,1024]{1,0:T(1,128)S(1)}, f32[1,1024]{1,0:T(1,128)S(1)}) custom-call(s32[1]{0:T(128)} %bitcast.refs_0_, f32[12,288]{1,0:T(8,128)S(1)} %copy-done.6, f32[2,2,288,8,128]{4,3,2,1,0:T(8,128)S(1)} %bitcast.47, ...), custom_call_target="tpu_custom_call" | custom-call | flops 23592960 | bytes 4718592 | tf_op jit(solution)/shard_map/stencil/pallas_call | solution.py:36
  28.3 4.8 %stencil.3 = (f32[2,288,8,128]{3,2,1,0:T(8,128)S(1)}, f32[2,288,8,128]{3,2,1,0:T(8,128)S(1)}, f32[1,1024]{1,0:T(1,128)S(1)}, f32[1,1024]{1,0:T(1,128)S(1)}, f32[1,1024]{1,0:T(1,128)S(1)}) custom-call(s32[1]{0:T(128)} %bitcast.refs_0_, f32[12,288]{1,0:T(8,128)S(1)} %copy-done.6, f32[2,2,288,8,128]{4,3,2,1,0:T(8,128)S(1)} %bitcast.47, ...), custom_call_target="tpu_custom_call" | custom-call | flops 23592960 | bytes 4718592 | tf_op jit(solution)/shard_map/stencil/pallas_call | solution.py:36
  33.1 1.9 %collective-permute-done.1 = f16[256,1024]{1,0:T(8,128)(2,1)S(1)} collective-permute-done((f16[256,1024]{1,0:T(8,128)(2,1)S(1)}, f16[256,1024]{1,0:T(8,128)(2,1)S(1)}, u32[]{:S(2)}, u32[]{:S(2)}) %collective-permute-start.1) | collective-permute-done | bytes 524320 | tf_op jit(solution)/shard_map/ppermute | solution.py:27
  35.5 2.8 %decode.4 = (f32[2,288,8,128]{3,2,1,0:T(8,128)S(1)}, f32[288,256]{1,0:T(8,128)S(1)}, f32[256,1024]{1,0:T(8,128)S(1)}, f32[1,1024]{1,0:T(1,128)}) custom-call(s32[1]{0:T(128)} %bitcast.refs_0_, s32[16]{0:T(128)S(1)} %copy-done.8, bf16[256,1024]{1,0:T(8,128)(2,1)S(1)} %get-tuple-element.82.refs_2_, ...), custom_call_target="tpu_custom_call", output_to_operand_aliasing={{0}: (4, {})} | custom-call | flops 452984832 | bytes 3538944 | tf_op jit(solution)/shard_map/decode/pallas_call | solution.py:36
  40.2 2.2 %decode.5 = (f32[2,288,8,128]{3,2,1,0:T(8,128)S(1)}, f32[288,256]{1,0:T(8,128)S(1)}, f32[256,1024]{1,0:T(8,128)S(1)}, f32[1,1024]{1,0:T(1,128)S(1)}) custom-call(s32[1]{0:T(128)} %bitcast.refs_0_, s32[16]{0:T(128)S(1)} %copy-done.8, bf16[256,1024]{1,0:T(8,128)(2,1)S(1)} %collective-permute-done.5.refs_2_, ...), custom_call_target="tpu_custom_call", output_to_operand_aliasing={{0}: (4, {})} | custom-call | flops 452984832 | bytes 3538944 | tf_op jit(solution)/shard_map/decode/pallas_call | solution.py:36
  42.4 10.5 %collective-permute-done.7 = f16[256,1024]{1,0:T(8,128)(2,1)S(1)} collective-permute-done((f16[256,1024]{1,0:T(8,128)(2,1)S(1)}, f16[256,1024]{1,0:T(8,128)(2,1)S(1)}, u32[]{:S(2)}, u32[]{:S(2)}) %collective-permute-start.7) | collective-permute-done | bytes 524320 | tf_op jit(solution)/shard_map/ppermute | solution.py:27
  53.6 2.6 %decode.6 = (f32[2,288,8,128]{3,2,1,0:T(8,128)S(1)}, f32[288,256]{1,0:T(8,128)S(1)}, f32[256,1024]{1,0:T(8,128)S(1)}, f32[1,1024]{1,0:T(1,128)}) custom-call(s32[1]{0:T(128)} %bitcast.refs_0_, s32[16]{0:T(128)S(1)} %copy-done.8, bf16[256,1024]{1,0:T(8,128)(2,1)S(1)} %get-tuple-element.84.refs_2_, ...), custom_call_target="tpu_custom_call", output_to_operand_aliasing={{0}: (4, {})} | custom-call | flops 452984832 | bytes 3538944 | tf_op jit(solution)/shard_map/decode/pallas_call | solution.py:36
  59.7 2.7 %decode.7 = (f32[2,288,8,128]{3,2,1,0:T(8,128)S(1)}, f32[288,256]{1,0:T(8,128)S(1)}, f32[256,1024]{1,0:T(8,128)S(1)}, f32[1,1024]{1,0:T(1,128)}) custom-call(s32[1]{0:T(128)} %bitcast.refs_0_, s32[16]{0:T(128)S(1)} %copy-done.8, bf16[256,1024]{1,0:T(8,128)(2,1)S(1)} %collective-permute-done.8.refs_2_, ...), custom_call_target="tpu_custom_call", output_to_operand_aliasing={{0}: (4, {})} | custom-call | flops 452984832 | bytes 3538944 | tf_op jit(solution)/shard_map/decode/pallas_call | solution.py:36
  62.4 8.3 %collective-permute-done.14 = f16[256,1024]{1,0:T(8,128)(2,1)S(1)} collective-permute-done((f16[256,1024]{1,0:T(8,128)(2,1)S(1)}, f16[256,1024]{1,0:T(8,128)(2,1)S(1)}, u32[]{:S(2)}, u32[]{:S(2)}) %collective-permute-start.14) | collective-permute-done | bytes 524320 | tf_op jit(solution)/shard_map/ppermute | solution.py:27
  74.6 2.2 %store.1 = f32[288,16,256]{2,1,0:T(8,128)} custom-call(f32[2,288,8,128]{3,2,1,0:T(8,128)S(1)} %get-tuple-element.45.refs_0_, f32[2,288,8,128]{3,2,1,0:T(8,128)S(1)} %get-tuple-element.56.refs_1_, f32[8,128]{1,0:T(8,128)S(1)} %slice_convert_fusion.refs_2_.refs_1_), custom_call_target="tpu_custom_call" | custom-call | bytes 9437184 | tf_op jit(solution)/shard_map/store/pallas_call | solution.py:36
  77.2 2.0 %collective-permute-done.17 = f16[304,256]{1,0:T(8,128)(2,1)S(1)} collective-permute-done((f16[304,256]{1,0:T(8,128)(2,1)S(1)}, f16[304,256]{1,0:T(8,128)(2,1)S(1)}, u32[]{:S(2)}, u32[]{:S(2)}) %collective-permute-start.17) | collective-permute-done | bytes 155680 | tf_op jit(solution)/shard_map/ppermute | solution.py:27
  79.5 1.9 %collective-permute-start.18 = (f16[304,256]{1,0:T(8,128)(2,1)S(1)}, f16[304,256]{1,0:T(8,128)(2,1)S(1)}, u32[]{:S(2)}, u32[]{:S(2)}) collective-permute-start(f16[304,256]{1,0:T(8,128)(2,1)S(1)} %get-tuple-element.76), channel_id=1, source_target_pairs={{0,8},{4,12},{8,0},{12,4},{16,24},{20,28},{24,16},{28,20},{1,9},{5... | collective-permute-start | bytes 466952 | tf_op jit(solution)/shard_map/ppermute | solution.py:27
  81.4 3.6 %collective-permute-done.18 = f16[304,256]{1,0:T(8,128)(2,1)S(1)} collective-permute-done((f16[304,256]{1,0:T(8,128)(2,1)S(1)}, f16[304,256]{1,0:T(8,128)(2,1)S(1)}, u32[]{:S(2)}, u32[]{:S(2)}) %collective-permute-start.18) | collective-permute-done | bytes 155680 | tf_op jit(solution)/shard_map/ppermute | solution.py:27
  85.3 2.8 %collective-permute-start.19 = (f16[304,256]{1,0:T(8,128)(2,1)S(1)}, f16[304,256]{1,0:T(8,128)(2,1)S(1)}, u32[]{:S(2)}, u32[]{:S(2)}) collective-permute-start(f16[304,256]{1,0:T(8,128)(2,1)S(1)} %get-tuple-element.74), channel_id=1, source_target_pairs={{0,16},{4,20},{8,24},{12,28},{16,0},{20,4},{24,8},{28,12},{1,17},{... | collective-permute-start | bytes 466952 | tf_op jit(solution)/shard_map/ppermute | solution.py:27
  88.5 5.6 %collective-permute-done.19 = f16[304,256]{1,0:T(8,128)(2,1)S(1)} collective-permute-done((f16[304,256]{1,0:T(8,128)(2,1)S(1)}, f16[304,256]{1,0:T(8,128)(2,1)S(1)}, u32[]{:S(2)}, u32[]{:S(2)}) %collective-permute-start.19) | collective-permute-done | bytes 155680 | tf_op jit(solution)/shard_map/ppermute | solution.py:27
  96.6 3.9 %collective-permute-done.20 = f16[304,256]{1,0:T(8,128)(2,1)S(1)} collective-permute-done((f16[304,256]{1,0:T(8,128)(2,1)S(1)}, f16[304,256]{1,0:T(8,128)(2,1)S(1)}, u32[]{:S(2)}, u32[]{:S(2)}) %collective-permute-start.20) | collective-permute-done | bytes 155680 | tf_op jit(solution)/shard_map/ppermute | solution.py:27
  101.6 4.5 %collective-permute-done.21 = f16[304,256]{1,0:T(8,128)(2,1)S(1)} collective-permute-done((f16[304,256]{1,0:T(8,128)(2,1)S(1)}, f16[304,256]{1,0:T(8,128)(2,1)S(1)}, u32[]{:S(2)}, u32[]{:S(2)}) %collective-permute-start.21) | collective-permute-done | bytes 155680 | tf_op jit(solution)/shard_map/ppermute | solution.py:27
  106.4 2.1 %collective-permute-start.22 = (f16[304,256]{1,0:T(8,128)(2,1)S(1)}, f16[304,256]{1,0:T(8,128)(2,1)S(1)}, u32[]{:S(2)}, u32[]{:S(2)}) collective-permute-start(f16[304,256]{1,0:T(8,128)(2,1)S(1)} %get-tuple-element.68), channel_id=1, source_target_pairs={{0,16},{4,20},{8,24},{12,28},{16,0},{20,4},{24,8},{28,12},{1,17},{... | collective-permute-start | bytes 466952 | tf_op jit(solution)/shard_map/ppermute | solution.py:27
  108.6 5.7 %collective-permute-done.22 = f16[304,256]{1,0:T(8,128)(2,1)S(1)} collective-permute-done((f16[304,256]{1,0:T(8,128)(2,1)S(1)}, f16[304,256]{1,0:T(8,128)(2,1)S(1)}, u32[]{:S(2)}, u32[]{:S(2)}) %collective-permute-start.22) | collective-permute-done | bytes 155680 | tf_op jit(solution)/shard_map/ppermute | solution.py:27
  (121 shorter events, 22.5 us)
Async XLA Ops:
  6.8 13.0 %collective-permute-start = (f32[256,1024]{1,0:T(8,128)}, f32[256,1024]{1,0:T(8,128)S(1)}, u32[]{:S(2)}, u32[]{:S(2)}) collective-permute-start(f32[256,1024]{1,0:T(8,128)} %get-tuple-element.37), channel_id=1, source_target_pairs={{0,1},{1,0},{2,3},{3,2},{4,5},{5,4},{6,7},{7,6},{8,9},{9,8},{10,11... | collective-permute-start | bytes 3145736 | tf_op jit(solution)/shard_map/ppermute | solution.py:27
  9.2 10.5 %collective-permute-start.4 = (f16[288,256]{1,0:T(8,128)(2,1)S(1)}, f16[288,256]{1,0:T(8,128)(2,1)S(1)}, u32[]{:S(2)}, u32[]{:S(2)}) collective-permute-start(f16[288,256]{1,0:T(8,128)(2,1)S(1)} %fusion.6), channel_id=1, source_target_pairs={{0,4},{1,5},{4,8},{5,9},{6,2},{7,3},{8,12},{9,13},{10,6},{11,7},{1... | collective-permute-start | bytes 442376 | tf_op jit(solution)/shard_map/ppermute | solution.py:434
  15.0 8.4 %collective-permute-start.3 = (f16[32,16,256]{2,1,0:T(8,128)(2,1)S(1)}, f16[32,16,256]{2,1,0:T(8,128)(2,1)S(1)}, u32[]{:S(2)}, u32[]{:S(2)}) collective-permute-start(f16[32,16,256]{2,1,0:T(8,128)(2,1)S(1)} %get-tuple-element.79), channel_id=1, source_target_pairs={{0,3},{1,2},{2,1},{3,0},{4,7},{5,6},{6,5},{7,4},{8,11},{9,10},{10,... | collective-permute-start | bytes 786440 | tf_op jit(solution)/shard_map/ppermute | solution.py:27
  15.1 8.3 %collective-permute-start.2 = (f16[32,16,256]{2,1,0:T(8,128)(2,1)S(1)}, f16[32,16,256]{2,1,0:T(8,128)(2,1)S(1)}, u32[]{:S(2)}, u32[]{:S(2)}) collective-permute-start(f16[32,16,256]{2,1,0:T(8,128)(2,1)S(1)} %get-tuple-element.80), channel_id=1, source_target_pairs={{0,1},{1,0},{2,3},{3,2},{4,5},{5,4},{6,7},{7,6},{8,9},{9,8},{10,11... | collective-permute-start | bytes 786440 | tf_op jit(solution)/shard_map/ppermute | solution.py:27
  18.3 20.5 %collective-permute-start.6 = (f32[256,1024]{1,0:T(8,128)S(1)}, f32[256,1024]{1,0:T(8,128)S(1)}, u32[]{:S(2)}, u32[]{:S(2)}) collective-permute-start(f32[256,1024]{1,0:T(8,128)S(1)} %get-tuple-element.46), channel_id=1, source_target_pairs={{0,1},{1,0},{2,3},{3,2},{4,5},{5,4},{6,7},{7,6},{8,9},{9,8},{10,11... | collective-permute-start | bytes 3145736 | tf_op jit(solution)/shard_map/ppermute | solution.py:27
  20.0 14.9 %collective-permute-start.1 = (f16[256,1024]{1,0:T(8,128)(2,1)S(1)}, f16[256,1024]{1,0:T(8,128)(2,1)S(1)}, u32[]{:S(2)}, u32[]{:S(2)}) collective-permute-start(f16[256,1024]{1,0:T(8,128)(2,1)S(1)} %multiply_convert_fusion.7), channel_id=1, source_target_pairs={{0,2},{1,3},{2,0},{3,1},{4,6},{5,7},{6,4},{7,5},{8,10},{9,11},{10,... | collective-permute-start | bytes 1572872 | tf_op jit(solution)/shard_map/ppermute | solution.py:27
  35.4 4.8 %collective-permute-start.5 = (bf16[256,1024]{1,0:T(8,128)(2,1)S(1)}, bf16[256,1024]{1,0:T(8,128)(2,1)S(1)}, u32[]{:S(2)}, u32[]{:S(2)}) collective-permute-start(bf16[256,1024]{1,0:T(8,128)(2,1)S(1)} %get-tuple-element.82.refs_2_), channel_id=1, source_target_pairs={{0,1},{1,0},{2,3},{3,2},{4,5},{5,4},{6,7},{7,6},{8,9},{9,8},{10,11... | collective-permute-start | bytes 1572872 | tf_op jit(solution)/shard_map/ppermute | solution.py:27
  38.3 15.1 %collective-permute-start.9 = (f32[256,1024]{1,0:T(8,128)S(1)}, f32[256,1024]{1,0:T(8,128)S(1)}, u32[]{:S(2)}, u32[]{:S(2)}) collective-permute-start(f32[256,1024]{1,0:T(8,128)S(1)} %get-tuple-element.52), channel_id=1, source_target_pairs={{0,1},{1,0},{2,3},{3,2},{4,5},{5,4},{6,7},{7,6},{8,9},{9,8},{10,11... | collective-permute-start | bytes 3145736 | tf_op jit(solution)/shard_map/ppermute | solution.py:27
  39.0 13.9 %collective-permute-start.7 = (f16[256,1024]{1,0:T(8,128)(2,1)S(1)}, f16[256,1024]{1,0:T(8,128)(2,1)S(1)}, u32[]{:S(2)}, u32[]{:S(2)}) collective-permute-start(f16[256,1024]{1,0:T(8,128)(2,1)S(1)} %multiply_convert_fusion.5), channel_id=1, source_target_pairs={{0,2},{1,3},{2,0},{3,1},{4,6},{5,7},{6,4},{7,5},{8,10},{9,11},{10,... | collective-permute-start | bytes 1572872 | tf_op jit(solution)/shard_map/ppermute | solution.py:27
  40.2 22.2 %collective-permute-start.15 = (f32[256,1024]{1,0:T(8,128)S(1)}, f32[256,1024]{1,0:T(8,128)S(1)}, u32[]{:S(2)}, u32[]{:S(2)}) collective-permute-start(f32[256,1024]{1,0:T(8,128)S(1)} %get-tuple-element.81), channel_id=1, source_target_pairs={{0,1},{1,0},{2,3},{3,2},{4,5},{5,4},{6,7},{7,6},{8,9},{9,8},{10,11... | collective-permute-start | bytes 3145736 | tf_op jit(solution)/shard_map/ppermute | solution.py:27
  56.3 15.1 %collective-permute-start.10 = (f32[256,1024]{1,0:T(8,128)S(1)}, f32[256,1024]{1,0:T(8,128)S(1)}, u32[]{:S(2)}, u32[]{:S(2)}) collective-permute-start(f32[256,1024]{1,0:T(8,128)S(1)} %get-tuple-element.58), channel_id=1, source_target_pairs={{0,1},{1,0},{2,3},{3,2},{4,5},{5,4},{6,7},{7,6},{8,9},{9,8},{10,11... | collective-permute-start | bytes 3145736 | tf_op jit(solution)/shard_map/ppermute | solution.py:27
  56.3 3.4 %collective-permute-start.8 = (bf16[256,1024]{1,0:T(8,128)(2,1)S(1)}, bf16[256,1024]{1,0:T(8,128)(2,1)S(1)}, u32[]{:S(2)}, u32[]{:S(2)}) collective-permute-start(bf16[256,1024]{1,0:T(8,128)(2,1)S(1)} %get-tuple-element.84.refs_2_), channel_id=1, source_target_pairs={{0,1},{1,0},{2,3},{3,2},{4,5},{5,4},{6,7},{7,6},{8,9},{9,8},{10,11... | collective-permute-start | bytes 1572872 | tf_op jit(solution)/shard_map/ppermute | solution.py:27
  56.8 13.8 %collective-permute-start.14 = (f16[256,1024]{1,0:T(8,128)(2,1)S(1)}, f16[256,1024]{1,0:T(8,128)(2,1)S(1)}, u32[]{:S(2)}, u32[]{:S(2)}) collective-permute-start(f16[256,1024]{1,0:T(8,128)(2,1)S(1)} %multiply_convert_fusion.3), channel_id=1, source_target_pairs={{0,2},{1,3},{2,0},{3,1},{4,6},{5,7},{6,4},{7,5},{8,10},{9,11},{10,... | collective-permute-start | bytes 1572872 | tf_op jit(solution)/shard_map/ppermute | solution.py:27
  57.9 30.2 %collective-permute-start.12 = (f32[256,1024]{1,0:T(8,128)S(1)}, f32[256,1024]{1,0:T(8,128)S(1)}, u32[]{:S(2)}, u32[]{:S(2)}) collective-permute-start(f32[256,1024]{1,0:T(8,128)S(1)} %get-tuple-element.83), channel_id=1, source_target_pairs={{0,1},{1,0},{2,3},{3,2},{4,5},{5,4},{6,7},{7,6},{8,9},{9,8},{10,11... | collective-permute-start | bytes 3145736 | tf_op jit(solution)/shard_map/ppermute | solution.py:27
  62.4 8.6 %copy-start.5 = (bf16[288,1024]{1,0:T(8,128)(2,1)S(1)}, bf16[288,1024]{1,0:T(8,128)(2,1)}, u32[]{:S(2)}) copy-start(bf16[288,1024]{1,0:T(8,128)(2,1)} %get-tuple-element.65.refs_0_) | copy-start | bytes 1769476
  70.9 5.9 %collective-permute-start.16 = (bf16[256,1024]{1,0:T(8,128)(2,1)S(1)}, bf16[256,1024]{1,0:T(8,128)(2,1)S(1)}, u32[]{:S(2)}, u32[]{:S(2)}) collective-permute-start(bf16[256,1024]{1,0:T(8,128)(2,1)S(1)} %multiply_convert_fusion.refs_1_), channel_id=1, source_target_pairs={{0,1},{1,0},{2,3},{3,2},{4,5},{5,4},{6,7},{7,6},{8,9},{9,8},{10,11... | collective-permute-start | bytes 1572872 | tf_op jit(solution)/shard_map/ppermute | solution.py:27
  71.6 16.5 %collective-permute-start.11 = (f16[256,1024]{1,0:T(8,128)(2,1)S(1)}, f16[256,1024]{1,0:T(8,128)(2,1)S(1)}, u32[]{:S(2)}, u32[]{:S(2)}) collective-permute-start(f16[256,1024]{1,0:T(8,128)(2,1)S(1)} %multiply_convert_fusion.2), channel_id=1, source_target_pairs={{0,2},{1,3},{2,0},{3,1},{4,6},{5,7},{6,4},{7,5},{8,10},{9,11},{10,... | collective-permute-start | bytes 1572872 | tf_op jit(solution)/shard_map/ppermute | solution.py:27
  73.0 6.2 %collective-permute-start.17 = (f16[304,256]{1,0:T(8,128)(2,1)S(1)}, f16[304,256]{1,0:T(8,128)(2,1)S(1)}, u32[]{:S(2)}, u32[]{:S(2)}) collective-permute-start(f16[304,256]{1,0:T(8,128)(2,1)S(1)} %get-tuple-element.78), channel_id=1, source_target_pairs={{0,4},{4,0},{8,12},{12,8},{16,20},{20,16},{24,28},{28,24},{1,5},{5... | collective-permute-start | bytes 466952 | tf_op jit(solution)/shard_map/ppermute | solution.py:27
  79.5 5.5 %collective-permute-start.18 = (f16[304,256]{1,0:T(8,128)(2,1)S(1)}, f16[304,256]{1,0:T(8,128)(2,1)S(1)}, u32[]{:S(2)}, u32[]{:S(2)}) collective-permute-start(f16[304,256]{1,0:T(8,128)(2,1)S(1)} %get-tuple-element.76), channel_id=1, source_target_pairs={{0,8},{4,12},{8,0},{12,4},{16,24},{20,28},{24,16},{28,20},{1,9},{5... | collective-permute-start | bytes 466952 | tf_op jit(solution)/shard_map/ppermute | solution.py:27
  85.3 8.8 %collective-permute-start.19 = (f16[304,256]{1,0:T(8,128)(2,1)S(1)}, f16[304,256]{1,0:T(8,128)(2,1)S(1)}, u32[]{:S(2)}, u32[]{:S(2)}) collective-permute-start(f16[304,256]{1,0:T(8,128)(2,1)S(1)} %get-tuple-element.74), channel_id=1, source_target_pairs={{0,16},{4,20},{8,24},{12,28},{16,0},{20,4},{24,8},{28,12},{1,17},{... | collective-permute-start | bytes 466952 | tf_op jit(solution)/shard_map/ppermute | solution.py:27
  88.4 6.2 %collective-permute-start.13 = (bf16[256,1024]{1,0:T(8,128)(2,1)S(1)}, bf16[256,1024]{1,0:T(8,128)(2,1)S(1)}, u32[]{:S(2)}, u32[]{:S(2)}) collective-permute-start(bf16[256,1024]{1,0:T(8,128)(2,1)S(1)} %multiply_convert_fusion.1.refs_1_), channel_id=1, source_target_pairs={{0,1},{1,0},{2,3},{3,2},{4,5},{5,4},{6,7},{7,6},{8,9},{9,8},{10,11... | collective-permute-start | bytes 1572872 | tf_op jit(solution)/shard_map/ppermute | solution.py:27
  95.2 5.3 %collective-permute-start.20 = (f16[304,256]{1,0:T(8,128)(2,1)S(1)}, f16[304,256]{1,0:T(8,128)(2,1)S(1)}, u32[]{:S(2)}, u32[]{:S(2)}) collective-permute-start(f16[304,256]{1,0:T(8,128)(2,1)S(1)} %get-tuple-element.72), channel_id=1, source_target_pairs={{0,4},{4,0},{8,12},{12,8},{16,20},{20,16},{24,28},{28,24},{1,5},{5... | collective-permute-start | bytes 466952 | tf_op jit(solution)/shard_map/ppermute | solution.py:27
  100.8 5.3 %collective-permute-start.21 = (f16[304,256]{1,0:T(8,128)(2,1)S(1)}, f16[304,256]{1,0:T(8,128)(2,1)S(1)}, u32[]{:S(2)}, u32[]{:S(2)}) collective-permute-start(f16[304,256]{1,0:T(8,128)(2,1)S(1)} %get-tuple-element.70), channel_id=1, source_target_pairs={{0,8},{4,12},{8,0},{12,4},{16,24},{20,28},{24,16},{28,20},{1,9},{5... | collective-permute-start | bytes 466952 | tf_op jit(solution)/shard_map/ppermute | solution.py:27
  106.4 7.9 %collective-permute-start.22 = (f16[304,256]{1,0:T(8,128)(2,1)S(1)}, f16[304,256]{1,0:T(8,128)(2,1)S(1)}, u32[]{:S(2)}, u32[]{:S(2)}) collective-permute-start(f16[304,256]{1,0:T(8,128)(2,1)S(1)} %get-tuple-element.68), channel_id=1, source_target_pairs={{0,16},{4,20},{8,24},{12,28},{16,0},{20,4},{24,8},{28,12},{1,17},{... | collective-permute-start | bytes 466952 | tf_op jit(solution)/shard_map/ppermute | solution.py:27
  (12 other events, 56.6 us)

commit v3 on v2

v3 whole, which is shorter than its diff:
```python
import math

import jax
import jax.numpy as jnp
import numpy as np
from jax import lax
from jax.experimental import pallas as pl
from jax.experimental.pallas import tpu as pltpu
from jax.sharding import PartitionSpec as P

NDIR = 36
ROWS = 8
LANES = 128
PRE_SCALE = 64.0
BACK_SCALE = 2.0**-8
LIMIT1 = 16
POWER_ROWS = 16

BF16, F16, F32 = jnp.bfloat16, jnp.float16, jnp.float32
VMEM = pl.BlockSpec(memory_space=pltpu.VMEM)
SMEM = pl.BlockSpec(memory_space=pltpu.SMEM)
HBM = pl.BlockSpec(memory_space=pltpu.HBM)
ANY = pl.BlockSpec(memory_space=pl.ANY)
FREE = pl.BlockSpec(memory_space=pltpu.VMEM)


def swap(value, axis, bit):
    count = lax.axis_size(axis)
    return lax.ppermute(value, axis, [(i, i ^ bit) for i in range(count)])


def call(body, ins, outs, cost, after=(), aliases=None, scratch=(), limit=16, name=None):
    n = len(ins)

    def run(*refs):
        body(*refs[:n], *refs[n + len(after) :])

    def placed(dims, dtype, spec=VMEM):
        if spec is FREE:
            return jax.ShapeDtypeStruct(dims, dtype)
        return (pltpu.HBM if spec is HBM else pltpu.VMEM)(dims, dtype)

    values = [pltpu.with_memory_space_constraint(v, pltpu.HBM) if spec is HBM else v for v, spec in ins]
    return pl.pallas_call(
        run,
        in_specs=[spec for _, spec in ins] + [ANY] * len(after),
        out_specs=[VMEM if len(out) == 2 else out[2] for out in outs],
        out_shape=[placed(*out) for out in outs],
        scratch_shapes=list(scratch),
        input_output_aliases=aliases or {},
        compiler_params=pltpu.CompilerParams(vmem_limit_bytes=limit << 20),
        name=name,
    )(*values, *after)


def first_row(core, own):
    half = ROWS // 2
    return core * half if own else (1 - core) * half


def pick(ref, core, own, chunk, i, j):
    at = chunk * ROWS + i
    lanes = slice(j * LANES, (j + 1) * LANES)
    low, high = ref[at : at + 1, lanes], ref[at + ROWS // 2 : at + ROWS // 2 + 1, lanes]
    return jnp.where((core == 0) == own, low, high).astype(F32)


def count_of(count_ref, core, own, chunk, i):
    value = count_ref[chunk * ROWS + first_row(core, own) + i]
    return jnp.full((1, LANES), value, jnp.int32).astype(F32)


def write_columns(refs, start, value):
    offset = 0
    for ref in refs:
        for k in range(value.shape[1] // LANES):
            at = start + k * LANES - offset
            if 0 <= at < ref.shape[1]:
                ref[:, at : at + LANES] = value[:, k * LANES : (k + 1) * LANES]
        offset += ref.shape[1]


def read_columns(refs, start, width):
    found, offset = [], 0
    for ref in refs:
        low, high = max(start - offset, 0), min(start + width - offset, ref.shape[1])
        if low < high:
            found.append(ref[:, low:high])
        offset += ref.shape[1]
    return found[0] if len(found) == 1 else jnp.concatenate(found, axis=1)


def pieces_of(dims, dtype, cut):
    widths = cut if isinstance(cut, tuple) else (dims[1] // cut,) * cut
    return [((dims[0], width), dtype) for width in widths]


def encode_rows(place_ref, tiles_ref, mask_ref, w_ref, spec_ref, out_refs, chunk, own):
    parts, bins = tiles_ref.shape[1:3]
    half = ROWS // 2
    wide = half * LANES
    core = place_ref[0] % 2
    first = first_row(core, own)
    for j in range(parts):
        flat = tiles_ref.at[chunk, j].reshape(bins * ROWS, LANES)
        cols = []
        for i in range(half):
            row = flat[pl.ds(first + i, bins, stride=ROWS), :]
            cols.append((row * pick(mask_ref, core, own, chunk, i, j)).astype(BF16))
        field = jnp.concatenate(cols, axis=1)
        spec_ref[:, j * wide : (j + 1) * wide] = field
        out = lax.dot_general(w_ref[...], field, (((0,), (0,)), ((), ())), preferred_element_type=F32)
        write_columns(out_refs, j * wide, out)


def encode_first(place, state, mask, w_in, cut, after=()):
    bins, rows, lon = state.shape
    hidden = w_in.shape[1]
    chunks, parts = rows // ROWS, lon // LANES
    cells = parts * ROWS * LANES // 2

    def body(place_ref, state_ref, mask_hbm, w_hbm, tiles_ref, spec_ref, *refs):
        out_refs, (mask_ref, w_ref, sems) = refs[:cut], refs[cut:]
        small = [
            pltpu.make_async_copy(a, b, sems.at[chunks * parts + k])
            for k, (a, b) in enumerate([(mask_hbm, mask_ref), (w_hbm, w_ref)])
        ]
        copies = [
            [
                pltpu.make_async_copy(
                    state_ref.at[:, pl.ds(c * ROWS, ROWS), pl.ds(j * LANES, LANES)],
                    tiles_ref.at[c, j],
                    sems.at[c * parts + j],
                )
                for j in range(parts)
            ]
            for c in range(chunks)
        ]
        for row in copies:
            for copy in row:
                copy.start()
        for copy in small:
            copy.start()
        for copy in copies[0] + small:
            copy.wait()
        encode_rows(place_ref, tiles_ref, mask_ref, w_ref, spec_ref, out_refs, 0, False)
        for row in copies[1:]:
            for copy in row:
                copy.wait()

    return call(
        body,
        [(place, SMEM), (state, HBM), (mask, HBM), (w_in, HBM)],
        [((chunks, parts, bins, ROWS, LANES), F32), ((bins, cells), BF16), *pieces_of((hidden, cells), F32, cut)]
        + [(mask.shape, mask.dtype), (w_in.shape, w_in.dtype)],
        (2 * bins * hidden * cells, 4 * bins * rows * lon),
        scratch=[pltpu.SemaphoreType.DMA((chunks * parts + 2,))],
        after=after,
        limit=LIMIT1,
        name="encode_first",
    )


def encode(place, tiles, mask, w_in, chunk, own, cut=1, after=()):
    parts, bins = tiles.shape[1:3]
    hidden = w_in.shape[1]
    cells = parts * ROWS * LANES // 2

    def body(place_ref, tiles_ref, mask_ref, w_ref, spec_ref, *out_refs):
        encode_rows(place_ref, tiles_ref, mask_ref, w_ref, spec_ref, out_refs, chunk, own)

    return call(
        body,
        [(place, SMEM), (tiles, VMEM), (mask, VMEM), (w_in, VMEM)],
        [((bins, cells), BF16)] + pieces_of((hidden, cells), F32, cut),
        (2 * bins * hidden * cells, 4 * bins * cells),
        after=after,
        name="encode",
    )


def edge_bin(place, tiles, ndir, own, after=()):
    chunks, parts, bins = tiles.shape[:3]
    nfreq = bins // ndir

    def body(place_ref, tiles_ref, out_ref):
        upper = place_ref[0] % 2
        start = pl.multiple_of((1 - upper if own else upper) * (bins - nfreq), 8)
        for c in range(chunks):
            for j in range(parts):
                out_ref[c, j] = tiles_ref[c, j, pl.ds(start, nfreq)]

    ins = [(place, SMEM), (tiles, VMEM)]
    return call(body, ins, [((chunks, parts, nfreq, ROWS, LANES), F32)], (0, 0), after=after, name="edge_bin")[0]


def edge_row(place, tiles, mask, after=()):
    chunks, parts, bins = tiles.shape[:3]

    def body(place_ref, tiles_ref, mask_ref, edge_ref):
        for north in (False, True):
            c, i = (0, 0) if north else (chunks - 1, ROWS - 1)

            @pl.when((place_ref[0] >= 2) == north)
            def _():
                for j in range(parts):
                    mask = mask_ref[c * ROWS + i : c * ROWS + i + 1, j * LANES : (j + 1) * LANES].astype(F32)
                    flat = tiles_ref.at[c, j].reshape(bins * ROWS, LANES)
                    edge_ref[j] = flat[pl.ds(i, bins, stride=ROWS), :] * mask

    ins = [(place, SMEM), (tiles, VMEM), (mask, VMEM)]
    return call(body, ins, [((parts, bins, LANES), F32)], (0, 0), after=after, name="edge_row")[0]


def join(own, received, scale, cut, after=()):
    n, m = len(own), len(received)
    rows, width = own[0].shape[0], n * own[0].shape[1]

    def body(scale_ref, *refs):
        for k in range(width // LANES):
            at = slice(k * LANES, (k + 1) * LANES)
            total = read_columns(refs[:n], k * LANES, LANES) + read_columns(refs[n : n + m], k * LANES, LANES)
            write_columns(refs[n + m :], k * LANES, total * scale_ref[:, at])

    values = [(v, VMEM) for v in (scale, *own, *received)]
    return call(body, values, pieces_of((rows, width), F32, cut), (0, 0), after=after, name="join")


def cross(pieces):
    return [swap(v.astype(F16), "dir", 2).astype(F32) for v in pieces]


def activate(own, received, cut, after=()):
    n = len(own)
    rows, width = own[0].shape[0], n * own[0].shape[1]

    def body(*refs):
        own_refs, received_refs, slope_ref, hid_refs = refs[:n], refs[n : 2 * n], refs[2 * n], refs[2 * n + 1 :]
        for k in range(width // LANES):
            at = slice(k * LANES, (k + 1) * LANES)
            pre = read_columns(own_refs, k * LANES, LANES) + read_columns(received_refs, k * LANES, LANES)
            pre = pre * (1.0 / PRE_SCALE)
            sig = 1.0 / (1.0 + jnp.exp(-pre))
            slope_ref[:, at] = sig * (1.0 + pre * (1.0 - sig))
            write_columns(hid_refs, k * LANES, (pre * sig).astype(BF16))

    outs = [((rows, width), F32), *pieces_of((rows, width), BF16, cut)]
    slope, *hid = call(body, [(v, VMEM) for v in (*own, *received)], outs, (0, 0), after=after, name="activate")
    return hid, slope


def slope_back(own, received, up, slope, cut, after=()):
    n = len(own)

    def body(up_ref, slope_ref, *refs):
        for k in range(slope.shape[1] // LANES):
            at = slice(k * LANES, (k + 1) * LANES)
            total = read_columns(refs[:n], k * LANES, LANES) + read_columns(refs[n : 2 * n], k * LANES, LANES)
            write_columns(refs[2 * n :], k * LANES, (total * up_ref[:, at] * slope_ref[:, at]).astype(BF16))

    values = [(v, VMEM) for v in (up, slope, *own, *received)]
    return call(body, values, pieces_of(slope.shape, BF16, cut), (0, 0), after=after, name="slope_back")


def stencil(place, coef, tiles, near, mask, sign, count, target, extra, chunk, ndir, after=()):
    chunks, parts, bins = tiles.shape[:3]
    nfreq = bins // ndir
    half = ROWS // 2
    wide = half * LANES

    def body(
        place_ref, coef_ref, tiles_ref, near_ref, mask_ref, sign_ref, count_ref, target_ref, extra_ref,
        base_ref, goal_ref, down_ref, up_ref, kept_ref, sems,
    ):
        copies = []
        for j in range(parts):
            copy = pltpu.make_async_copy(
                target_ref.at[:, pl.ds(chunk * ROWS, ROWS), pl.ds(j * LANES, LANES)], goal_ref.at[j], sems.at[j]
            )
            copy.start()
            copies.append(copy)
        copies.append(pltpu.make_async_copy(extra_ref, kept_ref, sems.at[parts]))
        copies[-1].start()
        place = place_ref[0]
        for i in range(half):
            counts = count_of(count_ref, place % 2, True, chunk, i)
            for j in range(parts):
                at = slice(j * wide + i * LANES, j * wide + (i + 1) * LANES)
                down_ref[:, at] = counts * BACK_SCALE
                up_ref[:, at] = (1.0 / BACK_SCALE) / counts
        lane = lax.broadcasted_iota(jnp.int32, (ROWS, LANES), 1)
        row = lax.broadcasted_iota(jnp.int32, (ROWS, LANES), 0)

        def plane(ref, c, j):
            return ref[c * ROWS : (c + 1) * ROWS, j * LANES : (j + 1) * LANES]

        masks = [[plane(mask_ref, c, j).astype(F32) for j in range(parts)] for c in range(chunks)]
        ahead = [plane(sign_ref, chunk, j) > 0 for j in range(parts)]

        def quadrant(q):
            east = q in (1, 2)
            north = q in (2, 3)
            beside = chunk + 1 if north else chunk - 1

            def sector(d, below, above):
                def group(g, _):
                    start = pl.multiple_of(d * nfreq + g * 8, 8)
                    for u in range(8):
                        b, f = start + u, g * 8 + u
                        here = [tiles_ref[chunk, j, b] for j in range(parts)]
                        field = [here[j] * masks[chunk][j] for j in range(parts)]
                        for j in range(parts):
                            k = j + 1 if east else j - 1
                            outer = field[k] if 0 <= k < parts else 0.0
                            if east:
                                x = pltpu.roll(jnp.where(lane == 0, outer, field[j]), LANES - 1, 1)
                            else:
                                x = pltpu.roll(jnp.where(lane == LANES - 1, outer, field[j]), 1, 1)
                            outer = 0.0
                            if 0 <= beside < chunks:
                                outer = tiles_ref[beside, j, b] * masks[beside][j]
                            if north:
                                y = pltpu.roll(jnp.where(row == 0, outer, field[j]), ROWS - 1, 0)
                            else:
                                y = pltpu.roll(jnp.where(row == ROWS - 1, outer, field[j]), 1, 0)
                            upstream = jnp.where(ahead[j], below(b, f, j), above(b, f, j))
                            total = coef_ref[3 * q, b] * here[j] + coef_ref[3 * q + 1, b] * x
                            total = total + (coef_ref[3 * q + 2, b] * y + 0.3 * upstream)
                            base_ref[j, b] = total * masks[chunk][j]
                    return 0

                lax.fori_loop(0, nfreq // 8, group, 0)

            def far(b, f, j):
                return jnp.zeros((ROWS, LANES), F32)

            def near(b, f, j):
                return near_ref[chunk, j, f]

            def inside(shift):
                return lambda b, f, j: tiles_ref[chunk, j, b + shift]

            sector(0, near if q % 2 else far, inside(nfreq))

            def middle(d, _):
                sector(d, inside(-nfreq), inside(nfreq))
                return 0

            lax.fori_loop(1, ndir - 1, middle, 0)
            sector(ndir - 1, inside(-nfreq), far if q % 2 else near)

        for q in range(4):
            pl.when(place == q)(lambda q=q: quadrant(q))
        for copy in copies:
            copy.wait()

    cells = parts * ROWS * LANES
    return call(
        body,
        [(place, SMEM), (coef, SMEM)]
        + [(v, VMEM) for v in (tiles, near, mask, sign)]
        + [(count, SMEM), (target, HBM), (extra, HBM)],
        [
            ((parts, bins, ROWS, LANES), F32),
            ((parts, bins, ROWS, LANES), F32),
            ((1, cells // 2), F32),
            ((1, cells // 2), F32),
            (extra.shape, extra.dtype),
        ],
        (40 * bins * cells, 8 * bins * cells),
        scratch=[pltpu.SemaphoreType.DMA((parts + 1,))],
        after=after,
        limit=32,
        name="stencil",
    )


def turn_in(place, coef, base, far, edge, mask, sign, chunk, chunks, ndir, after=()):
    parts, bins = base.shape[:2]
    nfreq = bins // ndir

    def body(place_ref, coef_ref, base_ref, far_ref, edge_ref, mask_ref, sign_ref, out_ref):
        place = place_ref[0]
        upper = place % 2
        start = pl.multiple_of(upper * (bins - nfreq), 8)
        for j in range(parts):
            at = (slice(chunk * ROWS, (chunk + 1) * ROWS), slice(j * LANES, (j + 1) * LANES))
            ahead = jnp.where(sign_ref[at] > 0, 1, 0)
            share = jnp.where(ahead != upper, 0.3 * mask_ref[at].astype(F32), 0.0)
            bin_edge = pl.ds(start, nfreq)
            out_ref[j, bin_edge] = base_ref[j, bin_edge] + share[None] * far_ref[chunk, j]
        freq = lax.broadcasted_iota(jnp.int32, (nfreq, LANES), 0).astype(F32)
        speed = 1.0 / (1.0 + 2.3 * freq / nfreq)

        def blow(i):
            for j in range(parts):
                flat = out_ref.at[j].reshape(bins * ROWS, LANES)
                lanes = slice(j * LANES, (j + 1) * LANES)
                mask = mask_ref[chunk * ROWS + i : chunk * ROWS + i + 1, lanes].astype(F32)
                for d in range(ndir):
                    at = pl.ds(d * nfreq * ROWS + i, nfreq, stride=ROWS)
                    cy = coef_ref[3 * place + 2, d * nfreq] * speed
                    flat[at, :] = flat[at, :] + (mask * cy) * edge_ref[j, d * nfreq : (d + 1) * nfreq, :]

        if chunk == 0:
            pl.when(place < 2)(lambda: blow(0))
        if chunk == chunks - 1:
            pl.when(place >= 2)(lambda: blow(ROWS - 1))

    ins = [(place, SMEM), (coef, SMEM)] + [(v, VMEM) for v in (base, far, edge, mask, sign)]
    return call(body, ins, [(base.shape, F32)], (0, 0), after=after, aliases={2: 0}, name="turn_in")[0]


def decode(place, hid, w_out, base, goal, mask, count, seed, chunk, own, which, cut=1, after=()):
    bins = base.shape[1]
    hidden = w_out.shape[1]
    half = ROWS // 2
    wide = half * LANES
    cells = len(which) * wide
    seeds = [seed] if seed is not None else []

    def body(place_ref, count_ref, w_ref, base_ref, goal_ref, mask_ref, *refs):
        hid_refs, refs = refs[: len(hid)], refs[len(hid) :]
        next_ref, grad_ref, *out_refs, back_ref = refs[len(seeds) :]
        core = place_ref[0] % 2
        first = first_row(core, own)
        total = refs[0][...] if seeds else jnp.zeros(grad_ref.shape, F32)
        for k, j in enumerate(which):
            base = base_ref.at[j].reshape(bins * ROWS, LANES)
            goal = goal_ref.at[j].reshape(bins * ROWS, LANES)
            result = next_ref.at[j].reshape(bins * ROWS, LANES)
            units = read_columns(hid_refs, j * wide, wide)
            source = jnp.dot(w_ref[...], units, preferred_element_type=F32)
            for i in range(half):
                at = pl.ds(first + i, bins, stride=ROWS)
                mask = pick(mask_ref, core, own, chunk, i, j)
                weight = (1.0 / count_of(count_ref, core, own, chunk, i)) * mask
                part = source[:, i * LANES : (i + 1) * LANES]
                new = base[at, :] + (0.5 * mask) * part
                result[at, :] = new
                back_ref[:, i * LANES : (i + 1) * LANES] = (weight * (new - goal[at, :])).astype(BF16)
            back = back_ref[...]
            total = total + lax.dot_general(back, units, (((1,), (1,)), ((), ())), preferred_element_type=F32)
            out = lax.dot_general(w_ref[...], back, (((0,), (0,)), ((), ())), preferred_element_type=F32)
            write_columns(out_refs, k * wide, out)
        grad_ref[...] = total

    return call(
        body,
        [(place, SMEM), (count, SMEM)] + [(v, VMEM) for v in (w_out, base, goal, mask, *hid, *seeds)],
        [(base.shape, F32), ((bins, hidden), F32)]
        + pieces_of((hidden, cells), F32, cut),
        (6 * bins * hidden * cells, 12 * bins * cells),
        scratch=[pltpu.VMEM((bins, wide), BF16)],
        aliases={3: 0},
        after=after,
        name="decode",
    )


def store(nexts, rows, after=()):
    parts, bins = nexts[0].shape[:2]
    n = len(nexts)

    def body(*refs):
        copies = []
        for c in range(n):
            for j in range(parts):
                to = refs[n].at[:, pl.ds(c * ROWS, ROWS), pl.ds(j * LANES, LANES)]
                copies.append(pltpu.make_async_copy(refs[c].at[j], to, refs[n + 2].at[c * parts + j]))
        for copy in copies:
            copy.start()
        refs[n + 1][...] = jnp.zeros(refs[n + 1].shape, F32)
        for copy in copies:
            copy.wait()

    size = bins * rows * parts * LANES
    return call(
        body,
        [(v, VMEM) for v in nexts],
        [((bins, rows, parts * LANES), F32, HBM), ((ROWS, LANES), F32)],
        (0, 8 * size),
        scratch=[pltpu.SemaphoreType.DMA((n * parts,))],
        after=after,
        name="store",
    )


def write_packed(ref, total):
    n = total.shape[0]
    most = jnp.max(jnp.max(jnp.abs(total), axis=1, keepdims=True), axis=0, keepdims=True)
    power = jnp.ceil(jnp.log2(jnp.maximum(most, 2.0**-100)))
    ref[0:n, :] = total
    ref[n:, :] = jnp.broadcast_to(power, (POWER_ROWS, total.shape[1]))


def write_scaled(refs, total, power):
    n, width = total.shape
    value = jnp.concatenate([total * jnp.exp2(-power), jnp.broadcast_to(power, (POWER_ROWS, width))], axis=0)
    write_columns(refs, 0, value)


def write_packed(refs, total):
    most = jnp.max(jnp.max(jnp.abs(total), axis=1, keepdims=True), axis=0, keepdims=True)
    power = jnp.ceil(jnp.log2(jnp.maximum(most, 2.0**-100)))
    write_scaled(refs, total, jnp.broadcast_to(power, (1, total.shape[1])))


def pack(total, cut, after=()):
    def body(total_ref, *out_refs):
        write_packed(out_refs, total_ref[...])

    n, width = total.shape
    outs = pieces_of((n + POWER_ROWS, width), F32, cut)
    return call(body, [(total, VMEM)], outs, (0, 0), after=after, name="pack")


def collect(spec, back, seed, cut=0, after=()):
    bins, cells = spec.shape
    hidden = back[0].shape[0]
    seeds = [seed] if seed is not None else []

    def body(spec_ref, *refs):
        values = read_columns(refs[: len(back)], 0, cells)
        total = lax.dot_general(spec_ref[...], values, (((1,), (1,)), ((), ())), preferred_element_type=F32)
        if seeds:
            total = total + refs[len(back)][...]
        if cut:
            write_packed(refs[len(back) + len(seeds) :], total)
        else:
            refs[-1][...] = total

    return call(
        body,
        [(v, VMEM) for v in (spec, *back, *seeds)],
        pieces_of((bins + POWER_ROWS, hidden), F32, cut) if cut else [((bins, hidden), F32)],
        (2 * bins * hidden * cells, 2 * bins * cells + 2 * hidden * cells),
        after=after,
        name="collect",
    )


def merge(mine, other, spare, after=()):
    rows, width = mine.shape
    n = rows - POWER_ROWS

    def body(mine_ref, other_ref, out_ref):
        here, there = mine_ref[n : n + 1], other_ref[n : n + 1]
        total = mine_ref[0:n] * jnp.exp2(here) + other_ref[0:n] * jnp.exp2(there)
        write_scaled([out_ref.at[0:rows]], total, jnp.maximum(here, there) + 1.0)
        if spare:
            out_ref[rows:] = jnp.zeros((spare, width), F32)

    values = [(mine, VMEM), (other, VMEM)]
    return call(body, values, [((rows + spare, width), F32)], (0, 0), after=after, name="merge")[0]


def merge_last(mine, other, n, after=()):
    k = len(mine)
    width = sum(v.shape[1] for v in mine)

    def body(*refs):
        out_ref, done_ref = refs[2 * k :]
        at = 0
        for a, b in zip(refs[:k], refs[k : 2 * k]):
            here, there = a[n : n + 1], b[n : n + 1]
            out_ref[:, at : at + a.shape[1]] = a[0:n] * jnp.exp2(here) + b[0:n] * jnp.exp2(there)
            at += a.shape[1]
        done_ref[...] = jnp.zeros(done_ref.shape, F32)

    values = [(v, VMEM) for v in (*mine, *other)]
    outs = [((n, width), F32, FREE), ((ROWS, LANES), F32)]
    return call(body, values, outs, (0, 0), after=after, name="merge_last")


def space_sum(packed, spare=0):
    n = packed[0].shape[0] - POWER_ROWS
    count = lax.axis_size("space")
    assert count & (count - 1) == 0 and count > 1
    bit = 1
    while True:
        mine = [lax.optimization_barrier(v.astype(F16)) for v in packed]
        other = [swap(v, "space", bit).astype(F32) for v in mine]
        mine = [v.astype(F32) for v in mine]
        bit *= 2
        after = yield packed[0]
        if bit >= count:
            yield merge_last(mine, other, n, after)
            return
        packed = [merge(a, b, spare if 2 * bit >= count else 0, after) for a, b in zip(mine, other)]


def courant(sectors, ndir, nfreq):
    angle = 2.0 * math.pi * (np.arange(NDIR) + 0.5) / NDIR
    speed = 1.0 / (1.0 + 2.3 * np.arange(nfreq) / nfreq)
    cx = np.abs(0.4 * np.cos(angle)[:, None] * speed[None, :])
    cy = np.abs(0.4 * np.sin(angle)[:, None] * speed[None, :])
    table = np.stack([1.0 - cx - cy - 0.3, cx, cy]).reshape(3, sectors, ndir * nfreq)
    return np.ascontiguousarray(table.transpose(1, 0, 2).reshape(3 * sectors, ndir * nfreq), np.float32)


def on_device(state, target, w_in, w_out, sea_mask, sea_count, turn_sign):
    ndir, nfreq, rows, lon = state.shape
    bins = ndir * nfreq
    hidden = w_in.shape[2]
    place = lax.axis_index("dir")
    sectors = lax.axis_size("dir")
    spaces = lax.axis_size("space")
    assert sectors == 4 and ndir * sectors == NDIR
    chunks, parts = rows // ROWS, lon // LANES
    place_ref = place.reshape(1)
    state = state.reshape(bins, rows, lon)
    target = target.reshape(bins, rows, lon)
    w_in = w_in.reshape(bins, hidden)
    w_out = jnp.transpose(w_out, (1, 2, 0)).reshape(bins, hidden)
    coef = jnp.asarray(courant(sectors, ndir, nfreq))

    tiles, spec, *send, mask, w_in = encode_first(place_ref, state, sea_mask, w_in, 4)
    pairs = []
    for s in range(spaces):
        for d in range(sectors):
            to = s - 1 if d >= sectors // 2 else s + 1
            if 0 <= to < spaces:
                pairs.append((s * sectors + d, to * sectors + d))
    near = swap(edge_bin(place_ref, tiles, ndir, True).astype(F16), "dir", 1).astype(F32)

    first = jnp.full((1, spec.shape[1]), PRE_SCALE, F32)
    specs, chips, crossed = [spec], [], []
    after = []
    for c in range(chunks):
        if c > 0:
            spec, *send = encode(place_ref, tiles, mask, w_in, c, False, 4, after=after)
            specs.append(spec)
            after = [spec]
        received = [swap(v, "dir", 1) for v in send]
        spec, own = encode(place_ref, tiles, mask, w_in, c, True, after=after)
        specs.append(spec)
        chips.append(join([own], received, first, 1))
        crossed.append(cross(chips[c]))
        after = chips[c][:1]

    far = edge_bin(place_ref, tiles, ndir, False, after=chips[0])
    far = swap(far.astype(F16), "dir", 3).astype(F32)
    edge = edge_row(place_ref, tiles, mask, after=chips[0])
    edge = lax.ppermute(edge.astype(F16), ("space", "dir"), pairs).astype(F32)

    stencils = []
    for c in range(chunks):
        stencils.append(
            stencil(
                place_ref, coef, tiles, near, mask, turn_sign, sea_count, target, [w_out, turn_sign][c % 2], c, ndir,
                after=[stencils[-1][0]] if c else chips[0],
            )
        )
    w_out = stencils[0][-1]
    after = [stencils[-1][0]]

    grad_out = None
    slopes, nexts, backs, back_crossed = [], [], [], []
    for c in range(chunks):
        base, goal, down, _, _ = stencils[c]
        base = turn_in(place_ref, coef, base, far, edge, mask, turn_sign, c, chunks, ndir, after=after)
        hid, slope = activate(chips[c], crossed[c], 4, after=[base])
        slopes.append(slope)
        other = [swap(v, "dir", 1) for v in hid]
        own = []
        for mine, which in ((True, range(1)), (False, range(parts)), (True, range(1, parts))):
            base, grad_out, *out = decode(
                place_ref, hid if mine else other, w_out, base, goal, mask, sea_count, grad_out, c, mine, which,
                cut=len(which) if mine else 4,
            )
            if mine:
                own += out
            else:
                received = [swap(v, "dir", 1) for v in out]
        nexts.append(base)
        backs.append(join(own, received, down, 2 if c + 1 == chunks else 1))
        back_crossed.append(cross(backs[c]))
        after = backs[c][:1]

    out_sum = space_sum(pack(grad_out, 1), 112)
    next(out_sum)
    merged = out_sum.send(())
    next_state, stored = store(nexts, rows, after=[merged])

    grad_in = None
    after = []
    for c in range(chunks):
        last = c + 1 == chunks
        back = slope_back(
            backs[c], back_crossed[c], stencils[c][3], slopes[c], 4 if last else 2, after=after[:2]
        )
        (grad_in,) = collect(specs[2 * c + 1], back, grad_in)
        grad_in = collect(
            specs[2 * c], [swap(v, "dir", 1) for v in back], grad_in, cut=2 if last else 0
        )
        if c + 2 == chunks:
            (grad_in,) = grad_in
            waits = [stored]
            while not isinstance(merged, (tuple, list)):
                before, merged, waits = merged, out_sum.send(waits), ()
            grad_out, summed = merged
            after = [before, grad_in, summed]
        elif not last:
            (grad_in,) = grad_in

    in_sum = space_sum(grad_in)
    next(in_sum)
    merged = in_sum.send([summed])
    while not isinstance(merged, (tuple, list)):
        merged = in_sum.send(())
    grad_in = merged[0]
    return (
        next_state.reshape(ndir, nfreq, rows, lon),
        grad_in.reshape(ndir, nfreq, hidden),
        jnp.transpose(grad_out.reshape(ndir, nfreq, hidden), (2, 0, 1)),
    )


def solution(mesh):
    in_specs = (
        P("dir", None, "space", None),
        P("dir", None, "space", None),
        P("dir", None, None),
        P(None, "dir", None),
        P("space", None),
        P("space"),
        P("space", None),
    )
    out_specs = (P("dir", None, "space", None), P("dir", None, None), P(None, "dir", None))
    return jax.shard_map(
        on_device, mesh=mesh, in_specs=in_specs, out_specs=out_specs, check_vma=False
    )
```

time: 115 us -> 88 us (0.77)
  waiting for transfers between devices: 49.3 us -> 15.9 us
  starting transfers between devices: 22.8 us -> 34.1 us
  other arithmetic: 6.25 us -> 1.26 us
  local copies, waits for them, and re-layouts: 4.3 us -> 0.37 us
  Pallas kernels: 31.2 us -> 34.6 us
    ppermute x22 -> x46, waiting for transfers between devices: 49.3 us -> 15.9 us  [swap(): return lax.ppermute(value, axis, [(i, i ^ bit) for i in range(count)])]
    ppermute x22 -> x46, starting transfers between devices: 18.3 us -> 30.6 us  [swap(): return lax.ppermute(value, axis, [(i, i ^ bit) for i in range(count)])]
    pallas_call x16 -> x39, Pallas kernels: 31.2 us -> 34.6 us  [call(): pl.pallas_call(run, in_specs=[spec for _, spec in ins] + [ANY] * len(afte...]
    convert_element_type x23 -> x41, other arithmetic: 3.69 us -> 1.22 us  [the longest x10 0.62 us: cross(): return [swap(v.astype(F16), 'dir', 2).astype(F32) for v in pieces]]
    unnamed x26 -> x8, local copies, waits for them, and re-layouts: 2.41 us -> 0.37 us
    dynamic_slice x1 -> x0, local copies, waits for them, and re-layouts: 1.88 us -> none  [on_device(): edge = lax.dynamic_index_in_dim(state, at, 1, False)]
    select_n x6 -> x0, other arithmetic: 1.42 us -> none  [space_sum(): jnp.where(body, mine * jnp.exp2(here) + other * jnp.exp2(there), jnp.maxi...]
  transfers between devices with their start and end apart: 23 -> 47, of which waited for: 11 -> 17; matrix products, arithmetic and copies ran while one was open for 6% -> 1% of each run, Pallas kernels for 21% -> 34%
where the time goes in v3:
time: 88 us; the launch traced here: 87.8 us
  Pallas kernels  34.6 us (39%)
  starting transfers between devices  34.1 us (39%)
  waiting for transfers between devices  15.9 us (18%)
  between operations  1.43 us (2%)
  other arithmetic  1.26 us (1%)
    pallas_call x39, Pallas kernels, call(): pl.pallas_call(run, in_specs=[spec for _, spec in ins] + [ANY] * len(afte...  34.6 us
    ppermute x46, starting transfers between devices, swap(): return lax.ppermute(value, axis, [(i, i ^ bit) for i in range(count)])  30.6 us
    ppermute x46, waiting for transfers between devices, swap(): return lax.ppermute(value, axis, [(i, i ^ bit) for i in range(count)])  15.9 us
    ppermute x1, starting transfers between devices, on_device(): edge = lax.ppermute(edge.astype(F16), ('space', 'dir'), pairs).astype(F32)  3.51 us
  transfers between devices with their start and end apart: 47, of which 17 were waited for; matrix products, arithmetic and copies ran while one was open for 1% of the time, Pallas kernels for 34%

profile of v3, /device:TPU:0, one launch (start us, length us, event | category | flops | bytes accessed | tf_op | source)
XLA Modules:
  0.0 87.8 jit_solution(2634506134478885818)
XLA Ops:
  0.6 3.0 %encode_first.1 = (f32[2,2,288,8,128]{4,3,2,1,0:T(8,128)S(1)}, bf16[288,1024]{1,0:T(8,128)(2,1)S(1)}, f32[256,256]{1,0:T(8,128)S(1)}, f32[256,256]{1,0:T(8,128)S...) custom-call(s32[1]{0:T(128)} %bitcast.refs_0_, ...), custom_call_target="tpu_custom_call" | custom-call | tf_op jit(solution)/shard_map/encode_first/pallas_call | solution.py:44
  7.9 2.9 %collective-permute-start.7 = (f16[256,1024]{1,0:T(8,128)(2,1)S(1)}, f16[256,1024]{1,0:T(8,128)(2,1)S(1)}, u32[]{:S(2)}, u32[]{:S(2)}) collective-permute-start(f16[256,1024]{1,0:T(8,128)(2,1)S(1)} %convert_element_type.135), channel_id=1, source_target_pairs={{0,2},{1,3},{2,0},{3,1},{4,6},{5,7},{6,4},{7,5},{8,10},{9,11},{10,... | collective-permute-start | bytes 1572872 | tf_op jit(solution)/shard_map/ppermute | solution.py:29
  12.4 3.5 %collective-permute-start.6 = (f16[2,288,128]{2,1,0:T(8,128)(2,1)S(1)}, f16[2,288,128]{2,1,0:T(8,128)(2,1)S(1)}, u32[]{:S(2)}, u32[]{:S(2)}) collective-permute-start(f16[2,288,128]{2,1,0:T(8,128)(2,1)S(1)} %convert_element_type.133), channel_id=1, source_target_pairs={{0,4},{1,5},{4,8},{5,9},{6,2},{7,3},{8,12},{9,13},{10,6},{11,7},{1... | collective-permute-start | bytes 442376 | tf_op jit(solution)/shard_map/ppermute | solution.py:645
  17.2 4.3 %stencil.2 = (f32[2,288,8,128]{3,2,1,0:T(8,128)S(1)}, f32[2,288,8,128]{3,2,1,0:T(8,128)S(1)}, f32[1,1024]{1,0:T(1,128)S(1)}, f32[1,1024]{1,0:T(1,128)S(1)}, bf16[288,256]{1,0:T(8,128)(2,1)S(1)}) custom-call(s32[1]{0:T(128)} %bitcast.refs_0_, f32[12,288]{1,0:T(8,128)S(1)} %copy-done.2, f32[2,2,288,8,128]{4,3,2,1,0:T(8,128)S(1)} %get-tuple-element.78.refs_1_.refs_2_, ...), custom_call_target="tpu_custom_call" | custom-call | tf_op jit(solution)/shard_map/stencil/pallas_call | solution.py:44
  21.5 4.9 %stencil.3 = (f32[2,288,8,128]{3,2,1,0:T(8,128)S(1)}, f32[2,288,8,128]{3,2,1,0:T(8,128)S(1)}, f32[1,1024]{1,0:T(1,128)S(1)}, f32[1,1024]{1,0:T(1,128)S(1)}, s32[16,256]{1,0:T(8,128)}) custom-call(s32[1]{0:T(128)} %bitcast.refs_0_, f32[12,288]{1,0:T(8,128)S(1)} %copy-done.2, f32[2,2,288,8,128]{4,3,2,1,0:T(8,128)S(1)} %get-tuple-element.78.refs_1_.refs_2_, ...), custom_call_target="tpu_custom_call" | custom-call | tf_op jit(solution)/shard_map/stencil/pallas_call | solution.py:44
  26.4 2.3 %collective-permute-done.5 = f16[2,2,32,8,128]{4,3,2,1,0:T(8,128)(2,1)S(1)} collective-permute-done((f16[2,2,32,8,128]{4,3,2,1,0:T(8,128)(2,1)S(1)}, f16[2,2,32,8,128]{4,3,2,1,0:T(8,128)(2,1)S(1)}, u32[]{:S(2)}, u32[]{:S(2)}) %collective-permute-start.5) | collective-permute-done | bytes 262176 | tf_op jit(solution)/shard_map/ppermute | solution.py:29
  31.6 1.5 %decode.6 = (f32[2,288,8,128]{3,2,1,0:T(8,128)S(1)}, f32[288,256]{1,0:T(8,128)S(1)}, f32[256,512]{1,0:T(8,128)S(1)}) custom-call(s32[1]{0:T(128)} %bitcast.refs_0_, s32[16]{0:T(128)S(1)} %copy-done.3, bf16[288,256]{1,0:T(8,128)(2,1)S(1)} %get-tuple-element.86.refs_2_, ...), custom_call_target="tpu_custom_call", output_to_operand_aliasing={{0}: (3, {})} | custom-call | tf_op jit(solution)/shard_map/decode/pallas_call | solution.py:44
  33.1 2.3 %decode.7 = (f32[2,288,8,128]{3,2,1,0:T(8,128)S(1)}, f32[288,256]{1,0:T(8,128)S(1)}, f32[256,256]{1,0:T(8,128)S(1)}, f32[256,256]{1,0:T(8,128)S(1)}, f32[256,256]{1,0:T(8,128)S(1)}, /*index=5*/f32[256,256]{1,0:T(8,128)S(1)}) custom-call(s32[1]{0:T(128)} %bitcast.refs_0_, s32[16]{0:T(128)S(1)} %copy-done.3, ...), custom_call_target="tpu_custom_call", output_to_operand_aliasing={{0}: (3, {})} | custom-call | tf_op jit(solution)/shard_map/decode/pallas_call | solution.py:44
  36.4 1.5 %decode.8 = (f32[2,288,8,128]{3,2,1,0:T(8,128)S(1)}, f32[288,256]{1,0:T(8,128)S(1)}, f32[256,512]{1,0:T(8,128)S(1)}) custom-call(s32[1]{0:T(128)} %bitcast.refs_0_, s32[16]{0:T(128)S(1)} %copy-done.3, bf16[288,256]{1,0:T(8,128)(2,1)S(1)} %get-tuple-element.86.refs_2_, ...), custom_call_target="tpu_custom_call", output_to_operand_aliasing={{0}: (3, {})} | custom-call | tf_op jit(solution)/shard_map/decode/pallas_call | solution.py:44
  38.3 1.9 %collective-permute-start.33 = (f16[256,1024]{1,0:T(8,128)(2,1)S(1)}, f16[256,1024]{1,0:T(8,128)(2,1)S(1)}, u32[]{:S(2)}, u32[]{:S(2)}) collective-permute-start(f16[256,1024]{1,0:T(8,128)(2,1)S(1)} %convert_element_type.149), channel_id=1, source_target_pairs={{0,2},{1,3},{2,0},{3,1},{4,6},{5,7},{6,4},{7,5},{8,10},{9,11},{10,... | collective-permute-start | bytes 1572872 | tf_op jit(solution)/shard_map/ppermute | solution.py:29
  43.1 1.5 %decode.9 = (f32[2,288,8,128]{3,2,1,0:T(8,128)S(1)}, f32[288,256]{1,0:T(8,128)S(1)}, f32[256,512]{1,0:T(8,128)S(1)}) custom-call(s32[1]{0:T(128)} %bitcast.refs_0_, s32[16]{0:T(128)S(1)} %copy-done.3, bf16[288,256]{1,0:T(8,128)(2,1)S(1)} %get-tuple-element.86.refs_2_, ...), custom_call_target="tpu_custom_call", output_to_operand_aliasing={{0}: (3, {})} | custom-call | tf_op jit(solution)/shard_map/decode/pallas_call | solution.py:44
  44.6 2.2 %decode.10 = (f32[2,288,8,128]{3,2,1,0:T(8,128)S(1)}, f32[288,256]{1,0:T(8,128)S(1)}, f32[256,256]{1,0:T(8,128)S(1)}, f32[256,256]{1,0:T(8,128)S(1)}, f32[256,256]{1,0:T(8,128)S(1)}, /*index=5*/f32[256,256]{1,0:T(8,128)S(1)}) custom-call(s32[1]{0:T(128)} %bitcast.refs_0_, s32[16]{0:T(128)S(1)} %copy-done.3, ...), custom_call_target="tpu_custom_call", output_to_operand_aliasing={{0}: (3, {})} | custom-call | tf_op jit(solution)/shard_map/decode/pallas_call | solution.py:44
  47.9 1.5 %decode.11 = (f32[2,288,8,128]{3,2,1,0:T(8,128)S(1)}, f32[288,256]{1,0:T(8,128)S(1)}, f32[256,512]{1,0:T(8,128)S(1)}) custom-call(s32[1]{0:T(128)} %bitcast.refs_0_, s32[16]{0:T(128)S(1)} %copy-done.3, bf16[288,256]{1,0:T(8,128)(2,1)S(1)} %get-tuple-element.86.refs_2_, ...), custom_call_target="tpu_custom_call", output_to_operand_aliasing={{0}: (3, {})} | custom-call | tf_op jit(solution)/shard_map/decode/pallas_call | solution.py:44
  49.6 1.6 %collective-permute-start.25 = (f16[304,256]{1,0:T(8,128)(2,1)S(1)}, f16[304,256]{1,0:T(8,128)(2,1)S(1)}, u32[]{:S(2)}, u32[]{:S(2)}) collective-permute-start(f16[304,256]{1,0:T(8,128)(2,1)S(1)} %convert_element_type.139), channel_id=1, source_target_pairs={{0,4},{4,0},{8,12},{12,8},{16,20},{20,16},{24,28},{28,24},{1,5},{5... | collective-permute-start | bytes 466952 | tf_op jit(solution)/shard_map/ppermute | solution.py:29
  51.4 1.5 %collective-permute-start.30 = (f16[256,512]{1,0:T(8,128)(2,1)S(1)}, f16[256,512]{1,0:T(8,128)(2,1)S(1)}, u32[]{:S(2)}, u32[]{:S(2)}) collective-permute-start(f16[256,512]{1,0:T(8,128)(2,1)S(1)} %convert_element_type.142), channel_id=1, source_target_pairs={{0,2},{1,3},{2,0},{3,1},{4,6},{5,7},{6,4},{7,5},{8,10},{9,11},{10,... | collective-permute-start | bytes 786440 | tf_op jit(solution)/shard_map/ppermute | solution.py:29
  55.8 1.6 %collective-permute-start.32 = (f16[304,256]{1,0:T(8,128)(2,1)S(1)}, f16[304,256]{1,0:T(8,128)(2,1)S(1)}, u32[]{:S(2)}, u32[]{:S(2)}) collective-permute-start(f16[304,256]{1,0:T(8,128)(2,1)S(1)} %convert_element_type.146), channel_id=1, source_target_pairs={{0,8},{4,12},{8,0},{12,4},{16,24},{20,28},{24,16},{28,20},{1,9},{5... | collective-permute-start | bytes 466952 | tf_op jit(solution)/shard_map/ppermute | solution.py:29
  57.5 2.2 %store.1 = (f32[288,16,256]{2,1,0:T(8,128)}, f32[8,128]{1,0:T(8,128)S(1)}) custom-call(f32[2,288,8,128]{3,2,1,0:T(8,128)S(1)} %get-tuple-element.98.refs_0_, f32[2,288,8,128]{3,2,1,0:T(8,128)S(1)} %get-tuple-element.122.refs_1_, f32[304,256]{1,0:T(8,128)S(1)} %merge.6.refs_2_), custom_call_target="tpu_custom_call" | custom-call | tf_op jit(solution)/shard_map/store/pallas_call | solution.py:44
  61.2 2.7 %collective-permute-start.41 = (f16[416,256]{1,0:T(8,128)(2,1)S(1)}, f16[416,256]{1,0:T(8,128)(2,1)S(1)}, u32[]{:S(2)}, u32[]{:S(2)}) collective-permute-start(f16[416,256]{1,0:T(8,128)(2,1)S(1)} %convert_element_type.154), channel_id=1, source_target_pairs={{0,16},{4,20},{8,24},{12,28},{16,0},{20,4},{24,8},{28,12},{1,17},{... | collective-permute-start | bytes 638984 | tf_op jit(solution)/shard_map/ppermute | solution.py:29
  70.8 1.5 %collective-permute-done.41 = f16[416,256]{1,0:T(8,128)(2,1)S(1)} collective-permute-done((f16[416,256]{1,0:T(8,128)(2,1)S(1)}, f16[416,256]{1,0:T(8,128)(2,1)S(1)}, u32[]{:S(2)}, u32[]{:S(2)}) %collective-permute-start.41) | collective-permute-done | bytes 213024 | tf_op jit(solution)/shard_map/ppermute | solution.py:29
  73.9 1.6 %collective-permute-start.44 = (f16[304,128]{1,0:T(8,128)(2,1)S(1)}, f16[304,128]{1,0:T(8,128)(2,1)S(1)}, u32[]{:S(2)}, u32[]{:S(2)}) collective-permute-start(f16[304,128]{1,0:T(8,128)(2,1)S(1)} %convert_element_type.165), channel_id=1, source_target_pairs={{0,8},{4,12},{8,0},{12,4},{16,24},{20,28},{24,16},{28,20},{1,9},{5... | collective-permute-start | bytes 233480 | tf_op jit(solution)/shard_map/ppermute | solution.py:29
  76.6 2.2 %collective-permute-done.44 = f16[304,128]{1,0:T(8,128)(2,1)S(1)} collective-permute-done((f16[304,128]{1,0:T(8,128)(2,1)S(1)}, f16[304,128]{1,0:T(8,128)(2,1)S(1)}, u32[]{:S(2)}, u32[]{:S(2)}) %collective-permute-start.44) | collective-permute-done | bytes 77856 | tf_op jit(solution)/shard_map/ppermute | solution.py:29
  78.9 2.7 %collective-permute-start.46 = (f16[304,128]{1,0:T(8,128)(2,1)S(1)}, f16[304,128]{1,0:T(8,128)(2,1)S(1)}, u32[]{:S(2)}, u32[]{:S(2)}) collective-permute-start(f16[304,128]{1,0:T(8,128)(2,1)S(1)} %convert_element_type.168), channel_id=1, source_target_pairs={{0,16},{4,20},{8,24},{12,28},{16,0},{20,4},{24,8},{28,12},{1,17},{... | collective-permute-start | bytes 233480 | tf_op jit(solution)/shard_map/ppermute | solution.py:29
  81.6 1.6 %collective-permute-start.45 = (f16[304,128]{1,0:T(8,128)(2,1)S(1)}, f16[304,128]{1,0:T(8,128)(2,1)S(1)}, u32[]{:S(2)}, u32[]{:S(2)}) collective-permute-start(f16[304,128]{1,0:T(8,128)(2,1)S(1)} %convert_element_type.160), channel_id=1, source_target_pairs={{0,16},{4,20},{8,24},{12,28},{16,0},{20,4},{24,8},{28,12},{1,17},{... | collective-permute-start | bytes 233480 | tf_op jit(solution)/shard_map/ppermute | solution.py:29
  83.3 2.6 %collective-permute-done.46 = f16[304,128]{1,0:T(8,128)(2,1)S(1)} collective-permute-done((f16[304,128]{1,0:T(8,128)(2,1)S(1)}, f16[304,128]{1,0:T(8,128)(2,1)S(1)}, u32[]{:S(2)}, u32[]{:S(2)}) %collective-permute-start.46) | collective-permute-done | bytes 77856 | tf_op jit(solution)/shard_map/ppermute | solution.py:29
  (161 shorter events, 31.2 us)
Async XLA Ops:
  7.2 4.2 %collective-permute-start.16 = (f32[256,256]{1,0:T(8,128)S(1)}, f32[256,256]{1,0:T(8,128)S(1)}, u32[]{:S(2)}, u32[]{:S(2)}) collective-permute-start(f32[256,256]{1,0:T(8,128)S(1)} %get-tuple-element.109), channel_id=1, source_target_pairs={{0,1},{1,0},{2,3},{3,2},{4,5},{5,4},{6,7},{7,6},{8,9},{9,8},{10,11... | collective-permute-start | bytes 786440 | tf_op jit(solution)/shard_map/ppermute | solution.py:29
  7.6 4.0 %collective-permute-start.17 = (f32[256,256]{1,0:T(8,128)S(1)}, f32[256,256]{1,0:T(8,128)S(1)}, u32[]{:S(2)}, u32[]{:S(2)}) collective-permute-start(f32[256,256]{1,0:T(8,128)S(1)} %get-tuple-element.110), channel_id=1, source_target_pairs={{0,1},{1,0},{2,3},{3,2},{4,5},{5,4},{6,7},{7,6},{8,9},{9,8},{10,11... | collective-permute-start | bytes 786440 | tf_op jit(solution)/shard_map/ppermute | solution.py:29
  7.9 22.0 %collective-permute-start.7 = (f16[256,1024]{1,0:T(8,128)(2,1)S(1)}, f16[256,1024]{1,0:T(8,128)(2,1)S(1)}, u32[]{:S(2)}, u32[]{:S(2)}) collective-permute-start(f16[256,1024]{1,0:T(8,128)(2,1)S(1)} %convert_element_type.135), channel_id=1, source_target_pairs={{0,2},{1,3},{2,0},{3,1},{4,6},{5,7},{6,4},{7,5},{8,10},{9,11},{10,... | collective-permute-start | bytes 1572872 | tf_op jit(solution)/shard_map/ppermute | solution.py:29
  10.8 5.6 %collective-permute-start.19 = (f32[256,256]{1,0:T(8,128)S(1)}, f32[256,256]{1,0:T(8,128)S(1)}, u32[]{:S(2)}, u32[]{:S(2)}) collective-permute-start(f32[256,256]{1,0:T(8,128)S(1)} %get-tuple-element.112), channel_id=1, source_target_pairs={{0,1},{1,0},{2,3},{3,2},{4,5},{5,4},{6,7},{7,6},{8,9},{9,8},{10,11... | collective-permute-start | bytes 786440 | tf_op jit(solution)/shard_map/ppermute | solution.py:29
  11.4 5.4 %collective-permute-start = (f16[2,2,32,8,128]{4,3,2,1,0:T(8,128)(2,1)S(1)}, f16[2,2,32,8,128]{4,3,2,1,0:T(8,128)(2,1)S(1)}, u32[]{:S(2)}, u32[]{:S(2)}) collective-permute-start(f16[2,2,32,8,128]{4,3,2,1,0:T(8,128)(2,1)S(1)} %convert_element_type.129), channel_id=1, source_target_pairs={{0,1},{1,0},{2,3},{3,2},{4,5},{5,4},{6,7},{7,6},{8,9},{9,8},{10,11... | collective-permute-start | bytes 786440 | tf_op jit(solution)/shard_map/ppermute | solution.py:29
  11.6 17.1 %collective-permute-start.5 = (f16[2,2,32,8,128]{4,3,2,1,0:T(8,128)(2,1)S(1)}, f16[2,2,32,8,128]{4,3,2,1,0:T(8,128)(2,1)S(1)}, u32[]{:S(2)}, u32[]{:S(2)}) collective-permute-start(f16[2,2,32,8,128]{4,3,2,1,0:T(8,128)(2,1)S(1)} %convert_element_type.131), channel_id=1, source_target_pairs={{0,3},{1,2},{2,1},{3,0},{4,7},{5,6},{6,5},{7,4},{8,11},{9,10},{10,... | collective-permute-start | bytes 786440 | tf_op jit(solution)/shard_map/ppermute | solution.py:29
  12.4 14.0 %collective-permute-start.6 = (f16[2,288,128]{2,1,0:T(8,128)(2,1)S(1)}, f16[2,288,128]{2,1,0:T(8,128)(2,1)S(1)}, u32[]{:S(2)}, u32[]{:S(2)}) collective-permute-start(f16[2,288,128]{2,1,0:T(8,128)(2,1)S(1)} %convert_element_type.133), channel_id=1, source_target_pairs={{0,4},{1,5},{4,8},{5,9},{6,2},{7,3},{8,12},{9,13},{10,6},{11,7},{1... | collective-permute-start | bytes 442376 | tf_op jit(solution)/shard_map/ppermute | solution.py:645
  16.7 23.5 %collective-permute-start.20 = (f16[256,1024]{1,0:T(8,128)(2,1)S(1)}, f16[256,1024]{1,0:T(8,128)(2,1)S(1)}, u32[]{:S(2)}, u32[]{:S(2)}) collective-permute-start(f16[256,1024]{1,0:T(8,128)(2,1)S(1)} %convert_element_type.137), channel_id=1, source_target_pairs={{0,2},{1,3},{2,0},{3,1},{4,6},{5,7},{6,4},{7,5},{8,10},{9,11},{10,... | collective-permute-start | bytes 1572872 | tf_op jit(solution)/shard_map/ppermute | solution.py:29
  38.3 15.3 %collective-permute-start.33 = (f16[256,1024]{1,0:T(8,128)(2,1)S(1)}, f16[256,1024]{1,0:T(8,128)(2,1)S(1)}, u32[]{:S(2)}, u32[]{:S(2)}) collective-permute-start(f16[256,1024]{1,0:T(8,128)(2,1)S(1)} %convert_element_type.149), channel_id=1, source_target_pairs={{0,2},{1,3},{2,0},{3,1},{4,6},{5,7},{6,4},{7,5},{8,10},{9,11},{10,... | collective-permute-start | bytes 1572872 | tf_op jit(solution)/shard_map/ppermute | solution.py:29
  47.0 4.2 %collective-permute-start.27 = (f32[256,256]{1,0:T(8,128)S(1)}, f32[256,256]{1,0:T(8,128)S(1)}, u32[]{:S(2)}, u32[]{:S(2)}) collective-permute-start(f32[256,256]{1,0:T(8,128)S(1)} %get-tuple-element.131), channel_id=1, source_target_pairs={{0,1},{1,0},{2,3},{3,2},{4,5},{5,4},{6,7},{7,6},{8,9},{9,8},{10,11... | collective-permute-start | bytes 786440 | tf_op jit(solution)/shard_map/ppermute | solution.py:29
  47.4 3.8 %collective-permute-start.28 = (f32[256,256]{1,0:T(8,128)S(1)}, f32[256,256]{1,0:T(8,128)S(1)}, u32[]{:S(2)}, u32[]{:S(2)}) collective-permute-start(f32[256,256]{1,0:T(8,128)S(1)} %get-tuple-element.132), channel_id=1, source_target_pairs={{0,1},{1,0},{2,3},{3,2},{4,5},{5,4},{6,7},{7,6},{8,9},{9,8},{10,11... | collective-permute-start | bytes 786440 | tf_op jit(solution)/shard_map/ppermute | solution.py:29
  49.6 6.1 %collective-permute-start.25 = (f16[304,256]{1,0:T(8,128)(2,1)S(1)}, f16[304,256]{1,0:T(8,128)(2,1)S(1)}, u32[]{:S(2)}, u32[]{:S(2)}) collective-permute-start(f16[304,256]{1,0:T(8,128)(2,1)S(1)} %convert_element_type.139), channel_id=1, source_target_pairs={{0,4},{4,0},{8,12},{12,8},{16,20},{20,16},{24,28},{28,24},{1,5},{5... | collective-permute-start | bytes 466952 | tf_op jit(solution)/shard_map/ppermute | solution.py:29
  51.4 12.8 %collective-permute-start.30 = (f16[256,512]{1,0:T(8,128)(2,1)S(1)}, f16[256,512]{1,0:T(8,128)(2,1)S(1)}, u32[]{:S(2)}, u32[]{:S(2)}) collective-permute-start(f16[256,512]{1,0:T(8,128)(2,1)S(1)} %convert_element_type.142), channel_id=1, source_target_pairs={{0,2},{1,3},{2,0},{3,1},{4,6},{5,7},{6,4},{7,5},{8,10},{9,11},{10,... | collective-permute-start | bytes 786440 | tf_op jit(solution)/shard_map/ppermute | solution.py:29
  53.0 12.1 %collective-permute-start.31 = (f16[256,512]{1,0:T(8,128)(2,1)S(1)}, f16[256,512]{1,0:T(8,128)(2,1)S(1)}, u32[]{:S(2)}, u32[]{:S(2)}) collective-permute-start(f16[256,512]{1,0:T(8,128)(2,1)S(1)} %convert_element_type.144), channel_id=1, source_target_pairs={{0,2},{1,3},{2,0},{3,1},{4,6},{5,7},{6,4},{7,5},{8,10},{9,11},{10,... | collective-permute-start | bytes 786440 | tf_op jit(solution)/shard_map/ppermute | solution.py:29
  54.1 11.2 %collective-permute-start.34 = (bf16[256,512]{1,0:T(8,128)(2,1)S(1)}, bf16[256,512]{1,0:T(8,128)(2,1)S(1)}, u32[]{:S(2)}, u32[]{:S(2)}) collective-permute-start(bf16[256,512]{1,0:T(8,128)(2,1)S(1)} %get-tuple-element.140.refs_1_), channel_id=1, source_target_pairs={{0,1},{1,0},{2,3},{3,2},{4,5},{5,4},{6,7},{7,6},{8,9},{9,8},{10,11... | collective-permute-start | bytes 786440 | tf_op jit(solution)/shard_map/ppermute | solution.py:29
  54.1 11.1 %collective-permute-start.35 = (bf16[256,512]{1,0:T(8,128)(2,1)S(1)}, bf16[256,512]{1,0:T(8,128)(2,1)S(1)}, u32[]{:S(2)}, u32[]{:S(2)}) collective-permute-start(bf16[256,512]{1,0:T(8,128)(2,1)S(1)} %get-tuple-element.141.refs_2_), channel_id=1, source_target_pairs={{0,1},{1,0},{2,3},{3,2},{4,5},{5,4},{6,7},{7,6},{8,9},{9,8},{10,11... | collective-permute-start | bytes 786440 | tf_op jit(solution)/shard_map/ppermute | solution.py:29
  55.8 5.3 %collective-permute-start.32 = (f16[304,256]{1,0:T(8,128)(2,1)S(1)}, f16[304,256]{1,0:T(8,128)(2,1)S(1)}, u32[]{:S(2)}, u32[]{:S(2)}) collective-permute-start(f16[304,256]{1,0:T(8,128)(2,1)S(1)} %convert_element_type.146), channel_id=1, source_target_pairs={{0,8},{4,12},{8,0},{12,4},{16,24},{20,28},{24,16},{28,20},{1,9},{5... | collective-permute-start | bytes 466952 | tf_op jit(solution)/shard_map/ppermute | solution.py:29
  61.2 11.1 %collective-permute-start.41 = (f16[416,256]{1,0:T(8,128)(2,1)S(1)}, f16[416,256]{1,0:T(8,128)(2,1)S(1)}, u32[]{:S(2)}, u32[]{:S(2)}) collective-permute-start(f16[416,256]{1,0:T(8,128)(2,1)S(1)} %convert_element_type.154), channel_id=1, source_target_pairs={{0,16},{4,20},{8,24},{12,28},{16,0},{20,4},{24,8},{28,12},{1,17},{... | collective-permute-start | bytes 638984 | tf_op jit(solution)/shard_map/ppermute | solution.py:29
  68.6 5.2 %collective-permute-start.43 = (f16[304,128]{1,0:T(8,128)(2,1)S(1)}, f16[304,128]{1,0:T(8,128)(2,1)S(1)}, u32[]{:S(2)}, u32[]{:S(2)}) collective-permute-start(f16[304,128]{1,0:T(8,128)(2,1)S(1)} %convert_element_type.162), channel_id=1, source_target_pairs={{0,4},{4,0},{8,12},{12,8},{16,20},{20,16},{24,28},{28,24},{1,5},{5... | collective-permute-start | bytes 233480 | tf_op jit(solution)/shard_map/ppermute | solution.py:29
  69.3 6.2 %collective-permute-start.40 = (f16[304,128]{1,0:T(8,128)(2,1)S(1)}, f16[304,128]{1,0:T(8,128)(2,1)S(1)}, u32[]{:S(2)}, u32[]{:S(2)}) collective-permute-start(f16[304,128]{1,0:T(8,128)(2,1)S(1)} %convert_element_type.151), channel_id=1, source_target_pairs={{0,4},{4,0},{8,12},{12,8},{16,20},{20,16},{24,28},{28,24},{1,5},{5... | collective-permute-start | bytes 233480 | tf_op jit(solution)/shard_map/ppermute | solution.py:29
  73.9 4.9 %collective-permute-start.44 = (f16[304,128]{1,0:T(8,128)(2,1)S(1)}, f16[304,128]{1,0:T(8,128)(2,1)S(1)}, u32[]{:S(2)}, u32[]{:S(2)}) collective-permute-start(f16[304,128]{1,0:T(8,128)(2,1)S(1)} %convert_element_type.165), channel_id=1, source_target_pairs={{0,8},{4,12},{8,0},{12,4},{16,24},{20,28},{24,16},{28,20},{1,9},{5... | collective-permute-start | bytes 233480 | tf_op jit(solution)/shard_map/ppermute | solution.py:29
  75.6 5.9 %collective-permute-start.42 = (f16[304,128]{1,0:T(8,128)(2,1)S(1)}, f16[304,128]{1,0:T(8,128)(2,1)S(1)}, u32[]{:S(2)}, u32[]{:S(2)}) collective-permute-start(f16[304,128]{1,0:T(8,128)(2,1)S(1)} %convert_element_type.157), channel_id=1, source_target_pairs={{0,8},{4,12},{8,0},{12,4},{16,24},{20,28},{24,16},{28,20},{1,9},{5... | collective-permute-start | bytes 233480 | tf_op jit(solution)/shard_map/ppermute | solution.py:29
  78.9 7.0 %collective-permute-start.46 = (f16[304,128]{1,0:T(8,128)(2,1)S(1)}, f16[304,128]{1,0:T(8,128)(2,1)S(1)}, u32[]{:S(2)}, u32[]{:S(2)}) collective-permute-start(f16[304,128]{1,0:T(8,128)(2,1)S(1)} %convert_element_type.168), channel_id=1, source_target_pairs={{0,16},{4,20},{8,24},{12,28},{16,0},{20,4},{24,8},{28,12},{1,17},{... | collective-permute-start | bytes 233480 | tf_op jit(solution)/shard_map/ppermute | solution.py:29
  81.6 5.4 %collective-permute-start.45 = (f16[304,128]{1,0:T(8,128)(2,1)S(1)}, f16[304,128]{1,0:T(8,128)(2,1)S(1)}, u32[]{:S(2)}, u32[]{:S(2)}) collective-permute-start(f16[304,128]{1,0:T(8,128)(2,1)S(1)} %convert_element_type.160), channel_id=1, source_target_pairs={{0,16},{4,20},{8,24},{12,28},{16,0},{20,4},{24,8},{28,12},{1,17},{... | collective-permute-start | bytes 233480 | tf_op jit(solution)/shard_map/ppermute | solution.py:29
  (27 other events, 56.2 us)

commit v4 on v3

--- a/solution.py
+++ b/solution.py
@@ -14,6 +14,7 @@
 PRE_SCALE = 64.0
 BACK_SCALE = 2.0**-8
 LIMIT1 = 16
+UNROLL = 32
 POWER_ROWS = 16
 
 BF16, F16, F32 = jnp.bfloat16, jnp.float16, jnp.float32
@@ -96,13 +97,13 @@
 
 
 def encode_rows(place_ref, tiles_ref, mask_ref, w_ref, spec_ref, out_refs, chunk, own):
-    parts, bins = tiles_ref.shape[1:3]
+    parts, bins = tiles_ref.shape[:2]
     half = ROWS // 2
     wide = half * LANES
     core = place_ref[0] % 2
     first = first_row(core, own)
     for j in range(parts):
-        flat = tiles_ref.at[chunk, j].reshape(bins * ROWS, LANES)
+        flat = tiles_ref.at[j].reshape(bins * ROWS, LANES)
         cols = []
         for i in range(half):
             row = flat[pl.ds(first + i, bins, stride=ROWS), :]
@@ -113,56 +114,103 @@
         write_columns(out_refs, j * wide, out)
 
 
-def encode_first(place, state, mask, w_in, cut, after=()):
+def block(ref, c, j, bins=slice(None)):
+    return ref.at[bins, pl.ds(c * ROWS, ROWS), pl.ds(j * LANES, LANES)]
+
+
+def copy_near(place, tiles_ref, near_refs, nfreq):
+    start = pl.multiple_of((1 - place % 2) * (tiles_ref.shape[1] - nfreq), 8)
+    for j, ref in enumerate(near_refs):
+        ref[...] = tiles_ref[j, pl.ds(start, nfreq)]
+
+
+def encode_first(place, state, mask, w_in, ndir, cut, after=()):
     bins, rows, lon = state.shape
+    nfreq = bins // ndir
     hidden = w_in.shape[1]
     chunks, parts = rows // ROWS, lon // LANES
     cells = parts * ROWS * LANES // 2
 
-    def body(place_ref, state_ref, mask_hbm, w_hbm, tiles_ref, spec_ref, *refs):
-        out_refs, (mask_ref, w_ref, sems) = refs[:cut], refs[cut:]
-        small = [
-            pltpu.make_async_copy(a, b, sems.at[chunks * parts + k])
-            for k, (a, b) in enumerate([(mask_hbm, mask_ref), (w_hbm, w_ref)])
-        ]
-        copies = [
-            [
-                pltpu.make_async_copy(
-                    state_ref.at[:, pl.ds(c * ROWS, ROWS), pl.ds(j * LANES, LANES)],
-                    tiles_ref.at[c, j],
-                    sems.at[c * parts + j],
-                )
-                for j in range(parts)
-            ]
-            for c in range(chunks)
-        ]
-        for row in copies:
-            for copy in row:
-                copy.start()
-        for copy in small:
+    def body(place_ref, state_ref, mask_hbm, w_hbm, tiles_ref, far_ref, spec_ref, *refs):
+        out_refs, near_refs, (mask_ref, w_ref, sems) = refs[:cut], refs[cut : cut + parts], refs[cut + parts :]
+        place = place_ref[0]
+        copies = [(block(state_ref, 0, j), tiles_ref.at[j]) for j in range(parts)]
+        copies += [(mask_hbm, mask_ref), (w_hbm, w_ref)]
+        edge = pl.ds(pl.multiple_of((place % 2) * (bins - nfreq), 8), nfreq)
+        copies += [(block(state_ref, c, j, edge), far_ref.at[c, j]) for c in range(chunks) for j in range(parts)]
+        copies = [pltpu.make_async_copy(*copy, sems.at[k]) for k, copy in enumerate(copies)]
+        for copy in copies:
             copy.start()
-        for copy in copies[0] + small:
+        for copy in copies[: parts + 2]:
             copy.wait()
         encode_rows(place_ref, tiles_ref, mask_ref, w_ref, spec_ref, out_refs, 0, False)
-        for row in copies[1:]:
-            for copy in row:
-                copy.wait()
+        copy_near(place, tiles_ref, near_refs, nfreq)
+        for copy in copies[parts + 2 :]:
+            copy.wait()
 
     return call(
         body,
         [(place, SMEM), (state, HBM), (mask, HBM), (w_in, HBM)],
-        [((chunks, parts, bins, ROWS, LANES), F32), ((bins, cells), BF16), *pieces_of((hidden, cells), F32, cut)]
-        + [(mask.shape, mask.dtype), (w_in.shape, w_in.dtype)],
+        [
+            ((parts, bins, ROWS, LANES), F32),
+            ((chunks, parts, nfreq, ROWS, LANES), F32),
+            ((bins, cells), BF16),
+            *pieces_of((hidden, cells), F32, cut),
+            *[((nfreq, ROWS, LANES), F32)] * parts,
+            (mask.shape, mask.dtype),
+            (w_in.shape, w_in.dtype),
+        ],
         (2 * bins * hidden * cells, 4 * bins * rows * lon),
-        scratch=[pltpu.SemaphoreType.DMA((chunks * parts + 2,))],
+        scratch=[pltpu.SemaphoreType.DMA(((1 + chunks) * parts + 2,))],
         after=after,
-        limit=LIMIT1,
         name="encode_first",
     )
 
 
+def load_rest(place, state, tiles, mask, ndir, after=()):
+    bins, rows, lon = state.shape
+    nfreq = bins // ndir
+    chunks, parts = rows // ROWS, lon // LANES
+    rest = chunks - 1
+
+    def body(place_ref, state_ref, first_ref, mask_ref, *refs):
+        tiles_refs, near_refs, (edge_ref, sems) = refs[:rest], refs[rest : rest + rest * parts], refs[rest + rest * parts :]
+        copies = [
+            pltpu.make_async_copy(block(state_ref, c + 1, j), tiles_refs[c].at[j], sems.at[c * parts + j])
+            for c in range(rest)
+            for j in range(parts)
+        ]
+        for copy in copies:
+            copy.start()
+        for copy in copies:
+            copy.wait()
+        for c in range(rest):
+            copy_near(place_ref[0], tiles_refs[c], near_refs[c * parts : (c + 1) * parts], nfreq)
+        for north in (False, True):
+            at, i, ref = (0, 0, first_ref) if north else (rows - ROWS, ROWS - 1, tiles_refs[-1])
+
+            @pl.when((place_ref[0] >= 2) == north)
+            def _():
+                for j in range(parts):
+                    mask = mask_ref[at + i : at + i + 1, j * LANES : (j + 1) * LANES].astype(F32)
+                    flat = ref.at[j].reshape(bins * ROWS, LANES)
+                    edge_ref[j] = flat[pl.ds(i, bins, stride=ROWS), :] * mask
+
+    outs = call(
+        body,
+        [(place, SMEM), (state, HBM), (tiles, VMEM), (mask, VMEM)],
+        [(tiles.shape, F32)] * rest + [((nfreq, ROWS, LANES), F32)] * (rest * parts) + [((parts, bins, LANES), F32)],
+        (0, 4 * bins * rows * lon),
+        scratch=[pltpu.SemaphoreType.DMA((rest * parts,))],
+        after=after,
+        name="load_rest",
+    )
+    near = [outs[rest + c * parts : rest + (c + 1) * parts] for c in range(rest)]
+    return outs[:rest], near, outs[-1]
+
+
 def encode(place, tiles, mask, w_in, chunk, own, cut=1, after=()):
-    parts, bins = tiles.shape[1:3]
+    parts, bins = tiles.shape[:2]
     hidden = w_in.shape[1]
     cells = parts * ROWS * LANES // 2
 
@@ -177,39 +225,6 @@
         after=after,
         name="encode",
     )
-
-
-def edge_bin(place, tiles, ndir, own, after=()):
-    chunks, parts, bins = tiles.shape[:3]
-    nfreq = bins // ndir
-
-    def body(place_ref, tiles_ref, out_ref):
-        upper = place_ref[0] % 2
-        start = pl.multiple_of((1 - upper if own else upper) * (bins - nfreq), 8)
-        for c in range(chunks):
-            for j in range(parts):
-                out_ref[c, j] = tiles_ref[c, j, pl.ds(start, nfreq)]
-
-    ins = [(place, SMEM), (tiles, VMEM)]
-    return call(body, ins, [((chunks, parts, nfreq, ROWS, LANES), F32)], (0, 0), after=after, name="edge_bin")[0]
-
-
-def edge_row(place, tiles, mask, after=()):
-    chunks, parts, bins = tiles.shape[:3]
-
-    def body(place_ref, tiles_ref, mask_ref, edge_ref):
-        for north in (False, True):
-            c, i = (0, 0) if north else (chunks - 1, ROWS - 1)
-
-            @pl.when((place_ref[0] >= 2) == north)
-            def _():
-                for j in range(parts):
-                    mask = mask_ref[c * ROWS + i : c * ROWS + i + 1, j * LANES : (j + 1) * LANES].astype(F32)
-                    flat = tiles_ref.at[c, j].reshape(bins * ROWS, LANES)
-                    edge_ref[j] = flat[pl.ds(i, bins, stride=ROWS), :] * mask
-
-    ins = [(place, SMEM), (tiles, VMEM), (mask, VMEM)]
-    return call(body, ins, [((parts, bins, LANES), F32)], (0, 0), after=after, name="edge_row")[0]
 
 
 def join(own, received, scale, cut, after=()):
@@ -262,16 +277,20 @@
     return call(body, values, pieces_of(slope.shape, BF16, cut), (0, 0), after=after, name="slope_back")
 
 
-def stencil(place, coef, tiles, near, mask, sign, count, target, extra, chunk, ndir, after=()):
-    chunks, parts, bins = tiles.shape[:3]
+def stencil(place, coef, tiles, near, far, edge, mask, sign, count, target, extra, chunk, ndir, after=()):
+    chunks = len(tiles)
+    parts, bins = tiles[chunk].shape[:2]
     nfreq = bins // ndir
     half = ROWS // 2
     wide = half * LANES
-
-    def body(
-        place_ref, coef_ref, tiles_ref, near_ref, mask_ref, sign_ref, count_ref, target_ref, extra_ref,
-        base_ref, goal_ref, down_ref, up_ref, kept_ref, sems,
-    ):
+    around = {c: tiles[c] for c in range(max(chunk - 1, 0), min(chunk + 2, chunks))}
+    others = [far, edge] if far is not None else []
+
+    def body(place_ref, coef_ref, count_ref, target_ref, extra_ref, mask_ref, sign_ref, *refs):
+        tiles_refs = dict(zip(around, refs))
+        near_refs = refs[len(around) : len(around) + parts]
+        other_refs = refs[len(around) + parts : len(around) + parts + len(others)]
+        base_ref, goal_ref, down_ref, up_ref, kept_ref, sems = refs[len(around) + parts + len(others) :]
         copies = []
         for j in range(parts):
             copy = pltpu.make_async_copy(
@@ -304,10 +323,9 @@
 
             def sector(d, below, above):
                 def group(g, _):
-                    start = pl.multiple_of(d * nfreq + g * 8, 8)
-                    for u in range(8):
-                        b, f = start + u, g * 8 + u
-                        here = [tiles_ref[chunk, j, b] for j in range(parts)]
+                    for u in range(UNROLL):
+                        b, f = d * nfreq + g * UNROLL + u, g * UNROLL + u
+                        here = [tiles_refs[chunk][j, b] for j in range(parts)]
                         field = [here[j] * masks[chunk][j] for j in range(parts)]
                         for j in range(parts):
                             k = j + 1 if east else j - 1
@@ -318,7 +336,7 @@
                                 x = pltpu.roll(jnp.where(lane == LANES - 1, outer, field[j]), 1, 1)
                             outer = 0.0
                             if 0 <= beside < chunks:
-                                outer = tiles_ref[beside, j, b] * masks[beside][j]
+                                outer = tiles_refs[beside][j, b] * masks[beside][j]
                             if north:
                                 y = pltpu.roll(jnp.where(row == 0, outer, field[j]), ROWS - 1, 0)
                             else:
@@ -329,37 +347,38 @@
                             base_ref[j, b] = total * masks[chunk][j]
                     return 0
 
-                lax.fori_loop(0, nfreq // 8, group, 0)
-
-            def far(b, f, j):
-                return jnp.zeros((ROWS, LANES), F32)
-
-            def near(b, f, j):
-                return near_ref[chunk, j, f]
+                lax.fori_loop(0, nfreq // UNROLL, group, 0)
+
+            def far_bin(b, f, j):
+                return other_refs[0][chunk, j, f] if others else jnp.zeros((ROWS, LANES), F32)
+
+            def near_bin(b, f, j):
+                return near_refs[j][f]
 
             def inside(shift):
-                return lambda b, f, j: tiles_ref[chunk, j, b + shift]
-
-            sector(0, near if q % 2 else far, inside(nfreq))
+                return lambda b, f, j: tiles_refs[chunk][j, b + shift]
+
+            sector(0, near_bin if q % 2 else far_bin, inside(nfreq))
 
             def middle(d, _):
                 sector(d, inside(-nfreq), inside(nfreq))
                 return 0
 
             lax.fori_loop(1, ndir - 1, middle, 0)
-            sector(ndir - 1, inside(-nfreq), far if q % 2 else near)
+            sector(ndir - 1, inside(-nfreq), far_bin if q % 2 else near_bin)
 
         for q in range(4):
             pl.when(place == q)(lambda q=q: quadrant(q))
+        if others:
+            blow_in(place, coef_ref, other_refs[1], mask_ref, base_ref, chunk, chunks, ndir)
         for copy in copies:
             copy.wait()
 
     cells = parts * ROWS * LANES
     return call(
         body,
-        [(place, SMEM), (coef, SMEM)]
-        + [(v, VMEM) for v in (tiles, near, mask, sign)]
-        + [(count, SMEM), (target, HBM), (extra, HBM)],
+        [(place, SMEM), (coef, SMEM), (count, SMEM), (target, HBM), (extra, HBM)]
+        + [(v, VMEM) for v in (mask, sign, *around.values(), *near, *others)],
         [
             ((parts, bins, ROWS, LANES), F32),
             ((parts, bins, ROWS, LANES), F32),
@@ -375,6 +394,27 @@
     )
 
 
+def blow_in(place, coef_ref, edge_ref, mask_ref, base_ref, chunk, chunks, ndir):
+    parts, bins = base_ref.shape[:2]
+    nfreq = bins // ndir
+    freq = lax.broadcasted_iota(jnp.int32, (nfreq, LANES), 0).astype(F32)
+    speed = 1.0 / (1.0 + 2.3 * freq / nfreq)
+
+    def blow(i):
+        for j in range(parts):
+            flat = base_ref.at[j].reshape(bins * ROWS, LANES)
+            mask = mask_ref[chunk * ROWS + i : chunk * ROWS + i + 1, j * LANES : (j + 1) * LANES].astype(F32)
+            for d in range(ndir):
+                at = pl.ds(d * nfreq * ROWS + i, nfreq, stride=ROWS)
+                cy = coef_ref[3 * place + 2, d * nfreq] * speed
+                flat[at, :] = flat[at, :] + (mask * cy) * edge_ref[j, d * nfreq : (d + 1) * nfreq, :]
+
+    if chunk == 0:
+        pl.when(place < 2)(lambda: blow(0))
+    if chunk == chunks - 1:
+        pl.when(place >= 2)(lambda: blow(ROWS - 1))
+
+
 def turn_in(place, coef, base, far, edge, mask, sign, chunk, chunks, ndir, after=()):
     parts, bins = base.shape[:2]
     nfreq = bins // ndir
@@ -389,23 +429,7 @@
             share = jnp.where(ahead != upper, 0.3 * mask_ref[at].astype(F32), 0.0)
             bin_edge = pl.ds(start, nfreq)
             out_ref[j, bin_edge] = base_ref[j, bin_edge] + share[None] * far_ref[chunk, j]
-        freq = lax.broadcasted_iota(jnp.int32, (nfreq, LANES), 0).astype(F32)
-        speed = 1.0 / (1.0 + 2.3 * freq / nfreq)
-
-        def blow(i):
-            for j in range(parts):
-                flat = out_ref.at[j].reshape(bins * ROWS, LANES)
-                lanes = slice(j * LANES, (j + 1) * LANES)
-                mask = mask_ref[chunk * ROWS + i : chunk * ROWS + i + 1, lanes].astype(F32)
-                for d in range(ndir):
-                    at = pl.ds(d * nfreq * ROWS + i, nfreq, stride=ROWS)
-                    cy = coef_ref[3 * place + 2, d * nfreq] * speed
-                    flat[at, :] = flat[at, :] + (mask * cy) * edge_ref[j, d * nfreq : (d + 1) * nfreq, :]
-
-        if chunk == 0:
-            pl.when(place < 2)(lambda: blow(0))
-        if chunk == chunks - 1:
-            pl.when(place >= 2)(lambda: blow(ROWS - 1))
+        blow_in(place, coef_ref, edge_ref, mask_ref, out_ref, chunk, chunks, ndir)
 
     ins = [(place, SMEM), (coef, SMEM)] + [(v, VMEM) for v in (base, far, edge, mask, sign)]
     return call(body, ins, [(base.shape, F32)], (0, 0), after=after, aliases={2: 0}, name="turn_in")[0]
@@ -615,41 +639,43 @@
     w_out = jnp.transpose(w_out, (1, 2, 0)).reshape(bins, hidden)
     coef = jnp.asarray(courant(sectors, ndir, nfreq))
 
-    tiles, spec, *send, mask, w_in = encode_first(place_ref, state, sea_mask, w_in, 4)
+    tiles, far, spec, *send = encode_first(place_ref, state, sea_mask, w_in, ndir, 4)
+    mask, w_in = send[-2:]
+    near, send = send[4:-2], send[:4]
     pairs = []
     for s in range(spaces):
         for d in range(sectors):
             to = s - 1 if d >= sectors // 2 else s + 1
             if 0 <= to < spaces:
                 pairs.append((s * sectors + d, to * sectors + d))
-    near = swap(edge_bin(place_ref, tiles, ndir, True).astype(F16), "dir", 1).astype(F32)
+    far = swap(far.astype(F16), "dir", 3).astype(F32)
+
+    def beside(values):
+        return [swap(v.astype(F16), "dir", 1).astype(F32) for v in values]
 
     first = jnp.full((1, spec.shape[1]), PRE_SCALE, F32)
-    specs, chips, crossed = [spec], [], []
-    after = []
+    tiles, near, specs, chips, crossed, stencils = [tiles], [beside(near)], [spec], [], [], []
     for c in range(chunks):
         if c > 0:
-            spec, *send = encode(place_ref, tiles, mask, w_in, c, False, 4, after=after)
+            spec, *send = encode(
+                place_ref, tiles[c], mask, w_in, c, False, 4, after=[far, edge, stencils[0][0]] if c == 1 else after
+            )
             specs.append(spec)
-            after = [spec]
         received = [swap(v, "dir", 1) for v in send]
-        spec, own = encode(place_ref, tiles, mask, w_in, c, True, after=after)
+        spec, own = encode(place_ref, tiles[c], mask, w_in, c, True, after=[spec])
         specs.append(spec)
         chips.append(join([own], received, first, 1))
         crossed.append(cross(chips[c]))
         after = chips[c][:1]
-
-    far = edge_bin(place_ref, tiles, ndir, False, after=chips[0])
-    far = swap(far.astype(F16), "dir", 3).astype(F32)
-    edge = edge_row(place_ref, tiles, mask, after=chips[0])
-    edge = lax.ppermute(edge.astype(F16), ("space", "dir"), pairs).astype(F32)
-
-    stencils = []
-    for c in range(chunks):
+        if c == 0:
+            rest, more, edge = load_rest(place_ref, state, tiles[0], mask, ndir, after=after)
+            tiles += rest
+            near += [beside(v) for v in more]
+            edge = lax.ppermute(edge.astype(F16), ("space", "dir"), pairs).astype(F32)
         stencils.append(
             stencil(
-                place_ref, coef, tiles, near, mask, turn_sign, sea_count, target, [w_out, turn_sign][c % 2], c, ndir,
-                after=[stencils[-1][0]] if c else chips[0],
+                place_ref, coef, tiles, near[c], far if c else None, edge, mask, turn_sign, sea_count, target,
+                [w_out, turn_sign][c % 2], c, ndir, after=after,
             )
         )
     w_out = stencils[0][-1]
@@ -659,8 +685,9 @@
     slopes, nexts, backs, back_crossed = [], [], [], []
     for c in range(chunks):
         base, goal, down, _, _ = stencils[c]
-        base = turn_in(place_ref, coef, base, far, edge, mask, turn_sign, c, chunks, ndir, after=after)
-        hid, slope = activate(chips[c], crossed[c], 4, after=[base])
+        if c == 0:
+            base = turn_in(place_ref, coef, base, far, edge, mask, turn_sign, c, chunks, ndir, after=after)
+        hid, slope = activate(chips[c], crossed[c], 4, after=[base, stencils[-1][0]] if c == 0 else after)
         slopes.append(slope)
         other = [swap(v, "dir", 1) for v in hid]
         own = []

time: 88 us -> 85.6 us (0.973)
  starting transfers between devices: 34.1 us -> 37.6 us
  waiting for transfers between devices: 15.9 us -> 12.7 us
  Pallas kernels: 34.6 us -> 31.5 us
    ppermute x46 -> x49, starting transfers between devices: 30.6 us -> 34.2 us  [swap(): return lax.ppermute(value, axis, [(i, i ^ bit) for i in range(count)])]
    ppermute x46 -> x49, waiting for transfers between devices: 15.9 us -> 12.7 us  [swap(): return lax.ppermute(value, axis, [(i, i ^ bit) for i in range(count)])]
    pallas_call x39 -> x36, Pallas kernels: 34.6 us -> 31.5 us  [call(): pl.pallas_call(run, in_specs=[spec for _, spec in ins] + [ANY] * len(afte...]
  transfers between devices with their start and end apart: 47 -> 50, of which waited for: 17 -> 15; matrix products, arithmetic and copies ran while one was open for 1% -> 2% of each run, Pallas kernels for 34% -> 34%
where the time goes in v4:
time: 85.6 us; the launch traced here: 84.6 us
  starting transfers between devices  37.6 us (44%)
  Pallas kernels  31.5 us (37%)
  waiting for transfers between devices  12.7 us (15%)
  between operations  1.5 us (2%)
  other arithmetic  1.29 us (2%)
    ppermute x49, starting transfers between devices, swap(): return lax.ppermute(value, axis, [(i, i ^ bit) for i in range(count)])  34.2 us
    pallas_call x36, Pallas kernels, call(): pl.pallas_call(run, in_specs=[spec for _, spec in ins] + [ANY] * len(afte...  31.5 us
    ppermute x49, waiting for transfers between devices, swap(): return lax.ppermute(value, axis, [(i, i ^ bit) for i in range(count)])  12.7 us
    ppermute x1, starting transfers between devices, on_device(): edge = lax.ppermute(edge.astype(F16), ('space', 'dir'), pairs).astype(F32)  3.44 us
  transfers between devices with their start and end apart: 50, of which 15 were waited for; matrix products, arithmetic and copies ran while one was open for 2% of the time, Pallas kernels for 34%

profile of v4, /device:TPU:0, one launch (start us, length us, event | category | flops | bytes accessed | tf_op | source)
XLA Modules:
  0.0 84.6 jit_solution(6347304413890619101)
XLA Ops:
  0.6 2.4 %encode_first.1 = (f32[2,288,8,128]{3,2,1,0:T(8,128)S(1)}, f32[2,2,32,8,128]{4,3,2,1,0:T(8,128)S(1)}, bf16[288,1024]{1,0:T(8,128)(2,1)S(1)}, f32[256,256]{1,0:T(...) custom-call(s32[1]{0:T(128)} %bitcast.refs_0_, ...), custom_call_target="tpu_custom_call" | custom-call | tf_op jit(solution)/shard_map/encode_first/pallas_call | solution.py:45
  4.1 2.7 %collective-permute-start.6 = (f16[2,2,32,8,128]{4,3,2,1,0:T(8,128)(2,1)S(1)}, f16[2,2,32,8,128]{4,3,2,1,0:T(8,128)(2,1)S(1)}, u32[]{:S(2)}, u32[]{:S(2)}) collective-permute-start(f16[2,2,32,8,128]{4,3,2,1,0:T(8,128)(2,1)S(1)} %convert_element_type.151), channel_id=1, source_target_pairs={{0,3},{1,2},{2,1},{3,0},{4,7},{5,6},{6,5},{7,4},{8,11},{9,10},{10,... | collective-permute-start | bytes 786440 | tf_op jit(solution)/shard_map/ppermute | solution.py:30
  9.0 1.8 %load_rest.1 = (f32[2,288,8,128]{3,2,1,0:T(8,128)S(1)}, f32[32,8,128]{2,1,0:T(8,128)S(1)}, f32[32,8,128]{2,1,0:T(8,128)S(1)}, f32[2,288,128]{2,1,0:T(8,128)S(1)}) custom-call(s32[1]{0:T(128)} %bitcast.refs_0_, f32[288,16,256]{2,1,0:T(8,128)} %bitcast.13, f32[2,288,8,128]{3,2,1,0:T(8,128)S(1)} %get-tuple-element.86.refs_1_.refs_2_.refs_7_, ...), custom_call_target="tpu_custom_call" | custom-call | tf_op jit(solution)/shard_map/load_rest/pallas_call | solution.py:45
  10.8 3.4 %collective-permute-start.7 = (f16[2,288,128]{2,1,0:T(8,128)(2,1)S(1)}, f16[2,288,128]{2,1,0:T(8,128)(2,1)S(1)}, u32[]{:S(2)}, u32[]{:S(2)}) collective-permute-start(f16[2,288,128]{2,1,0:T(8,128)(2,1)S(1)} %convert_element_type.153), channel_id=1, source_target_pairs={{0,4},{1,5},{4,8},{5,9},{6,2},{7,3},{8,12},{9,13},{10,6},{11,7},{1... | collective-permute-start | bytes 442376 | tf_op jit(solution)/shard_map/ppermute | solution.py:674
  15.9 2.6 %stencil.2 = (f32[2,288,8,128]{3,2,1,0:T(8,128)S(1)}, f32[2,288,8,128]{3,2,1,0:T(8,128)S(1)}, f32[1,1024]{1,0:T(1,128)S(1)}, f32[1,1024]{1,0:T(1,128)S(1)}, bf16[288,256]{1,0:T(8,128)(2,1)S(1)}) custom-call(s32[1]{0:T(128)} %bitcast.refs_0_, f32[12,288]{1,0:T(8,128)S(1)} %copy-done.2, s32[16]{0:T(128)S(1)} %copy-done.3, f32[288,16,256]{2,1,0:T(8,128)} %bitcast.14, ...), custom_call_target="tpu_custom_call" | custom-call | tf_op jit(solution)/shard_map/stencil/pallas_call | solution.py:45
  23.1 3.4 %stencil.3 = (f32[2,288,8,128]{3,2,1,0:T(8,128)S(1)}, f32[2,288,8,128]{3,2,1,0:T(8,128)S(1)}, f32[1,1024]{1,0:T(1,128)S(1)}, f32[1,1024]{1,0:T(1,128)S(1)}, s32[16,256]{1,0:T(8,128)}) custom-call(s32[1]{0:T(128)} %bitcast.refs_0_, f32[12,288]{1,0:T(8,128)S(1)} %copy-done.2, s32[16]{0:T(128)S(1)} %copy-done.3, f32[288,16,256]{2,1,0:T(8,128)} %bitcast.15, ...), custom_call_target="tpu_custom_call" | custom-call | tf_op jit(solution)/shard_map/stencil/pallas_call | solution.py:45
  29.5 1.5 %decode.6 = (f32[2,288,8,128]{3,2,1,0:T(8,128)S(1)}, f32[288,256]{1,0:T(8,128)S(1)}, f32[256,512]{1,0:T(8,128)S(1)}) custom-call(s32[1]{0:T(128)} %bitcast.refs_0_, s32[16]{0:T(128)S(1)} %copy-done.3, bf16[288,256]{1,0:T(8,128)(2,1)S(1)} %get-tuple-element.97.refs_2_, ...), custom_call_target="tpu_custom_call", output_to_operand_aliasing={{0}: (3, {})} | custom-call | tf_op jit(solution)/shard_map/decode/pallas_call | solution.py:45
  31.0 2.3 %decode.7 = (f32[2,288,8,128]{3,2,1,0:T(8,128)S(1)}, f32[288,256]{1,0:T(8,128)S(1)}, f32[256,256]{1,0:T(8,128)S(1)}, f32[256,256]{1,0:T(8,128)S(1)}, f32[256,256]{1,0:T(8,128)S(1)}, /*index=5*/f32[256,256]{1,0:T(8,128)S(1)}) custom-call(s32[1]{0:T(128)} %bitcast.refs_0_, s32[16]{0:T(128)S(1)} %copy-done.3, ...), custom_call_target="tpu_custom_call", output_to_operand_aliasing={{0}: (3, {})} | custom-call | tf_op jit(solution)/shard_map/decode/pallas_call | solution.py:45
  34.4 1.5 %decode.8 = (f32[2,288,8,128]{3,2,1,0:T(8,128)S(1)}, f32[288,256]{1,0:T(8,128)S(1)}, f32[256,512]{1,0:T(8,128)S(1)}) custom-call(s32[1]{0:T(128)} %bitcast.refs_0_, s32[16]{0:T(128)S(1)} %copy-done.3, bf16[288,256]{1,0:T(8,128)(2,1)S(1)} %get-tuple-element.97.refs_2_, ...), custom_call_target="tpu_custom_call", output_to_operand_aliasing={{0}: (3, {})} | custom-call | tf_op jit(solution)/shard_map/decode/pallas_call | solution.py:45
  39.4 1.5 %decode.9 = (f32[2,288,8,128]{3,2,1,0:T(8,128)S(1)}, f32[288,256]{1,0:T(8,128)S(1)}, f32[256,512]{1,0:T(8,128)S(1)}) custom-call(s32[1]{0:T(128)} %bitcast.refs_0_, s32[16]{0:T(128)S(1)} %copy-done.3, bf16[288,256]{1,0:T(8,128)(2,1)S(1)} %get-tuple-element.97.refs_2_, ...), custom_call_target="tpu_custom_call", output_to_operand_aliasing={{0}: (3, {})} | custom-call | tf_op jit(solution)/shard_map/decode/pallas_call | solution.py:45
  40.9 2.3 %decode.10 = (f32[2,288,8,128]{3,2,1,0:T(8,128)S(1)}, f32[288,256]{1,0:T(8,128)S(1)}, f32[256,256]{1,0:T(8,128)S(1)}, f32[256,256]{1,0:T(8,128)S(1)}, f32[256,256]{1,0:T(8,128)S(1)}, /*index=5*/f32[256,256]{1,0:T(8,128)S(1)}) custom-call(s32[1]{0:T(128)} %bitcast.refs_0_, s32[16]{0:T(128)S(1)} %copy-done.3, ...), custom_call_target="tpu_custom_call", output_to_operand_aliasing={{0}: (3, {})} | custom-call | tf_op jit(solution)/shard_map/decode/pallas_call | solution.py:45
  44.2 1.5 %decode.11 = (f32[2,288,8,128]{3,2,1,0:T(8,128)S(1)}, f32[288,256]{1,0:T(8,128)S(1)}, f32[256,512]{1,0:T(8,128)S(1)}) custom-call(s32[1]{0:T(128)} %bitcast.refs_0_, s32[16]{0:T(128)S(1)} %copy-done.3, bf16[288,256]{1,0:T(8,128)(2,1)S(1)} %get-tuple-element.97.refs_2_, ...), custom_call_target="tpu_custom_call", output_to_operand_aliasing={{0}: (3, {})} | custom-call | tf_op jit(solution)/shard_map/decode/pallas_call | solution.py:45
  45.9 1.6 %collective-permute-start.28 = (f16[304,256]{1,0:T(8,128)(2,1)S(1)}, f16[304,256]{1,0:T(8,128)(2,1)S(1)}, u32[]{:S(2)}, u32[]{:S(2)}) collective-permute-start(f16[304,256]{1,0:T(8,128)(2,1)S(1)} %convert_element_type.163), channel_id=1, source_target_pairs={{0,4},{4,0},{8,12},{12,8},{16,20},{20,16},{24,28},{28,24},{1,5},{5... | collective-permute-start | bytes 466952 | tf_op jit(solution)/shard_map/ppermute | solution.py:30
  47.7 1.6 %collective-permute-start.33 = (f16[256,512]{1,0:T(8,128)(2,1)S(1)}, f16[256,512]{1,0:T(8,128)(2,1)S(1)}, u32[]{:S(2)}, u32[]{:S(2)}) collective-permute-start(f16[256,512]{1,0:T(8,128)(2,1)S(1)} %convert_element_type.166), channel_id=1, source_target_pairs={{0,2},{1,3},{2,0},{3,1},{4,6},{5,7},{6,4},{7,5},{8,10},{9,11},{10,... | collective-permute-start | bytes 786440 | tf_op jit(solution)/shard_map/ppermute | solution.py:30
  52.1 2.1 %collective-permute-start.35 = (f16[304,256]{1,0:T(8,128)(2,1)S(1)}, f16[304,256]{1,0:T(8,128)(2,1)S(1)}, u32[]{:S(2)}, u32[]{:S(2)}) collective-permute-start(f16[304,256]{1,0:T(8,128)(2,1)S(1)} %convert_element_type.170), channel_id=1, source_target_pairs={{0,8},{4,12},{8,0},{12,4},{16,24},{20,28},{24,16},{28,20},{1,9},{5... | collective-permute-start | bytes 466952 | tf_op jit(solution)/shard_map/ppermute | solution.py:30
  54.2 2.2 %store.1 = (f32[288,16,256]{2,1,0:T(8,128)}, f32[8,128]{1,0:T(8,128)S(1)}) custom-call(f32[2,288,8,128]{3,2,1,0:T(8,128)S(1)} %get-tuple-element.119.refs_0_, f32[2,288,8,128]{3,2,1,0:T(8,128)S(1)} %get-tuple-element.137.refs_1_, f32[304,256]{1,0:T(8,128)S(1)} %merge.6.refs_2_), custom_call_target="tpu_custom_call" | custom-call | tf_op jit(solution)/shard_map/store/pallas_call | solution.py:45
  57.7 3.2 %collective-permute-start.44 = (f16[416,256]{1,0:T(8,128)(2,1)S(1)}, f16[416,256]{1,0:T(8,128)(2,1)S(1)}, u32[]{:S(2)}, u32[]{:S(2)}) collective-permute-start(f16[416,256]{1,0:T(8,128)(2,1)S(1)} %convert_element_type.178), channel_id=1, source_target_pairs={{0,16},{4,20},{8,24},{12,28},{16,0},{20,4},{24,8},{28,12},{1,17},{... | collective-permute-start | bytes 638984 | tf_op jit(solution)/shard_map/ppermute | solution.py:30
  64.9 2.5 %collective-permute-start.46 = (f16[304,128]{1,0:T(8,128)(2,1)S(1)}, f16[304,128]{1,0:T(8,128)(2,1)S(1)}, u32[]{:S(2)}, u32[]{:S(2)}) collective-permute-start(f16[304,128]{1,0:T(8,128)(2,1)S(1)} %convert_element_type.186), channel_id=1, source_target_pairs={{0,4},{4,0},{8,12},{12,8},{16,20},{20,16},{24,28},{28,24},{1,5},{5... | collective-permute-start | bytes 233480 | tf_op jit(solution)/shard_map/ppermute | solution.py:30
  67.5 1.9 %collective-permute-done.44 = f16[416,256]{1,0:T(8,128)(2,1)S(1)} collective-permute-done((f16[416,256]{1,0:T(8,128)(2,1)S(1)}, f16[416,256]{1,0:T(8,128)(2,1)S(1)}, u32[]{:S(2)}, u32[]{:S(2)}) %collective-permute-start.44) | collective-permute-done | bytes 213024 | tf_op jit(solution)/shard_map/ppermute | solution.py:30
  70.4 1.6 %collective-permute-start.47 = (f16[304,128]{1,0:T(8,128)(2,1)S(1)}, f16[304,128]{1,0:T(8,128)(2,1)S(1)}, u32[]{:S(2)}, u32[]{:S(2)}) collective-permute-start(f16[304,128]{1,0:T(8,128)(2,1)S(1)} %convert_element_type.189), channel_id=1, source_target_pairs={{0,8},{4,12},{8,0},{12,4},{16,24},{20,28},{24,16},{28,20},{1,9},{5... | collective-permute-start | bytes 233480 | tf_op jit(solution)/shard_map/ppermute | solution.py:30
  72.1 1.5 %collective-permute-start.45 = (f16[304,128]{1,0:T(8,128)(2,1)S(1)}, f16[304,128]{1,0:T(8,128)(2,1)S(1)}, u32[]{:S(2)}, u32[]{:S(2)}) collective-permute-start(f16[304,128]{1,0:T(8,128)(2,1)S(1)} %convert_element_type.181), channel_id=1, source_target_pairs={{0,8},{4,12},{8,0},{12,4},{16,24},{20,28},{24,16},{28,20},{1,9},{5... | collective-permute-start | bytes 233480 | tf_op jit(solution)/shard_map/ppermute | solution.py:30
  73.7 1.9 %collective-permute-done.47 = f16[304,128]{1,0:T(8,128)(2,1)S(1)} collective-permute-done((f16[304,128]{1,0:T(8,128)(2,1)S(1)}, f16[304,128]{1,0:T(8,128)(2,1)S(1)}, u32[]{:S(2)}, u32[]{:S(2)}) %collective-permute-start.47) | collective-permute-done | bytes 77856 | tf_op jit(solution)/shard_map/ppermute | solution.py:30
  75.6 2.5 %collective-permute-start.49 = (f16[304,128]{1,0:T(8,128)(2,1)S(1)}, f16[304,128]{1,0:T(8,128)(2,1)S(1)}, u32[]{:S(2)}, u32[]{:S(2)}) collective-permute-start(f16[304,128]{1,0:T(8,128)(2,1)S(1)} %convert_element_type.192), channel_id=1, source_target_pairs={{0,16},{4,20},{8,24},{12,28},{16,0},{20,4},{24,8},{28,12},{1,17},{... | collective-permute-start | bytes 233480 | tf_op jit(solution)/shard_map/ppermute | solution.py:30
  79.7 3.3 %collective-permute-done.49 = f16[304,128]{1,0:T(8,128)(2,1)S(1)} collective-permute-done((f16[304,128]{1,0:T(8,128)(2,1)S(1)}, f16[304,128]{1,0:T(8,128)(2,1)S(1)}, u32[]{:S(2)}, u32[]{:S(2)}) %collective-permute-start.49) | collective-permute-done | bytes 77856 | tf_op jit(solution)/shard_map/ppermute | solution.py:30
  (170 shorter events, 30.5 us)
Async XLA Ops:
  3.0 4.4 %collective-permute-start = (f32[256,256]{1,0:T(8,128)S(1)}, f32[256,256]{1,0:T(8,128)S(1)}, u32[]{:S(2)}, u32[]{:S(2)}) collective-permute-start(f32[256,256]{1,0:T(8,128)S(1)} %get-tuple-element.90), channel_id=1, source_target_pairs={{0,1},{1,0},{2,3},{3,2},{4,5},{5,4},{6,7},{7,6},{8,9},{9,8},{10,11... | collective-permute-start | bytes 786440 | tf_op jit(solution)/shard_map/ppermute | solution.py:30
  3.5 3.9 %collective-permute-start.1 = (f32[256,256]{1,0:T(8,128)S(1)}, f32[256,256]{1,0:T(8,128)S(1)}, u32[]{:S(2)}, u32[]{:S(2)}) collective-permute-start(f32[256,256]{1,0:T(8,128)S(1)} %get-tuple-element.91), channel_id=1, source_target_pairs={{0,1},{1,0},{2,3},{3,2},{4,5},{5,4},{6,7},{7,6},{8,9},{9,8},{10,11... | collective-permute-start | bytes 786440 | tf_op jit(solution)/shard_map/ppermute | solution.py:30
  3.6 3.8 %collective-permute-start.2 = (f32[256,256]{1,0:T(8,128)S(1)}, f32[256,256]{1,0:T(8,128)S(1)}, u32[]{:S(2)}, u32[]{:S(2)}) collective-permute-start(f32[256,256]{1,0:T(8,128)S(1)} %get-tuple-element.92), channel_id=1, source_target_pairs={{0,1},{1,0},{2,3},{3,2},{4,5},{5,4},{6,7},{7,6},{8,9},{9,8},{10,11... | collective-permute-start | bytes 786440 | tf_op jit(solution)/shard_map/ppermute | solution.py:30
  4.1 14.4 %collective-permute-start.6 = (f16[2,2,32,8,128]{4,3,2,1,0:T(8,128)(2,1)S(1)}, f16[2,2,32,8,128]{4,3,2,1,0:T(8,128)(2,1)S(1)}, u32[]{:S(2)}, u32[]{:S(2)}) collective-permute-start(f16[2,2,32,8,128]{4,3,2,1,0:T(8,128)(2,1)S(1)} %convert_element_type.151), channel_id=1, source_target_pairs={{0,3},{1,2},{2,1},{3,0},{4,7},{5,6},{6,5},{7,4},{8,11},{9,10},{10,... | collective-permute-start | bytes 786440 | tf_op jit(solution)/shard_map/ppermute | solution.py:30
  7.7 20.1 %collective-permute-start.14 = (f16[256,1024]{1,0:T(8,128)(2,1)S(1)}, f16[256,1024]{1,0:T(8,128)(2,1)S(1)}, u32[]{:S(2)}, u32[]{:S(2)}) collective-permute-start(f16[256,1024]{1,0:T(8,128)(2,1)S(1)} %convert_element_type.159), channel_id=1, source_target_pairs={{0,2},{1,3},{2,0},{3,1},{4,6},{5,7},{6,4},{7,5},{8,10},{9,11},{10,... | collective-permute-start | bytes 1572872 | tf_op jit(solution)/shard_map/ppermute | solution.py:30
  10.8 7.8 %collective-permute-start.7 = (f16[2,288,128]{2,1,0:T(8,128)(2,1)S(1)}, f16[2,288,128]{2,1,0:T(8,128)(2,1)S(1)}, u32[]{:S(2)}, u32[]{:S(2)}) collective-permute-start(f16[2,288,128]{2,1,0:T(8,128)(2,1)S(1)} %convert_element_type.153), channel_id=1, source_target_pairs={{0,4},{1,5},{4,8},{5,9},{6,2},{7,3},{8,12},{9,13},{10,6},{11,7},{1... | collective-permute-start | bytes 442376 | tf_op jit(solution)/shard_map/ppermute | solution.py:674
  22.3 15.3 %collective-permute-start.19 = (f16[256,1024]{1,0:T(8,128)(2,1)S(1)}, f16[256,1024]{1,0:T(8,128)(2,1)S(1)}, u32[]{:S(2)}, u32[]{:S(2)}) collective-permute-start(f16[256,1024]{1,0:T(8,128)(2,1)S(1)} %convert_element_type.161), channel_id=1, source_target_pairs={{0,2},{1,3},{2,0},{3,1},{4,6},{5,7},{6,4},{7,5},{8,10},{9,11},{10,... | collective-permute-start | bytes 1572872 | tf_op jit(solution)/shard_map/ppermute | solution.py:30
  36.2 14.1 %collective-permute-start.36 = (f16[256,1024]{1,0:T(8,128)(2,1)S(1)}, f16[256,1024]{1,0:T(8,128)(2,1)S(1)}, u32[]{:S(2)}, u32[]{:S(2)}) collective-permute-start(f16[256,1024]{1,0:T(8,128)(2,1)S(1)} %convert_element_type.173), channel_id=1, source_target_pairs={{0,2},{1,3},{2,0},{3,1},{4,6},{5,7},{6,4},{7,5},{8,10},{9,11},{10,... | collective-permute-start | bytes 1572872 | tf_op jit(solution)/shard_map/ppermute | solution.py:30
  43.3 4.2 %collective-permute-start.30 = (f32[256,256]{1,0:T(8,128)S(1)}, f32[256,256]{1,0:T(8,128)S(1)}, u32[]{:S(2)}, u32[]{:S(2)}) collective-permute-start(f32[256,256]{1,0:T(8,128)S(1)} %get-tuple-element.146), channel_id=1, source_target_pairs={{0,1},{1,0},{2,3},{3,2},{4,5},{5,4},{6,7},{7,6},{8,9},{9,8},{10,11... | collective-permute-start | bytes 786440 | tf_op jit(solution)/shard_map/ppermute | solution.py:30
  43.7 3.8 %collective-permute-start.31 = (f32[256,256]{1,0:T(8,128)S(1)}, f32[256,256]{1,0:T(8,128)S(1)}, u32[]{:S(2)}, u32[]{:S(2)}) collective-permute-start(f32[256,256]{1,0:T(8,128)S(1)} %get-tuple-element.147), channel_id=1, source_target_pairs={{0,1},{1,0},{2,3},{3,2},{4,5},{5,4},{6,7},{7,6},{8,9},{9,8},{10,11... | collective-permute-start | bytes 786440 | tf_op jit(solution)/shard_map/ppermute | solution.py:30
  43.8 3.7 %collective-permute-start.32 = (f32[256,256]{1,0:T(8,128)S(1)}, f32[256,256]{1,0:T(8,128)S(1)}, u32[]{:S(2)}, u32[]{:S(2)}) collective-permute-start(f32[256,256]{1,0:T(8,128)S(1)} %get-tuple-element.148), channel_id=1, source_target_pairs={{0,1},{1,0},{2,3},{3,2},{4,5},{5,4},{6,7},{7,6},{8,9},{9,8},{10,11... | collective-permute-start | bytes 786440 | tf_op jit(solution)/shard_map/ppermute | solution.py:30
  45.9 6.1 %collective-permute-start.28 = (f16[304,256]{1,0:T(8,128)(2,1)S(1)}, f16[304,256]{1,0:T(8,128)(2,1)S(1)}, u32[]{:S(2)}, u32[]{:S(2)}) collective-permute-start(f16[304,256]{1,0:T(8,128)(2,1)S(1)} %convert_element_type.163), channel_id=1, source_target_pairs={{0,4},{4,0},{8,12},{12,8},{16,20},{20,16},{24,28},{28,24},{1,5},{5... | collective-permute-start | bytes 466952 | tf_op jit(solution)/shard_map/ppermute | solution.py:30
  47.7 13.5 %collective-permute-start.33 = (f16[256,512]{1,0:T(8,128)(2,1)S(1)}, f16[256,512]{1,0:T(8,128)(2,1)S(1)}, u32[]{:S(2)}, u32[]{:S(2)}) collective-permute-start(f16[256,512]{1,0:T(8,128)(2,1)S(1)} %convert_element_type.166), channel_id=1, source_target_pairs={{0,2},{1,3},{2,0},{3,1},{4,6},{5,7},{6,4},{7,5},{8,10},{9,11},{10,... | collective-permute-start | bytes 786440 | tf_op jit(solution)/shard_map/ppermute | solution.py:30
  49.4 12.1 %collective-permute-start.34 = (f16[256,512]{1,0:T(8,128)(2,1)S(1)}, f16[256,512]{1,0:T(8,128)(2,1)S(1)}, u32[]{:S(2)}, u32[]{:S(2)}) collective-permute-start(f16[256,512]{1,0:T(8,128)(2,1)S(1)} %convert_element_type.168), channel_id=1, source_target_pairs={{0,2},{1,3},{2,0},{3,1},{4,6},{5,7},{6,4},{7,5},{8,10},{9,11},{10,... | collective-permute-start | bytes 786440 | tf_op jit(solution)/shard_map/ppermute | solution.py:30
  50.7 10.9 %collective-permute-start.37 = (bf16[256,512]{1,0:T(8,128)(2,1)S(1)}, bf16[256,512]{1,0:T(8,128)(2,1)S(1)}, u32[]{:S(2)}, u32[]{:S(2)}) collective-permute-start(bf16[256,512]{1,0:T(8,128)(2,1)S(1)} %get-tuple-element.154.refs_1_), channel_id=1, source_target_pairs={{0,1},{1,0},{2,3},{3,2},{4,5},{5,4},{6,7},{7,6},{8,9},{9,8},{10,11... | collective-permute-start | bytes 786440 | tf_op jit(solution)/shard_map/ppermute | solution.py:30
  50.8 10.8 %collective-permute-start.38 = (bf16[256,512]{1,0:T(8,128)(2,1)S(1)}, bf16[256,512]{1,0:T(8,128)(2,1)S(1)}, u32[]{:S(2)}, u32[]{:S(2)}) collective-permute-start(bf16[256,512]{1,0:T(8,128)(2,1)S(1)} %get-tuple-element.155.refs_2_), channel_id=1, source_target_pairs={{0,1},{1,0},{2,3},{3,2},{4,5},{5,4},{6,7},{7,6},{8,9},{9,8},{10,11... | collective-permute-start | bytes 786440 | tf_op jit(solution)/shard_map/ppermute | solution.py:30
  52.1 5.5 %collective-permute-start.35 = (f16[304,256]{1,0:T(8,128)(2,1)S(1)}, f16[304,256]{1,0:T(8,128)(2,1)S(1)}, u32[]{:S(2)}, u32[]{:S(2)}) collective-permute-start(f16[304,256]{1,0:T(8,128)(2,1)S(1)} %convert_element_type.170), channel_id=1, source_target_pairs={{0,8},{4,12},{8,0},{12,4},{16,24},{20,28},{24,16},{28,20},{1,9},{5... | collective-permute-start | bytes 466952 | tf_op jit(solution)/shard_map/ppermute | solution.py:30
  57.7 11.8 %collective-permute-start.44 = (f16[416,256]{1,0:T(8,128)(2,1)S(1)}, f16[416,256]{1,0:T(8,128)(2,1)S(1)}, u32[]{:S(2)}, u32[]{:S(2)}) collective-permute-start(f16[416,256]{1,0:T(8,128)(2,1)S(1)} %convert_element_type.178), channel_id=1, source_target_pairs={{0,16},{4,20},{8,24},{12,28},{16,0},{20,4},{24,8},{28,12},{1,17},{... | collective-permute-start | bytes 638984 | tf_op jit(solution)/shard_map/ppermute | solution.py:30
  64.9 5.4 %collective-permute-start.46 = (f16[304,128]{1,0:T(8,128)(2,1)S(1)}, f16[304,128]{1,0:T(8,128)(2,1)S(1)}, u32[]{:S(2)}, u32[]{:S(2)}) collective-permute-start(f16[304,128]{1,0:T(8,128)(2,1)S(1)} %convert_element_type.186), channel_id=1, source_target_pairs={{0,4},{4,0},{8,12},{12,8},{16,20},{20,16},{24,28},{28,24},{1,5},{5... | collective-permute-start | bytes 233480 | tf_op jit(solution)/shard_map/ppermute | solution.py:30
  67.4 4.6 %collective-permute-start.43 = (f16[304,128]{1,0:T(8,128)(2,1)S(1)}, f16[304,128]{1,0:T(8,128)(2,1)S(1)}, u32[]{:S(2)}, u32[]{:S(2)}) collective-permute-start(f16[304,128]{1,0:T(8,128)(2,1)S(1)} %convert_element_type.175), channel_id=1, source_target_pairs={{0,4},{4,0},{8,12},{12,8},{16,20},{20,16},{24,28},{28,24},{1,5},{5... | collective-permute-start | bytes 233480 | tf_op jit(solution)/shard_map/ppermute | solution.py:30
  70.4 5.1 %collective-permute-start.47 = (f16[304,128]{1,0:T(8,128)(2,1)S(1)}, f16[304,128]{1,0:T(8,128)(2,1)S(1)}, u32[]{:S(2)}, u32[]{:S(2)}) collective-permute-start(f16[304,128]{1,0:T(8,128)(2,1)S(1)} %convert_element_type.189), channel_id=1, source_target_pairs={{0,8},{4,12},{8,0},{12,4},{16,24},{20,28},{24,16},{28,20},{1,9},{5... | collective-permute-start | bytes 233480 | tf_op jit(solution)/shard_map/ppermute | solution.py:30
  72.1 6.0 %collective-permute-start.45 = (f16[304,128]{1,0:T(8,128)(2,1)S(1)}, f16[304,128]{1,0:T(8,128)(2,1)S(1)}, u32[]{:S(2)}, u32[]{:S(2)}) collective-permute-start(f16[304,128]{1,0:T(8,128)(2,1)S(1)} %convert_element_type.181), channel_id=1, source_target_pairs={{0,8},{4,12},{8,0},{12,4},{16,24},{20,28},{24,16},{28,20},{1,9},{5... | collective-permute-start | bytes 233480 | tf_op jit(solution)/shard_map/ppermute | solution.py:30
  75.6 7.3 %collective-permute-start.49 = (f16[304,128]{1,0:T(8,128)(2,1)S(1)}, f16[304,128]{1,0:T(8,128)(2,1)S(1)}, u32[]{:S(2)}, u32[]{:S(2)}) collective-permute-start(f16[304,128]{1,0:T(8,128)(2,1)S(1)} %convert_element_type.192), channel_id=1, source_target_pairs={{0,16},{4,20},{8,24},{12,28},{16,0},{20,4},{24,8},{28,12},{1,17},{... | collective-permute-start | bytes 233480 | tf_op jit(solution)/shard_map/ppermute | solution.py:30
  78.2 5.6 %collective-permute-start.48 = (f16[304,128]{1,0:T(8,128)(2,1)S(1)}, f16[304,128]{1,0:T(8,128)(2,1)S(1)}, u32[]{:S(2)}, u32[]{:S(2)}) collective-permute-start(f16[304,128]{1,0:T(8,128)(2,1)S(1)} %convert_element_type.184), channel_id=1, source_target_pairs={{0,16},{4,20},{8,24},{12,28},{16,0},{20,4},{24,8},{28,12},{1,17},{... | collective-permute-start | bytes 233480 | tf_op jit(solution)/shard_map/ppermute | solution.py:30
  (30 other events, 81.2 us)

commit v5 on v4

--- a/solution.py
+++ b/solution.py
@@ -373,6 +373,8 @@
             blow_in(place, coef_ref, other_refs[1], mask_ref, base_ref, chunk, chunks, ndir)
         for copy in copies:
             copy.wait()
+        if far is not None:
+            subtract(base_ref, goal_ref, goal_ref, nfreq)
 
     cells = parts * ROWS * LANES
     return call(
@@ -415,11 +417,23 @@
         pl.when(place >= 2)(lambda: blow(ROWS - 1))
 
 
-def turn_in(place, coef, base, far, edge, mask, sign, chunk, chunks, ndir, after=()):
+def subtract(base_ref, goal_ref, out_ref, nfreq):
+    parts, bins = base_ref.shape[:2]
+
+    def group(g, _):
+        at = pl.ds(g * nfreq, nfreq)
+        for j in range(parts):
+            out_ref[j, at] = base_ref[j, at] - goal_ref[j, at]
+        return 0
+
+    lax.fori_loop(0, bins // nfreq, group, 0)
+
+
+def turn_in(place, coef, base, goal, far, edge, mask, sign, chunk, chunks, ndir, after=()):
     parts, bins = base.shape[:2]
     nfreq = bins // ndir
 
-    def body(place_ref, coef_ref, base_ref, far_ref, edge_ref, mask_ref, sign_ref, out_ref):
+    def body(place_ref, coef_ref, base_ref, goal_ref, far_ref, edge_ref, mask_ref, sign_ref, out_ref, less_ref):
         place = place_ref[0]
         upper = place % 2
         start = pl.multiple_of(upper * (bins - nfreq), 8)
@@ -431,28 +445,29 @@
             out_ref[j, bin_edge] = base_ref[j, bin_edge] + share[None] * far_ref[chunk, j]
         blow_in(place, coef_ref, edge_ref, mask_ref, out_ref, chunk, chunks, ndir)
 
-    ins = [(place, SMEM), (coef, SMEM)] + [(v, VMEM) for v in (base, far, edge, mask, sign)]
-    return call(body, ins, [(base.shape, F32)], (0, 0), after=after, aliases={2: 0}, name="turn_in")[0]
-
-
-def decode(place, hid, w_out, base, goal, mask, count, seed, chunk, own, which, cut=1, after=()):
-    bins = base.shape[1]
+        subtract(out_ref, goal_ref, less_ref, nfreq)
+
+    ins = [(place, SMEM), (coef, SMEM)] + [(v, VMEM) for v in (base, goal, far, edge, mask, sign)]
+    outs = [(base.shape, F32), (base.shape, F32)]
+    return call(body, ins, outs, (0, 0), after=after, aliases={2: 0, 3: 1}, name="turn_in")
+
+
+def decode(place, hid, w_out, less, mask, count, seed, chunk, own, which, cut=1, after=()):
+    bins = less.shape[1]
     hidden = w_out.shape[1]
     half = ROWS // 2
     wide = half * LANES
     cells = len(which) * wide
     seeds = [seed] if seed is not None else []
 
-    def body(place_ref, count_ref, w_ref, base_ref, goal_ref, mask_ref, *refs):
+    def body(place_ref, count_ref, w_ref, less_ref, mask_ref, *refs):
         hid_refs, refs = refs[: len(hid)], refs[len(hid) :]
         next_ref, grad_ref, *out_refs, back_ref = refs[len(seeds) :]
         core = place_ref[0] % 2
         first = first_row(core, own)
         total = refs[0][...] if seeds else jnp.zeros(grad_ref.shape, F32)
         for k, j in enumerate(which):
-            base = base_ref.at[j].reshape(bins * ROWS, LANES)
-            goal = goal_ref.at[j].reshape(bins * ROWS, LANES)
-            result = next_ref.at[j].reshape(bins * ROWS, LANES)
+            rest = less_ref.at[j].reshape(bins * ROWS, LANES)
             units = read_columns(hid_refs, j * wide, wide)
             source = jnp.dot(w_ref[...], units, preferred_element_type=F32)
             for i in range(half):
@@ -460,9 +475,9 @@
                 mask = pick(mask_ref, core, own, chunk, i, j)
                 weight = (1.0 / count_of(count_ref, core, own, chunk, i)) * mask
                 part = source[:, i * LANES : (i + 1) * LANES]
-                new = base[at, :] + (0.5 * mask) * part
-                result[at, :] = new
-                back_ref[:, i * LANES : (i + 1) * LANES] = (weight * (new - goal[at, :])).astype(BF16)
+                new = (0.5 * mask) * part
+                next_ref[:, k * wide + i * LANES : k * wide + (i + 1) * LANES] = new
+                back_ref[:, i * LANES : (i + 1) * LANES] = (weight * (rest[at, :] + new)).astype(BF16)
             back = back_ref[...]
             total = total + lax.dot_general(back, units, (((1,), (1,)), ((), ())), preferred_element_type=F32)
             out = lax.dot_general(w_ref[...], back, (((0,), (0,)), ((), ())), preferred_element_type=F32)
@@ -471,51 +486,49 @@
 
     return call(
         body,
-        [(place, SMEM), (count, SMEM)] + [(v, VMEM) for v in (w_out, base, goal, mask, *hid, *seeds)],
-        [(base.shape, F32), ((bins, hidden), F32)]
-        + pieces_of((hidden, cells), F32, cut),
+        [(place, SMEM), (count, SMEM)] + [(v, VMEM) for v in (w_out, less, mask, *hid, *seeds)],
+        [((bins, cells), F32), ((bins, hidden), F32)] + pieces_of((hidden, cells), F32, cut),
         (6 * bins * hidden * cells, 12 * bins * cells),
         scratch=[pltpu.VMEM((bins, wide), BF16)],
-        aliases={3: 0},
         after=after,
         name="decode",
     )
 
 
-def store(nexts, rows, after=()):
-    parts, bins = nexts[0].shape[:2]
-    n = len(nexts)
-
-    def body(*refs):
+def store(place, base, own, other, chunk, rows, before=None, after=()):
+    bins = other.shape[0]
+    half = ROWS // 2
+    parts = other.shape[1] // (half * LANES)
+    n = len(own)
+    held = [before] if before is not None else []
+
+    def body(place_ref, base_ref, other_ref, *refs):
+        own_refs, (out_ref, done_ref, tiles_ref, sems) = refs[:n], refs[n + len(held) :]
+        core = place_ref[0] % 2
         copies = []
-        for c in range(n):
-            for j in range(parts):
-                to = refs[n].at[:, pl.ds(c * ROWS, ROWS), pl.ds(j * LANES, LANES)]
-                copies.append(pltpu.make_async_copy(refs[c].at[j], to, refs[n + 2].at[c * parts + j]))
-        for copy in copies:
-            copy.start()
-        refs[n + 1][...] = jnp.zeros(refs[n + 1].shape, F32)
+        for j in range(parts):
+            flat = tiles_ref.at[j].reshape(bins * ROWS, LANES)
+            base = base_ref.at[j].reshape(bins * ROWS, LANES)
+            for mine, values in ((True, own_refs), (False, [other_ref])):
+                for i in range(half):
+                    at = pl.ds(first_row(core, mine) + i, bins, stride=ROWS)
+                    flat[at, :] = base[at, :] + read_columns(values, (j * half + i) * LANES, LANES)
+            copies.append(pltpu.make_async_copy(tiles_ref.at[j], block(out_ref, chunk, j), sems.at[j]))
+            copies[j].start()
+        done_ref[...] = jnp.zeros(done_ref.shape, F32)
         for copy in copies:
             copy.wait()
 
-    size = bins * rows * parts * LANES
     return call(
         body,
-        [(v, VMEM) for v in nexts],
+        [(place, SMEM), (base, VMEM), (other, VMEM)] + [(v, VMEM) for v in own] + [(v, HBM) for v in held],
         [((bins, rows, parts * LANES), F32, HBM), ((ROWS, LANES), F32)],
-        (0, 8 * size),
-        scratch=[pltpu.SemaphoreType.DMA((n * parts,))],
+        (0, 0),
+        scratch=[pltpu.VMEM((parts, bins, ROWS, LANES), F32), pltpu.SemaphoreType.DMA((parts,))],
+        aliases={3 + n: 0} if held else None,
         after=after,
         name="store",
     )
-
-
-def write_packed(ref, total):
-    n = total.shape[0]
-    most = jnp.max(jnp.max(jnp.abs(total), axis=1, keepdims=True), axis=0, keepdims=True)
-    power = jnp.ceil(jnp.log2(jnp.maximum(most, 2.0**-100)))
-    ref[0:n, :] = total
-    ref[n:, :] = jnp.broadcast_to(power, (POWER_ROWS, total.shape[1]))
 
 
 def write_scaled(refs, total, power):
@@ -672,35 +685,45 @@
             tiles += rest
             near += [beside(v) for v in more]
             edge = lax.ppermute(edge.astype(F16), ("space", "dir"), pairs).astype(F32)
-        stencils.append(
-            stencil(
-                place_ref, coef, tiles, near[c], far if c else None, edge, mask, turn_sign, sea_count, target,
-                [w_out, turn_sign][c % 2], c, ndir, after=after,
-            )
-        )
+            stencils = [
+                stencil(
+                    place_ref, coef, tiles, near[0], None, edge, mask, turn_sign, sea_count, target, w_out, 0, ndir,
+                    after=after,
+                )
+            ]
     w_out = stencils[0][-1]
-    after = [stencils[-1][0]]
+    after = [*chips[-1], *[v for values in near[1:] for v in values]]
 
     grad_out = None
     slopes, nexts, backs, back_crossed = [], [], [], []
     for c in range(chunks):
+        if c > 0:
+            stencils.append(
+                stencil(
+                    place_ref, coef, tiles, near[c], far, edge, mask, turn_sign, sea_count, target, turn_sign, c,
+                    ndir, after=after,
+                )
+            )
+            after = stencils[c][:1]
         base, goal, down, _, _ = stencils[c]
         if c == 0:
-            base = turn_in(place_ref, coef, base, far, edge, mask, turn_sign, c, chunks, ndir, after=after)
-        hid, slope = activate(chips[c], crossed[c], 4, after=[base, stencils[-1][0]] if c == 0 else after)
+            base, goal = turn_in(place_ref, coef, base, goal, far, edge, mask, turn_sign, c, chunks, ndir, after=after)
+        hid, slope = activate(chips[c], crossed[c], 4, after=[base, goal] if c == 0 else after)
         slopes.append(slope)
         other = [swap(v, "dir", 1) for v in hid]
-        own = []
+        own, own_new = [], []
         for mine, which in ((True, range(1)), (False, range(parts)), (True, range(1, parts))):
-            base, grad_out, *out = decode(
-                place_ref, hid if mine else other, w_out, base, goal, mask, sea_count, grad_out, c, mine, which,
+            new, grad_out, *out = decode(
+                place_ref, hid if mine else other, w_out, goal, mask, sea_count, grad_out, c, mine, which,
                 cut=len(which) if mine else 4,
             )
             if mine:
                 own += out
+                own_new.append(new)
             else:
                 received = [swap(v, "dir", 1) for v in out]
-        nexts.append(base)
+                other_new = new
+        nexts.append((base, own_new, other_new))
         backs.append(join(own, received, down, 2 if c + 1 == chunks else 1))
         back_crossed.append(cross(backs[c]))
         after = backs[c][:1]
@@ -708,7 +731,7 @@
     out_sum = space_sum(pack(grad_out, 1), 112)
     next(out_sum)
     merged = out_sum.send(())
-    next_state, stored = store(nexts, rows, after=[merged])
+    next_state, stored = store(place_ref, *nexts[0], 0, rows, after=[merged])
 
     grad_in = None
     after = []
@@ -734,8 +757,11 @@
     in_sum = space_sum(grad_in)
     next(in_sum)
     merged = in_sum.send([summed])
+    for c in range(1, chunks):
+        next_state, stored = store(place_ref, *nexts[c], c, rows, next_state, after=[merged])
+    waits = [stored]
     while not isinstance(merged, (tuple, list)):
-        merged = in_sum.send(())
+        merged, waits = in_sum.send(waits), ()
     grad_in = merged[0]
     return (
         next_state.reshape(ndir, nfreq, rows, lon),

time: 85.6 us -> 85.2 us (level)
  waiting for transfers between devices: 12.7 us -> 13.9 us
    ppermute x49, waiting for transfers between devices: 12.7 us -> 13.9 us  [swap(): return lax.ppermute(value, axis, [(i, i ^ bit) for i in range(count)])]
    pallas_call x36 -> x37, Pallas kernels: 31.5 us -> 30.8 us  [call(): pl.pallas_call(run, in_specs=[spec for _, spec in ins] + [ANY] * len(afte...]
  transfers between devices with their start and end apart: 50 -> 50, of which waited for: 15 -> 17; matrix products, arithmetic and copies ran while one was open for 2% -> 2% of each run, Pallas kernels for 34% -> 33%
where the time goes in v5:
time: 85.2 us; the launch traced here: 85 us
  starting transfers between devices  37.4 us (44%)
  Pallas kernels  30.8 us (36%)
  waiting for transfers between devices  13.9 us (16%)
  between operations  1.5 us (2%)
  other arithmetic  1.29 us (2%)
    ppermute x49, starting transfers between devices, swap(): return lax.ppermute(value, axis, [(i, i ^ bit) for i in range(count)])  34 us
    pallas_call x37, Pallas kernels, call(): pl.pallas_call(run, in_specs=[spec for _, spec in ins] + [ANY] * len(afte...  30.8 us
    ppermute x49, waiting for transfers between devices, swap(): return lax.ppermute(value, axis, [(i, i ^ bit) for i in range(count)])  13.9 us
    ppermute x1, starting transfers between devices, on_device(): edge = lax.ppermute(edge.astype(F16), ('space', 'dir'), pairs).astype(F32)  3.44 us
  transfers between devices with their start and end apart: 50, of which 17 were waited for; matrix products, arithmetic and copies ran while one was open for 2% of the time, Pallas kernels for 33%

profile of v5, /device:TPU:0, one launch (start us, length us, event | category | flops | bytes accessed | tf_op | source)
XLA Modules:
  0.0 85.0 jit_solution(10848268323318437194)
XLA Ops:
  0.6 2.4 %encode_first.1 = (f32[2,288,8,128]{3,2,1,0:T(8,128)S(1)}, f32[2,2,32,8,128]{4,3,2,1,0:T(8,128)S(1)}, bf16[288,1024]{1,0:T(8,128)(2,1)S(1)}, f32[256,256]{1,0:T(...) custom-call(s32[1]{0:T(128)} %bitcast.refs_0_, ...), custom_call_target="tpu_custom_call" | custom-call | tf_op jit(solution)/shard_map/encode_first/pallas_call | solution.py:45
  4.1 2.7 %collective-permute-start.6 = (f16[2,2,32,8,128]{4,3,2,1,0:T(8,128)(2,1)S(1)}, f16[2,2,32,8,128]{4,3,2,1,0:T(8,128)(2,1)S(1)}, u32[]{:S(2)}, u32[]{:S(2)}) collective-permute-start(f16[2,2,32,8,128]{4,3,2,1,0:T(8,128)(2,1)S(1)} %convert_element_type.151), channel_id=1, source_target_pairs={{0,3},{1,2},{2,1},{3,0},{4,7},{5,6},{6,5},{7,4},{8,11},{9,10},{10,... | collective-permute-start | bytes 786440 | tf_op jit(solution)/shard_map/ppermute | solution.py:30
  9.0 1.8 %load_rest.1 = (f32[2,288,8,128]{3,2,1,0:T(8,128)S(1)}, f32[32,8,128]{2,1,0:T(8,128)S(1)}, f32[32,8,128]{2,1,0:T(8,128)S(1)}, f32[2,288,128]{2,1,0:T(8,128)S(1)}) custom-call(s32[1]{0:T(128)} %bitcast.refs_0_, f32[288,16,256]{2,1,0:T(8,128)} %bitcast.13, f32[2,288,8,128]{3,2,1,0:T(8,128)S(1)} %get-tuple-element.90.refs_1_.refs_2_.refs_7_, ...), custom_call_target="tpu_custom_call" | custom-call | tf_op jit(solution)/shard_map/load_rest/pallas_call | solution.py:45
  10.8 3.4 %collective-permute-start.7 = (f16[2,288,128]{2,1,0:T(8,128)(2,1)S(1)}, f16[2,288,128]{2,1,0:T(8,128)(2,1)S(1)}, u32[]{:S(2)}, u32[]{:S(2)}) collective-permute-start(f16[2,288,128]{2,1,0:T(8,128)(2,1)S(1)} %convert_element_type.153), channel_id=1, source_target_pairs={{0,4},{1,5},{4,8},{5,9},{6,2},{7,3},{8,12},{9,13},{10,6},{11,7},{1... | collective-permute-start | bytes 442376 | tf_op jit(solution)/shard_map/ppermute | solution.py:687
  15.9 2.6 %stencil.2 = (f32[2,288,8,128]{3,2,1,0:T(8,128)S(1)}, f32[2,288,8,128]{3,2,1,0:T(8,128)S(1)}, f32[1,1024]{1,0:T(1,128)S(1)}, f32[1,1024]{1,0:T(1,128)S(1)}, bf16[288,256]{1,0:T(8,128)(2,1)S(1)}) custom-call(s32[1]{0:T(128)} %bitcast.refs_0_, f32[12,288]{1,0:T(8,128)S(1)} %copy-done.1, s32[16]{0:T(128)S(1)} %copy-done.2, f32[288,16,256]{2,1,0:T(8,128)} %bitcast.14, ...), custom_call_target="tpu_custom_call" | custom-call | tf_op jit(solution)/shard_map/stencil/pallas_call | solution.py:45
  23.1 1.4 %turn_in.1 = (f32[2,288,8,128]{3,2,1,0:T(8,128)S(1)}, f32[2,288,8,128]{3,2,1,0:T(8,128)S(1)}) custom-call(s32[1]{0:T(128)} %bitcast.refs_0_, f32[12,288]{1,0:T(8,128)S(1)} %copy-done.1, f32[2,288,8,128]{3,2,1,0:T(8,128)S(1)} %get-tuple-element.107.refs_6_.refs_2_, ...), custom_call_target="tpu_custom_call", output_to_operand_aliasing={{0}: (2, {}), {1}: (3, {})} | custom-call | tf_op jit(solution)/shard_map/turn_in/pallas_call | solution.py:45
  27.8 1.6 %decode.7 = (f32[288,1024]{1,0:T(8,128)S(1)}, f32[288,256]{1,0:T(8,128)S(1)}, f32[256,256]{1,0:T(8,128)S(1)}, f32[256,256]{1,0:T(8,128)S(1)}, f32[256,256]{1,0:T(8,128)S(1)}, /*index=5*/f32[256,256]{1,0:T(8,128)S(1)}) custom-call(s32[1]{0:T(128)} %bitcast.refs_0_, s32[16]{0:T(128)S(1)} %copy-done.2, bf16[288,256]{1,0:T(8,128)(2,1)S(1)} %get-tuple-element.106.refs_2_, ...), custom_call_target="tpu_custom_call" | custom-call | tf_op jit(solution)/shard_map/decode/pallas_call | solution.py:45
  32.4 2.4 %collective-permute-start.36 = (f16[256,1024]{1,0:T(8,128)(2,1)S(1)}, f16[256,1024]{1,0:T(8,128)(2,1)S(1)}, u32[]{:S(2)}, u32[]{:S(2)}) collective-permute-start(f16[256,1024]{1,0:T(8,128)(2,1)S(1)} %convert_element_type.173), channel_id=1, source_target_pairs={{0,2},{1,3},{2,0},{3,1},{4,6},{5,7},{6,4},{7,5},{8,10},{9,11},{10,... | collective-permute-start | bytes 1572872 | tf_op jit(solution)/shard_map/ppermute | solution.py:30
  34.8 3.9 %stencil.3 = (f32[2,288,8,128]{3,2,1,0:T(8,128)S(1)}, f32[2,288,8,128]{3,2,1,0:T(8,128)S(1)}, f32[1,1024]{1,0:T(1,128)S(1)}, f32[1,1024]{1,0:T(1,128)S(1)}, s32[16,256]{1,0:T(8,128)}) custom-call(s32[1]{0:T(128)} %bitcast.refs_0_, f32[12,288]{1,0:T(8,128)S(1)} %copy-done.1, s32[16]{0:T(128)S(1)} %copy-done.2, f32[288,16,256]{2,1,0:T(8,128)} %bitcast.15, ...), custom_call_target="tpu_custom_call" | custom-call | tf_op jit(solution)/shard_map/stencil/pallas_call | solution.py:45
  41.6 1.6 %decode.10 = (f32[288,1024]{1,0:T(8,128)S(1)}, f32[288,256]{1,0:T(8,128)S(1)}, f32[256,256]{1,0:T(8,128)S(1)}, f32[256,256]{1,0:T(8,128)S(1)}, f32[256,256]{1,0:T(8,128)S(1)}, /*index=5*/f32[256,256]{1,0:T(8,128)S(1)}) custom-call(s32[1]{0:T(128)} %bitcast.refs_0_, s32[16]{0:T(128)S(1)} %copy-done.2, bf16[288,256]{1,0:T(8,128)(2,1)S(1)} %get-tuple-element.106.refs_2_, ...), custom_call_target="tpu_custom_call" | custom-call | tf_op jit(solution)/shard_map/decode/pallas_call | solution.py:45
  45.7 1.3 %collective-permute-start.28 = (f16[304,256]{1,0:T(8,128)(2,1)S(1)}, f16[304,256]{1,0:T(8,128)(2,1)S(1)}, u32[]{:S(2)}, u32[]{:S(2)}) collective-permute-start(f16[304,256]{1,0:T(8,128)(2,1)S(1)} %convert_element_type.163), channel_id=1, source_target_pairs={{0,4},{4,0},{8,12},{12,8},{16,20},{20,16},{24,28},{28,24},{1,5},{5... | collective-permute-start | bytes 466952 | tf_op jit(solution)/shard_map/ppermute | solution.py:30
  48.0 1.4 %collective-permute-start.34 = (f16[256,512]{1,0:T(8,128)(2,1)S(1)}, f16[256,512]{1,0:T(8,128)(2,1)S(1)}, u32[]{:S(2)}, u32[]{:S(2)}) collective-permute-start(f16[256,512]{1,0:T(8,128)(2,1)S(1)} %convert_element_type.168), channel_id=1, source_target_pairs={{0,2},{1,3},{2,0},{3,1},{4,6},{5,7},{6,4},{7,5},{8,10},{9,11},{10,... | collective-permute-start | bytes 786440 | tf_op jit(solution)/shard_map/ppermute | solution.py:30
  50.4 1.4 %collective-permute-done.28 = f16[304,256]{1,0:T(8,128)(2,1)S(1)} collective-permute-done((f16[304,256]{1,0:T(8,128)(2,1)S(1)}, f16[304,256]{1,0:T(8,128)(2,1)S(1)}, u32[]{:S(2)}, u32[]{:S(2)}) %collective-permute-start.28) | collective-permute-done | bytes 155680 | tf_op jit(solution)/shard_map/ppermute | solution.py:30
  51.9 1.6 %collective-permute-start.35 = (f16[304,256]{1,0:T(8,128)(2,1)S(1)}, f16[304,256]{1,0:T(8,128)(2,1)S(1)}, u32[]{:S(2)}, u32[]{:S(2)}) collective-permute-start(f16[304,256]{1,0:T(8,128)(2,1)S(1)} %convert_element_type.170), channel_id=1, source_target_pairs={{0,8},{4,12},{8,0},{12,4},{16,24},{20,28},{24,16},{28,20},{1,9},{5... | collective-permute-start | bytes 466952 | tf_op jit(solution)/shard_map/ppermute | solution.py:30
  53.6 1.8 %store.2 = (f32[288,16,256]{2,1,0:T(8,128)}, f32[8,128]{1,0:T(8,128)S(1)}) custom-call(s32[1]{0:T(128)} %bitcast.refs_0_, f32[2,288,8,128]{3,2,1,0:T(8,128)S(1)} %get-tuple-element.116.refs_2_.refs_1_, f32[288,1024]{1,0:T(8,128)S(1)} %get-tuple-element.141.refs_2_, f32[288,512]{1,0:T(8,128)S(1)} %get-tuple-element.142.refs_3_, ...), custom_call_target="tpu_custom_call" | custom-call | tf_op jit(solution)/shard_map/store/pallas_call | solution.py:45
  55.3 1.9 %collective-permute-done.35 = f16[304,256]{1,0:T(8,128)(2,1)S(1)} collective-permute-done((f16[304,256]{1,0:T(8,128)(2,1)S(1)}, f16[304,256]{1,0:T(8,128)(2,1)S(1)}, u32[]{:S(2)}, u32[]{:S(2)}) %collective-permute-start.35) | collective-permute-done | bytes 155680 | tf_op jit(solution)/shard_map/ppermute | solution.py:30
  57.3 2.7 %collective-permute-start.44 = (f16[416,256]{1,0:T(8,128)(2,1)S(1)}, f16[416,256]{1,0:T(8,128)(2,1)S(1)}, u32[]{:S(2)}, u32[]{:S(2)}) collective-permute-start(f16[416,256]{1,0:T(8,128)(2,1)S(1)} %convert_element_type.178), channel_id=1, source_target_pairs={{0,16},{4,20},{8,24},{12,28},{16,0},{20,4},{24,8},{28,12},{1,17},{... | collective-permute-start | bytes 638984 | tf_op jit(solution)/shard_map/ppermute | solution.py:30
  66.6 1.9 %collective-permute-done.44 = f16[416,256]{1,0:T(8,128)(2,1)S(1)} collective-permute-done((f16[416,256]{1,0:T(8,128)(2,1)S(1)}, f16[416,256]{1,0:T(8,128)(2,1)S(1)}, u32[]{:S(2)}, u32[]{:S(2)}) %collective-permute-start.44) | collective-permute-done | bytes 213024 | tf_op jit(solution)/shard_map/ppermute | solution.py:30
  69.7 1.6 %collective-permute-start.47 = (f16[304,128]{1,0:T(8,128)(2,1)S(1)}, f16[304,128]{1,0:T(8,128)(2,1)S(1)}, u32[]{:S(2)}, u32[]{:S(2)}) collective-permute-start(f16[304,128]{1,0:T(8,128)(2,1)S(1)} %convert_element_type.189), channel_id=1, source_target_pairs={{0,8},{4,12},{8,0},{12,4},{16,24},{20,28},{24,16},{28,20},{1,9},{5... | collective-permute-start | bytes 233480 | tf_op jit(solution)/shard_map/ppermute | solution.py:30
  72.4 1.8 %store.3 = (f32[288,16,256]{2,1,0:T(8,128)}, f32[8,128]{1,0:T(8,128)S(1)}) custom-call(s32[1]{0:T(128)} %bitcast.refs_0_, f32[2,288,8,128]{3,2,1,0:T(8,128)S(1)} %get-tuple-element.129.refs_2_.refs_1_, f32[288,1024]{1,0:T(8,128)S(1)} %get-tuple-element.137.refs_2_, f32[288,512]{1,0:T(8,128)S(1)} %get-tuple-element.138.refs_3_, ...), custom_call_target="tpu_custom_call", output_to_operand_aliasing={{0}: (5, {})} | custom-call | tf_op jit(solution)/shard_map/store/pallas_call | solution.py:45
  74.7 3.0 %collective-permute-start.49 = (f16[304,128]{1,0:T(8,128)(2,1)S(1)}, f16[304,128]{1,0:T(8,128)(2,1)S(1)}, u32[]{:S(2)}, u32[]{:S(2)}) collective-permute-start(f16[304,128]{1,0:T(8,128)(2,1)S(1)} %convert_element_type.192), channel_id=1, source_target_pairs={{0,16},{4,20},{8,24},{12,28},{16,0},{20,4},{24,8},{28,12},{1,17},{... | collective-permute-start | bytes 233480 | tf_op jit(solution)/shard_map/ppermute | solution.py:30
  77.7 1.9 %collective-permute-start.48 = (f16[304,128]{1,0:T(8,128)(2,1)S(1)}, f16[304,128]{1,0:T(8,128)(2,1)S(1)}, u32[]{:S(2)}, u32[]{:S(2)}) collective-permute-start(f16[304,128]{1,0:T(8,128)(2,1)S(1)} %convert_element_type.184), channel_id=1, source_target_pairs={{0,16},{4,20},{8,24},{12,28},{16,0},{20,4},{24,8},{28,12},{1,17},{... | collective-permute-start | bytes 233480 | tf_op jit(solution)/shard_map/ppermute | solution.py:30
  79.7 2.3 %collective-permute-done.49 = f16[304,128]{1,0:T(8,128)(2,1)S(1)} collective-permute-done((f16[304,128]{1,0:T(8,128)(2,1)S(1)}, f16[304,128]{1,0:T(8,128)(2,1)S(1)}, u32[]{:S(2)}, u32[]{:S(2)}) %collective-permute-start.49) | collective-permute-done | bytes 77856 | tf_op jit(solution)/shard_map/ppermute | solution.py:30
  82.0 2.2 %collective-permute-done.48 = f16[304,128]{1,0:T(8,128)(2,1)S(1)} collective-permute-done((f16[304,128]{1,0:T(8,128)(2,1)S(1)}, f16[304,128]{1,0:T(8,128)(2,1)S(1)}, u32[]{:S(2)}, u32[]{:S(2)}) %collective-permute-start.48) | collective-permute-done | bytes 77856 | tf_op jit(solution)/shard_map/ppermute | solution.py:30
  (169 shorter events, 32.9 us)
Async XLA Ops:
  3.0 4.3 %collective-permute-start = (f32[256,256]{1,0:T(8,128)S(1)}, f32[256,256]{1,0:T(8,128)S(1)}, u32[]{:S(2)}, u32[]{:S(2)}) collective-permute-start(f32[256,256]{1,0:T(8,128)S(1)} %get-tuple-element.94), channel_id=1, source_target_pairs={{0,1},{1,0},{2,3},{3,2},{4,5},{5,4},{6,7},{7,6},{8,9},{9,8},{10,11... | collective-permute-start | bytes 786440 | tf_op jit(solution)/shard_map/ppermute | solution.py:30
  3.5 3.9 %collective-permute-start.1 = (f32[256,256]{1,0:T(8,128)S(1)}, f32[256,256]{1,0:T(8,128)S(1)}, u32[]{:S(2)}, u32[]{:S(2)}) collective-permute-start(f32[256,256]{1,0:T(8,128)S(1)} %get-tuple-element.95), channel_id=1, source_target_pairs={{0,1},{1,0},{2,3},{3,2},{4,5},{5,4},{6,7},{7,6},{8,9},{9,8},{10,11... | collective-permute-start | bytes 786440 | tf_op jit(solution)/shard_map/ppermute | solution.py:30
  3.6 3.8 %collective-permute-start.2 = (f32[256,256]{1,0:T(8,128)S(1)}, f32[256,256]{1,0:T(8,128)S(1)}, u32[]{:S(2)}, u32[]{:S(2)}) collective-permute-start(f32[256,256]{1,0:T(8,128)S(1)} %get-tuple-element.96), channel_id=1, source_target_pairs={{0,1},{1,0},{2,3},{3,2},{4,5},{5,4},{6,7},{7,6},{8,9},{9,8},{10,11... | collective-permute-start | bytes 786440 | tf_op jit(solution)/shard_map/ppermute | solution.py:30
  4.0 3.4 %collective-permute-start.3 = (f32[256,256]{1,0:T(8,128)S(1)}, f32[256,256]{1,0:T(8,128)S(1)}, u32[]{:S(2)}, u32[]{:S(2)}) collective-permute-start(f32[256,256]{1,0:T(8,128)S(1)} %get-tuple-element.97), channel_id=1, source_target_pairs={{0,1},{1,0},{2,3},{3,2},{4,5},{5,4},{6,7},{7,6},{8,9},{9,8},{10,11... | collective-permute-start | bytes 786440 | tf_op jit(solution)/shard_map/ppermute | solution.py:30
  4.1 14.4 %collective-permute-start.6 = (f16[2,2,32,8,128]{4,3,2,1,0:T(8,128)(2,1)S(1)}, f16[2,2,32,8,128]{4,3,2,1,0:T(8,128)(2,1)S(1)}, u32[]{:S(2)}, u32[]{:S(2)}) collective-permute-start(f16[2,2,32,8,128]{4,3,2,1,0:T(8,128)(2,1)S(1)} %convert_element_type.151), channel_id=1, source_target_pairs={{0,3},{1,2},{2,1},{3,0},{4,7},{5,6},{6,5},{7,4},{8,11},{9,10},{10,... | collective-permute-start | bytes 786440 | tf_op jit(solution)/shard_map/ppermute | solution.py:30
  7.7 17.2 %collective-permute-start.14 = (f16[256,1024]{1,0:T(8,128)(2,1)S(1)}, f16[256,1024]{1,0:T(8,128)(2,1)S(1)}, u32[]{:S(2)}, u32[]{:S(2)}) collective-permute-start(f16[256,1024]{1,0:T(8,128)(2,1)S(1)} %convert_element_type.159), channel_id=1, source_target_pairs={{0,2},{1,3},{2,0},{3,1},{4,6},{5,7},{6,4},{7,5},{8,10},{9,11},{10,... | collective-permute-start | bytes 1572872 | tf_op jit(solution)/shard_map/ppermute | solution.py:30
  10.8 7.8 %collective-permute-start.7 = (f16[2,288,128]{2,1,0:T(8,128)(2,1)S(1)}, f16[2,288,128]{2,1,0:T(8,128)(2,1)S(1)}, u32[]{:S(2)}, u32[]{:S(2)}) collective-permute-start(f16[2,288,128]{2,1,0:T(8,128)(2,1)S(1)} %convert_element_type.153), channel_id=1, source_target_pairs={{0,4},{1,5},{4,8},{5,9},{6,2},{7,3},{8,12},{9,13},{10,6},{11,7},{1... | collective-permute-start | bytes 442376 | tf_op jit(solution)/shard_map/ppermute | solution.py:687
  22.4 16.3 %collective-permute-start.23 = (f16[256,1024]{1,0:T(8,128)(2,1)S(1)}, f16[256,1024]{1,0:T(8,128)(2,1)S(1)}, u32[]{:S(2)}, u32[]{:S(2)}) collective-permute-start(f16[256,1024]{1,0:T(8,128)(2,1)S(1)} %convert_element_type.161), channel_id=1, source_target_pairs={{0,2},{1,3},{2,0},{3,1},{4,6},{5,7},{6,4},{7,5},{8,10},{9,11},{10,... | collective-permute-start | bytes 1572872 | tf_op jit(solution)/shard_map/ppermute | solution.py:30
  32.4 17.0 %collective-permute-start.36 = (f16[256,1024]{1,0:T(8,128)(2,1)S(1)}, f16[256,1024]{1,0:T(8,128)(2,1)S(1)}, u32[]{:S(2)}, u32[]{:S(2)}) collective-permute-start(f16[256,1024]{1,0:T(8,128)(2,1)S(1)} %convert_element_type.173), channel_id=1, source_target_pairs={{0,2},{1,3},{2,0},{3,1},{4,6},{5,7},{6,4},{7,5},{8,10},{9,11},{10,... | collective-permute-start | bytes 1572872 | tf_op jit(solution)/shard_map/ppermute | solution.py:30
  43.4 3.6 %collective-permute-start.30 = (f32[256,256]{1,0:T(8,128)S(1)}, f32[256,256]{1,0:T(8,128)S(1)}, u32[]{:S(2)}, u32[]{:S(2)}) collective-permute-start(f32[256,256]{1,0:T(8,128)S(1)} %get-tuple-element.152), channel_id=1, source_target_pairs={{0,1},{1,0},{2,3},{3,2},{4,5},{5,4},{6,7},{7,6},{8,9},{9,8},{10,11... | collective-permute-start | bytes 786440 | tf_op jit(solution)/shard_map/ppermute | solution.py:30
  43.8 3.2 %collective-permute-start.31 = (f32[256,256]{1,0:T(8,128)S(1)}, f32[256,256]{1,0:T(8,128)S(1)}, u32[]{:S(2)}, u32[]{:S(2)}) collective-permute-start(f32[256,256]{1,0:T(8,128)S(1)} %get-tuple-element.153), channel_id=1, source_target_pairs={{0,1},{1,0},{2,3},{3,2},{4,5},{5,4},{6,7},{7,6},{8,9},{9,8},{10,11... | collective-permute-start | bytes 786440 | tf_op jit(solution)/shard_map/ppermute | solution.py:30
  45.7 6.1 %collective-permute-start.28 = (f16[304,256]{1,0:T(8,128)(2,1)S(1)}, f16[304,256]{1,0:T(8,128)(2,1)S(1)}, u32[]{:S(2)}, u32[]{:S(2)}) collective-permute-start(f16[304,256]{1,0:T(8,128)(2,1)S(1)} %convert_element_type.163), channel_id=1, source_target_pairs={{0,4},{4,0},{8,12},{12,8},{16,20},{20,16},{24,28},{28,24},{1,5},{5... | collective-permute-start | bytes 466952 | tf_op jit(solution)/shard_map/ppermute | solution.py:30
  47.2 13.1 %collective-permute-start.33 = (f16[256,512]{1,0:T(8,128)(2,1)S(1)}, f16[256,512]{1,0:T(8,128)(2,1)S(1)}, u32[]{:S(2)}, u32[]{:S(2)}) collective-permute-start(f16[256,512]{1,0:T(8,128)(2,1)S(1)} %convert_element_type.166), channel_id=1, source_target_pairs={{0,2},{1,3},{2,0},{3,1},{4,6},{5,7},{6,4},{7,5},{8,10},{9,11},{10,... | collective-permute-start | bytes 786440 | tf_op jit(solution)/shard_map/ppermute | solution.py:30
  48.0 13.0 %collective-permute-start.34 = (f16[256,512]{1,0:T(8,128)(2,1)S(1)}, f16[256,512]{1,0:T(8,128)(2,1)S(1)}, u32[]{:S(2)}, u32[]{:S(2)}) collective-permute-start(f16[256,512]{1,0:T(8,128)(2,1)S(1)} %convert_element_type.168), channel_id=1, source_target_pairs={{0,2},{1,3},{2,0},{3,1},{4,6},{5,7},{6,4},{7,5},{8,10},{9,11},{10,... | collective-permute-start | bytes 786440 | tf_op jit(solution)/shard_map/ppermute | solution.py:30
  49.8 11.2 %collective-permute-start.37 = (bf16[256,512]{1,0:T(8,128)(2,1)S(1)}, bf16[256,512]{1,0:T(8,128)(2,1)S(1)}, u32[]{:S(2)}, u32[]{:S(2)}) collective-permute-start(bf16[256,512]{1,0:T(8,128)(2,1)S(1)} %get-tuple-element.160.refs_1_), channel_id=1, source_target_pairs={{0,1},{1,0},{2,3},{3,2},{4,5},{5,4},{6,7},{7,6},{8,9},{9,8},{10,11... | collective-permute-start | bytes 786440 | tf_op jit(solution)/shard_map/ppermute | solution.py:30
  49.9 11.1 %collective-permute-start.38 = (bf16[256,512]{1,0:T(8,128)(2,1)S(1)}, bf16[256,512]{1,0:T(8,128)(2,1)S(1)}, u32[]{:S(2)}, u32[]{:S(2)}) collective-permute-start(bf16[256,512]{1,0:T(8,128)(2,1)S(1)} %get-tuple-element.161.refs_2_), channel_id=1, source_target_pairs={{0,1},{1,0},{2,3},{3,2},{4,5},{5,4},{6,7},{7,6},{8,9},{9,8},{10,11... | collective-permute-start | bytes 786440 | tf_op jit(solution)/shard_map/ppermute | solution.py:30
  51.9 5.3 %collective-permute-start.35 = (f16[304,256]{1,0:T(8,128)(2,1)S(1)}, f16[304,256]{1,0:T(8,128)(2,1)S(1)}, u32[]{:S(2)}, u32[]{:S(2)}) collective-permute-start(f16[304,256]{1,0:T(8,128)(2,1)S(1)} %convert_element_type.170), channel_id=1, source_target_pairs={{0,8},{4,12},{8,0},{12,4},{16,24},{20,28},{24,16},{28,20},{1,9},{5... | collective-permute-start | bytes 466952 | tf_op jit(solution)/shard_map/ppermute | solution.py:30
  57.3 11.1 %collective-permute-start.44 = (f16[416,256]{1,0:T(8,128)(2,1)S(1)}, f16[416,256]{1,0:T(8,128)(2,1)S(1)}, u32[]{:S(2)}, u32[]{:S(2)}) collective-permute-start(f16[416,256]{1,0:T(8,128)(2,1)S(1)} %convert_element_type.178), channel_id=1, source_target_pairs={{0,16},{4,20},{8,24},{12,28},{16,0},{20,4},{24,8},{28,12},{1,17},{... | collective-permute-start | bytes 638984 | tf_op jit(solution)/shard_map/ppermute | solution.py:30
  64.4 5.2 %collective-permute-start.46 = (f16[304,128]{1,0:T(8,128)(2,1)S(1)}, f16[304,128]{1,0:T(8,128)(2,1)S(1)}, u32[]{:S(2)}, u32[]{:S(2)}) collective-permute-start(f16[304,128]{1,0:T(8,128)(2,1)S(1)} %convert_element_type.186), channel_id=1, source_target_pairs={{0,4},{4,0},{8,12},{12,8},{16,20},{20,16},{24,28},{28,24},{1,5},{5... | collective-permute-start | bytes 233480 | tf_op jit(solution)/shard_map/ppermute | solution.py:30
  65.3 6.1 %collective-permute-start.43 = (f16[304,128]{1,0:T(8,128)(2,1)S(1)}, f16[304,128]{1,0:T(8,128)(2,1)S(1)}, u32[]{:S(2)}, u32[]{:S(2)}) collective-permute-start(f16[304,128]{1,0:T(8,128)(2,1)S(1)} %convert_element_type.175), channel_id=1, source_target_pairs={{0,4},{4,0},{8,12},{12,8},{16,20},{20,16},{24,28},{28,24},{1,5},{5... | collective-permute-start | bytes 233480 | tf_op jit(solution)/shard_map/ppermute | solution.py:30
  69.7 4.9 %collective-permute-start.47 = (f16[304,128]{1,0:T(8,128)(2,1)S(1)}, f16[304,128]{1,0:T(8,128)(2,1)S(1)}, u32[]{:S(2)}, u32[]{:S(2)}) collective-permute-start(f16[304,128]{1,0:T(8,128)(2,1)S(1)} %convert_element_type.189), channel_id=1, source_target_pairs={{0,8},{4,12},{8,0},{12,4},{16,24},{20,28},{24,16},{28,20},{1,9},{5... | collective-permute-start | bytes 233480 | tf_op jit(solution)/shard_map/ppermute | solution.py:30
  71.4 6.2 %collective-permute-start.45 = (f16[304,128]{1,0:T(8,128)(2,1)S(1)}, f16[304,128]{1,0:T(8,128)(2,1)S(1)}, u32[]{:S(2)}, u32[]{:S(2)}) collective-permute-start(f16[304,128]{1,0:T(8,128)(2,1)S(1)} %convert_element_type.181), channel_id=1, source_target_pairs={{0,8},{4,12},{8,0},{12,4},{16,24},{20,28},{24,16},{28,20},{1,9},{5... | collective-permute-start | bytes 233480 | tf_op jit(solution)/shard_map/ppermute | solution.py:30
  74.7 7.3 %collective-permute-start.49 = (f16[304,128]{1,0:T(8,128)(2,1)S(1)}, f16[304,128]{1,0:T(8,128)(2,1)S(1)}, u32[]{:S(2)}, u32[]{:S(2)}) collective-permute-start(f16[304,128]{1,0:T(8,128)(2,1)S(1)} %convert_element_type.192), channel_id=1, source_target_pairs={{0,16},{4,20},{8,24},{12,28},{16,0},{20,4},{24,8},{28,12},{1,17},{... | collective-permute-start | bytes 233480 | tf_op jit(solution)/shard_map/ppermute | solution.py:30
  77.7 6.5 %collective-permute-start.48 = (f16[304,128]{1,0:T(8,128)(2,1)S(1)}, f16[304,128]{1,0:T(8,128)(2,1)S(1)}, u32[]{:S(2)}, u32[]{:S(2)}) collective-permute-start(f16[304,128]{1,0:T(8,128)(2,1)S(1)} %convert_element_type.184), channel_id=1, source_target_pairs={{0,16},{4,20},{8,24},{12,28},{16,0},{20,4},{24,8},{28,12},{1,17},{... | collective-permute-start | bytes 233480 | tf_op jit(solution)/shard_map/ppermute | solution.py:30
  (29 other events, 73.8 us)
